TPU v7x, 256 devices: a whole 4x4x8 slice. The times are simulated.
256 devices in a mesh: cp: 128 (over y, x, z), hd: 2 (over core).
Axes of the slice: x: 4, y: 4, z: 8, core: 2. Of those that a mesh axis runs over, the one named last changes fastest.
Arguments:
- queries: bfloat16 [32768, 1024], P('cp', 'hd'), may hold values from -32 to 32
- keys: bfloat16 [32768, 256], P('cp', 'hd'), may hold values from -13 to 13
- values: bfloat16 [32768, 256], P('cp', 'hd'), may hold values from -6 to 6
- out_weight: bfloat16 [4096, 1024], P(None, 'hd'), may hold values from -0.1875 to 0.1875
- doc_lengths: int32 [64], replicated, may hold values from 1 to 1024, 32768 in all
- doc_full: int32 [64], replicated, may hold values 0 or 1
- out_grad: bfloat16 [32768, 4096], P('cp', 'hd'), may hold values from -6 to 6
Outputs:
- layer_out: bfloat16 [32768, 4096], P('cp', 'hd')
- query_grad: bfloat16 [32768, 1024], P('cp', 'hd')
- key_grad: bfloat16 [32768, 256], P('cp', 'hd')
- value_grad: bfloat16 [32768, 256], P('cp', 'hd')
Inputs may be any that keep to these rules, and one draw needn't show every extreme that they name: `doc_lengths`: the lengths add up to 32768; the longest document has exactly 1024 tokens.
All inputs are finite; a program needn't handle non-finite values.
Results may differ from a plain program's by a relative error of at most 0.035.
Values may be sent and summed in bfloat16 or wider, within the bound.
No kernel may reach another device: no remote copies, remote signals or barrier semaphores. Data moves between devices by JAX's collectives and lax.ppermute only.
A program may use at most 128 MiB of HBM per device.

v0:
```python
import math

import jax
import jax.numpy as jnp
from jax import lax
from jax.sharding import PartitionSpec as P

HQ = 8
HK = 2
DH = 128
SPAN = 4


def passed_along(block, axis, distance):
    devices = range(lax.axis_size(axis))
    route = [(i - distance, i) for i in devices if i - distance in devices]
    return lax.ppermute(block, axis, route)


def doc_layout(doc_lengths, doc_full, positions, total):
    ends = jnp.cumsum(doc_lengths)
    doc_index = jnp.sum((positions[:, None] >= ends[None, :]).astype(jnp.int32), axis=1)
    inside = (positions >= 0) & (positions < total)
    labels = jnp.arange(doc_lengths.shape[0], dtype=jnp.int32)
    full_flag = jnp.sum(
        jnp.where(doc_index[:, None] == labels[None, :], doc_full[None, :], 0), axis=1
    )
    return (doc_index, full_flag, inside)


def allowed_mask(doc_lengths, doc_full, query_pos, key_pos, total):
    query_doc, query_full, _ = doc_layout(doc_lengths, doc_full, query_pos, total)
    key_doc, _, key_inside = doc_layout(doc_lengths, doc_full, key_pos, total)
    same = key_doc[None, :] == query_doc[:, None]
    order = (query_full[:, None] == 1) | (key_pos[None, :] <= query_pos[:, None])
    return key_inside[None, :] & same & order


def reach_direct(keys, values, span):
    key_parts = []
    val_parts = []
    for offset in range(-span, span + 1):
        if offset == 0:
            key_parts.append(keys)
            val_parts.append(values)
        else:
            got = passed_along((keys, values), "cp", -offset)
            key_parts.append(got[0])
            val_parts.append(got[1])
    return (jnp.concatenate(key_parts, axis=0), jnp.concatenate(val_parts, axis=0))


def return_direct(key_win, val_win, span, rows):
    own_key = key_win[span * rows : (span + 1) * rows]
    own_val = val_win[span * rows : (span + 1) * rows]
    for offset in range(-span, span + 1):
        if offset != 0:
            low = (offset + span) * rows
            got = (
                passed_along(key_win[low : low + rows].astype(jnp.bfloat16), "cp", offset).astype(
                    jnp.float32
                ),
                passed_along(val_win[low : low + rows].astype(jnp.bfloat16), "cp", offset).astype(
                    jnp.float32
                ),
            )
            own_key = own_key + got[0]
            own_val = own_val + got[1]
    return (own_key, own_val)


def on_device(queries, keys, values, out_weight, doc_lengths, doc_full, out_grad):
    rows = queries.shape[0]
    span = SPAN
    devices = lax.axis_size("cp")
    index = lax.axis_index("cp")
    total = rows * devices
    width_rows = (2 * span + 1) * rows
    local_kv = keys.shape[1] // DH
    groups = HQ // HK
    scale = 1.0 / math.sqrt(DH)
    key_win, val_win = reach_direct(keys, values, span)
    query_pos = index * rows + jnp.arange(rows, dtype=jnp.int32)
    key_pos = (index - span) * rows + jnp.arange(width_rows, dtype=jnp.int32)
    mask = allowed_mask(doc_lengths, doc_full, query_pos, key_pos, total)
    q_heads = queries.reshape(rows, local_kv, groups, DH)
    k_heads = key_win.reshape(width_rows, local_kv, DH)
    v_heads = val_win.reshape(width_rows, local_kv, DH)
    scores = (
        jnp.einsum("tkgd,skd->kgts", q_heads, k_heads, preferred_element_type=jnp.float32) * scale
    )
    masked = jnp.where(mask[None, None], scores, jnp.float32(-1e30))
    top = jnp.max(masked, axis=-1, keepdims=True)
    expo = jnp.where(mask[None, None], jnp.exp(masked - top), jnp.float32(0.0))
    probs = expo / jnp.sum(expo, axis=-1, keepdims=True)
    weights = probs.astype(jnp.bfloat16)
    attn = jnp.einsum("kgts,skd->tkgd", weights, v_heads, preferred_element_type=jnp.float32)
    attn = attn.astype(jnp.bfloat16).reshape(rows, local_kv * groups * DH)
    partial_value = jnp.einsum("tc,fc->tf", attn, out_weight, preferred_element_type=jnp.float32)
    layer_out = lax.psum_scatter(
        partial_value.astype(jnp.bfloat16), "hd", scatter_dimension=1, tiled=True
    )
    cotangent = lax.all_gather(out_grad, "hd", axis=1, tiled=True)
    attn_grad = jnp.dot(cotangent, out_weight, preferred_element_type=jnp.float32).astype(
        jnp.bfloat16
    )
    grad_heads = attn_grad.reshape(rows, local_kv, groups, DH)
    delta = jnp.einsum(
        "tkgd,tkgd->kgt",
        grad_heads.astype(jnp.float32),
        attn.reshape(rows, local_kv, groups, DH).astype(jnp.float32),
    )
    dprob = jnp.einsum("tkgd,skd->kgts", grad_heads, v_heads, preferred_element_type=jnp.float32)
    dscore = (probs * (dprob - delta[..., None]) * scale).astype(jnp.bfloat16)
    query_grad = jnp.einsum("kgts,skd->tkgd", dscore, k_heads, preferred_element_type=jnp.float32)
    query_grad = query_grad.astype(jnp.bfloat16).reshape(rows, local_kv * groups * DH)
    key_terms = jnp.einsum(
        "kgts,tkgd->skd", dscore, q_heads, preferred_element_type=jnp.float32
    ).reshape(width_rows, local_kv * DH)
    val_terms = jnp.einsum(
        "kgts,tkgd->skd", weights, grad_heads, preferred_element_type=jnp.float32
    ).reshape(width_rows, local_kv * DH)
    own_key, own_val = return_direct(key_terms, val_terms, span, rows)
    return (layer_out, query_grad, own_key.astype(jnp.bfloat16), own_val.astype(jnp.bfloat16))


def solution(mesh):
    placed = (P("cp", "hd"), P("cp", "hd"), P("cp", "hd"), P(None, "hd"), P(), P(), P("cp", "hd"))
    return jax.shard_map(
        on_device,
        mesh=mesh,
        in_specs=placed,
        out_specs=(P("cp", "hd"), P("cp", "hd"), P("cp", "hd"), P("cp", "hd")),
        check_vma=False,
    )
```

profile of v0, /device:TPU:120, one launch (start us, length us, event | category | flops | bytes accessed | tf_op | source)
XLA Modules:
  0.0 241.0 jit_solution(4963313475059450090)
XLA Ops:
  7.2 6.5 %collective-permute-start.8 = (bf16[256,128]{1,0:T(8,128)(2,1)}, bf16[256,128]{1,0:T(8,128)(2,1)S(1)}, u32[]{:S(2)}, u32[]{:S(2)}) collective-permute-start(bf16[256,128]{1,0:T(8,128)(2,1)} %param.8), channel_id=1, source_target_pairs={{0,8},{2,10},{4,12},{6,14},{8,16},{10,18},{12,20},{14,22},{16,24},... | collective-permute-start | bytes 196616 | tf_op jit(solution)/shard_map/ppermute | solution.py:17
  13.8 2.9 %collective-permute-start.9 = (bf16[256,128]{1,0:T(8,128)(2,1)}, bf16[256,128]{1,0:T(8,128)(2,1)S(1)}, u32[]{:S(2)}, u32[]{:S(2)}) collective-permute-start(bf16[256,128]{1,0:T(8,128)(2,1)} %param.8), channel_id=1, source_target_pairs={{0,6},{2,8},{4,10},{6,12},{8,14},{10,16},{12,18},{14,20},{16,22},{... | collective-permute-start | bytes 196616 | tf_op jit(solution)/shard_map/ppermute | solution.py:17
  16.7 6.4 %collective-permute-start.10 = (bf16[256,128]{1,0:T(8,128)(2,1)}, bf16[256,128]{1,0:T(8,128)(2,1)S(1)}, u32[]{:S(2)}, u32[]{:S(2)}) collective-permute-start(bf16[256,128]{1,0:T(8,128)(2,1)} %param.8), channel_id=1, source_target_pairs={{0,4},{2,6},{4,8},{6,10},{8,12},{10,14},{12,16},{14,18},{16,20},{1... | collective-permute-start | bytes 196616 | tf_op jit(solution)/shard_map/ppermute | solution.py:17
  23.1 2.9 %collective-permute-start.11 = (bf16[256,128]{1,0:T(8,128)(2,1)}, bf16[256,128]{1,0:T(8,128)(2,1)S(1)}, u32[]{:S(2)}, u32[]{:S(2)}) collective-permute-start(bf16[256,128]{1,0:T(8,128)(2,1)} %param.8), channel_id=1, source_target_pairs={{0,2},{2,4},{4,6},{6,8},{8,10},{10,12},{12,14},{14,16},{16,18},{18... | collective-permute-start | bytes 196616 | tf_op jit(solution)/shard_map/ppermute | solution.py:17
  26.0 2.9 %collective-permute-start.12 = (bf16[256,128]{1,0:T(8,128)(2,1)}, bf16[256,128]{1,0:T(8,128)(2,1)S(1)}, u32[]{:S(2)}, u32[]{:S(2)}) collective-permute-start(bf16[256,128]{1,0:T(8,128)(2,1)} %param.8), channel_id=1, source_target_pairs={{2,0},{4,2},{6,4},{8,6},{10,8},{12,10},{14,12},{16,14},{18,16},{20... | collective-permute-start | bytes 196616 | tf_op jit(solution)/shard_map/ppermute | solution.py:17
  31.0 2.1 or_and_fusion
  34.1 1.9 collective-permute-start.13
  36.1 7.4 %collective-permute-start.14 = (bf16[256,128]{1,0:T(8,128)(2,1)}, bf16[256,128]{1,0:T(8,128)(2,1)S(1)}, u32[]{:S(2)}, u32[]{:S(2)}) collective-permute-start(bf16[256,128]{1,0:T(8,128)(2,1)} %param.8), channel_id=1, source_target_pairs={{6,0},{8,2},{10,4},{12,6},{14,8},{16,10},{18,12},{20,14},{22,16},{... | collective-permute-start | bytes 196616 | tf_op jit(solution)/shard_map/ppermute | solution.py:17
  43.5 4.5 %collective-permute-start.15 = (bf16[256,128]{1,0:T(8,128)(2,1)}, bf16[256,128]{1,0:T(8,128)(2,1)S(1)}, u32[]{:S(2)}, u32[]{:S(2)}) collective-permute-start(bf16[256,128]{1,0:T(8,128)(2,1)} %param.8), channel_id=1, source_target_pairs={{8,0},{10,2},{12,4},{14,6},{16,8},{18,10},{20,12},{22,14},{24,16},... | collective-permute-start | bytes 196616 | tf_op jit(solution)/shard_map/ppermute | solution.py:17
  48.0 5.3 %collective-permute-start = (bf16[256,128]{0,1:T(8,128)(2,1)S(1)}, bf16[256,128]{0,1:T(8,128)(2,1)S(1)}, u32[]{:S(2)}, u32[]{:S(2)}) collective-permute-start(bf16[256,128]{0,1:T(8,128)(2,1)S(1)} %copy.53), channel_id=1, source_target_pairs={{0,8},{2,10},{4,12},{6,14},{8,16},{10,18},{12,20},{14,22},{16,24},... | collective-permute-start | bytes 196616 | tf_op jit(solution)/shard_map/ppermute | solution.py:17
  54.1 6.9 %collective-permute-done = bf16[256,128]{0,1:T(8,128)(2,1)S(1)} collective-permute-done((bf16[256,128]{0,1:T(8,128)(2,1)S(1)}, bf16[256,128]{0,1:T(8,128)(2,1)S(1)}, u32[]{:S(2)}, u32[]{:S(2)}) %collective-permute-start) | collective-permute-done | bytes 65568 | tf_op jit(solution)/shard_map/ppermute | solution.py:17
  61.1 1.9 collective-permute-start.1
  63.6 5.4 %collective-permute-done.1 = bf16[256,128]{0,1:T(8,128)(2,1)S(1)} collective-permute-done((bf16[256,128]{0,1:T(8,128)(2,1)S(1)}, bf16[256,128]{0,1:T(8,128)(2,1)S(1)}, u32[]{:S(2)}, u32[]{:S(2)}) %collective-permute-start.1) | collective-permute-done | bytes 65568 | tf_op jit(solution)/shard_map/ppermute | solution.py:17
  69.1 4.4 %collective-permute-start.2 = (bf16[256,128]{0,1:T(8,128)(2,1)S(1)}, bf16[256,128]{0,1:T(8,128)(2,1)S(1)}, u32[]{:S(2)}, u32[]{:S(2)}) collective-permute-start(bf16[256,128]{0,1:T(8,128)(2,1)S(1)} %copy.53), channel_id=1, source_target_pairs={{0,4},{2,6},{4,8},{6,10},{8,12},{10,14},{12,16},{14,18},{16,20},{1... | collective-permute-start | bytes 196616 | tf_op jit(solution)/shard_map/ppermute | solution.py:17
  74.2 6.5 %collective-permute-done.2 = bf16[256,128]{0,1:T(8,128)(2,1)S(1)} collective-permute-done((bf16[256,128]{0,1:T(8,128)(2,1)S(1)}, bf16[256,128]{0,1:T(8,128)(2,1)S(1)}, u32[]{:S(2)}, u32[]{:S(2)}) %collective-permute-start.2) | collective-permute-done | bytes 65568 | tf_op jit(solution)/shard_map/ppermute | solution.py:17
  80.7 1.9 collective-permute-start.3
  83.3 3.6 %collective-permute-done.3 = bf16[256,128]{0,1:T(8,128)(2,1)S(1)} collective-permute-done((bf16[256,128]{0,1:T(8,128)(2,1)S(1)}, bf16[256,128]{0,1:T(8,128)(2,1)S(1)}, u32[]{:S(2)}, u32[]{:S(2)}) %collective-permute-start.3) | collective-permute-done | bytes 65568 | tf_op jit(solution)/shard_map/ppermute | solution.py:17
  86.9 7.6 %collective-permute-start.4 = (bf16[256,128]{0,1:T(8,128)(2,1)S(1)}, bf16[256,128]{0,1:T(8,128)(2,1)S(1)}, u32[]{:S(2)}, u32[]{:S(2)}) collective-permute-start(bf16[256,128]{0,1:T(8,128)(2,1)S(1)} %copy.53), channel_id=1, source_target_pairs={{2,0},{4,2},{6,4},{8,6},{10,8},{12,10},{14,12},{16,14},{18,16},{20... | collective-permute-start | bytes 196616 | tf_op jit(solution)/shard_map/ppermute | solution.py:17
  95.8 8.1 %collective-permute-start.5 = (bf16[256,128]{0,1:T(8,128)(2,1)S(1)}, bf16[256,128]{0,1:T(8,128)(2,1)S(1)}, u32[]{:S(2)}, u32[]{:S(2)}) collective-permute-start(bf16[256,128]{0,1:T(8,128)(2,1)S(1)} %copy.53), channel_id=1, source_target_pairs={{4,0},{6,2},{8,4},{10,6},{12,8},{14,10},{16,12},{18,14},{20,16},{2... | collective-permute-start | bytes 196616 | tf_op jit(solution)/shard_map/ppermute | solution.py:17
  103.9 1.9 collective-permute-start.6
  105.9 1.9 collective-permute-start.7
  109.2 4.4 %collective-permute-done.6 = bf16[256,128]{0,1:T(8,128)(2,1)S(1)} collective-permute-done((bf16[256,128]{0,1:T(8,128)(2,1)S(1)}, bf16[256,128]{0,1:T(8,128)(2,1)S(1)}, u32[]{:S(2)}, u32[]{:S(2)}) %collective-permute-start.6) | collective-permute-done | bytes 65568 | tf_op jit(solution)/shard_map/ppermute | solution.py:17
  114.2 1.7 collective-permute-done.7
  116.6 1.6 fusion.3
  118.2 3.7 %copy-done.1 = f32[2304,256,4]{1,0,2:T(8,128)} copy-done((f32[2304,256,4]{1,0,2:T(8,128)}, f32[2304,256,4]{1,0,2:T(8,128)S(1)}, u32[]{:S(2)}) %copy-start.1) | copy-done | bytes 9437208
  121.9 2.3 fusion.5
  124.2 4.1 %convolution_convert_fusion.1 = bf16[256,512]{1,0:T(8,128)(2,1)S(1)} fusion(bf16[256,4096]{1,0:T(8,128)(2,1)} %all-gather.2.cloned.1.call-done, bf16[4096,512]{1,0:T(8,128)(2,1)} %param.10), kind=kOutput, calls=%fused_computation.19 | convolution fusion | flops 1073872896 | bytes 6553600 | tf_op jit(solution)/shard_map/dot_general | solution.py:104
  128.8 7.1 %multiply_reduce_fusion = (f32[4,256]{1,0:T(4,128)S(1)}, bf16[128,4,256]{2,0,1:T(8,128)(2,1)S(1)}) fusion(f32[4,256,128]{1,2,0:T(8,128)S(1)} %copy.81, f32[4,256]{1,0:T(4,128)S(1)} %fusion.5, f32[4,256]{1,0:T(4,128)S(1)} %get-tuple-element.32, f32[2304,256,4]{1,0,2:T(8,128)} %copy-done.1, pred[256,2304]{0,1:T(8,128)(4,1)S(1)} %or_and_fusion, ...), kind=kOutput, calls=%fused_computation.28 | convolution fusion | flops 618658816 | bytes 11415552 | tf_op jit(solution)/shard_map/kgts,skd->tkgd/dot_general | solution.py:97
  136.0 2.6 %convolution_convert_fusion = bf16[256,4096]{1,0:T(8,128)(2,1)} fusion(bf16[256,512]{0,1:T(8,128)(2,1)S(1)} %bitcast.199, bf16[4096,512]{1,0:T(8,128)(2,1)S(1)} %copy-done.2), kind=kOutput, calls=%fused_computation.9 | convolution fusion | flops 1074790400 | bytes 6553600 | tf_op jit(solution)/shard_map/tc,fc->tf/dot_general | solution.py:99
  138.7 6.9 %fusion.48 = (bf16[2304,1,128]{0,2,1:T(8,128)(2,1)S(1)}, f32[2304,1,128]{0,2,1:T(8,128)}) fusion(bf16[256,4,128]{0,2,1:T(8,128)(2,1)S(1)} %copy.70, f32[4,256]{1,0:T(4,128)S(1)} %fusion.5, f32[4,256]{1,0:T(4,128)S(1)} %get-tuple-element.32, f32[2304,256,4]{1,0,2:T(8,128)} %copy-done.1, pred[256,2304]{0,1:T(8,128)(4,1)S(1)} %or_and_fusion), kind=kOutput, calls=%fused_computation.96 | convolution fusion | flops 618430464 | bytes 12066816 | tf_op jit(solution)/shard_map/kgts,tkgd->skd/dot_general | solution.py:120
  145.6 6.3 %collective-permute-start.24 = (bf16[256,128]{0,1:T(8,128)(2,1)S(1)}, bf16[256,128]{0,1:T(8,128)(2,1)S(1)}, u32[]{:S(2)}, u32[]{:S(2)}) collective-permute-start(bf16[256,128]{0,1:T(8,128)(2,1)S(1)} %get-tuple-element.16), channel_id=1, source_target_pairs={{8,0},{10,2},{12,4},{14,6},{16,8},{18,10},{20,12},{22,14},{24,16},... | collective-permute-start | bytes 196616 | tf_op jit(solution)/shard_map/ppermute | solution.py:17
  151.9 1.9 collective-permute-start.25
  153.9 1.9 collective-permute-start.26
  155.8 2.5 %collective-permute-start.27 = (bf16[256,128]{0,1:T(8,128)(2,1)S(1)}, bf16[256,128]{0,1:T(8,128)(2,1)S(1)}, u32[]{:S(2)}, u32[]{:S(2)}) collective-permute-start(bf16[256,128]{0,1:T(8,128)(2,1)S(1)} %get-tuple-element.21), channel_id=1, source_target_pairs={{2,0},{4,2},{6,4},{8,6},{10,8},{12,10},{14,12},{16,14},{18,16},{20... | collective-permute-start | bytes 196616 | tf_op jit(solution)/shard_map/ppermute | solution.py:17
  158.3 4.8 %collective-permute-start.28 = (bf16[256,128]{0,1:T(8,128)(2,1)S(1)}, bf16[256,128]{0,1:T(8,128)(2,1)S(1)}, u32[]{:S(2)}, u32[]{:S(2)}) collective-permute-start(bf16[256,128]{0,1:T(8,128)(2,1)S(1)} %get-tuple-element.20), channel_id=1, source_target_pairs={{0,2},{2,4},{4,6},{6,8},{8,10},{10,12},{12,14},{14,16},{16,18},{18... | collective-permute-start | bytes 196616 | tf_op jit(solution)/shard_map/ppermute | solution.py:17
  163.1 5.0 %fusion.6 = bf16[4,256,2304]{1,2,0:T(8,128)(2,1)S(1)} fusion(bf16[256,4,128]{0,2,1:T(8,128)(2,1)S(1)} %copy.70, f32[4,256]{1,0:T(4,128)S(1)} %get-tuple-element.34, f32[4,256]{1,0:T(4,128)S(1)} %fusion.5, f32[4,256]{1,0:T(4,128)S(1)} %get-tuple-element.32, f32[2304,256,4]{1,0,2:T(8,128)S(1)} %bitcast.197, pred[256,2304]{0,1:T(8,128)(4,1)S(1)} %or_and_fusion, ...), kind=kOutput, calls=%fused_computation.10 | convolution fusion | flops 625213440 | bytes 15609856 | tf_op jit(solution)/shard_map/tkgd,skd->kgts/dot_general | solution.py:113
  169.5 4.8 %collective-permute-start.29 = (bf16[256,128]{0,1:T(8,128)(2,1)S(1)}, bf16[256,128]{0,1:T(8,128)(2,1)S(1)}, u32[]{:S(2)}, u32[]{:S(2)}) collective-permute-start(bf16[256,128]{0,1:T(8,128)(2,1)S(1)} %get-tuple-element.19), channel_id=1, source_target_pairs={{0,4},{2,6},{4,8},{6,10},{8,12},{10,14},{12,16},{14,18},{16,20},{1... | collective-permute-start | bytes 196616 | tf_op jit(solution)/shard_map/ppermute | solution.py:17
  174.4 7.8 %collective-permute-start.30 = (bf16[256,128]{0,1:T(8,128)(2,1)S(1)}, bf16[256,128]{0,1:T(8,128)(2,1)S(1)}, u32[]{:S(2)}, u32[]{:S(2)}) collective-permute-start(bf16[256,128]{0,1:T(8,128)(2,1)S(1)} %get-tuple-element.18), channel_id=1, source_target_pairs={{0,6},{2,8},{4,10},{6,12},{8,14},{10,16},{12,18},{14,20},{16,22},{... | collective-permute-start | bytes 196616 | tf_op jit(solution)/shard_map/ppermute | solution.py:17
  182.3 4.5 %collective-permute-start.31 = (bf16[256,128]{0,1:T(8,128)(2,1)S(1)}, bf16[256,128]{0,1:T(8,128)(2,1)}, u32[]{:S(2)}, u32[]{:S(2)}) collective-permute-start(bf16[256,128]{0,1:T(8,128)(2,1)S(1)} %get-tuple-element.17), channel_id=1, source_target_pairs={{0,8},{2,10},{4,12},{6,14},{8,16},{10,18},{12,20},{14,22},{16,24},... | collective-permute-start | bytes 196616 | tf_op jit(solution)/shard_map/ppermute | solution.py:17
  186.8 8.3 %collective-permute-start.16 = (bf16[256,128]{1,0:T(8,128)(2,1)S(1)}, bf16[256,128]{1,0:T(8,128)(2,1)S(1)}, u32[]{:S(2)}, u32[]{:S(2)}) collective-permute-start(bf16[256,128]{1,0:T(8,128)(2,1)S(1)} %get-tuple-element.24), channel_id=1, source_target_pairs={{8,0},{10,2},{12,4},{14,6},{16,8},{18,10},{20,12},{22,14},{24,16},... | collective-permute-start | bytes 196616 | tf_op jit(solution)/shard_map/ppermute | solution.py:17
  195.1 1.9 collective-permute-start.17
  197.0 1.9 collective-permute-start.18
  200.7 2.5 %collective-permute-start.19 = (bf16[256,128]{1,0:T(8,128)(2,1)S(1)}, bf16[256,128]{1,0:T(8,128)(2,1)S(1)}, u32[]{:S(2)}, u32[]{:S(2)}) collective-permute-start(bf16[256,128]{1,0:T(8,128)(2,1)S(1)} %get-tuple-element.29), channel_id=1, source_target_pairs={{2,0},{4,2},{6,4},{8,6},{10,8},{12,10},{14,12},{16,14},{18,16},{20... | collective-permute-start | bytes 196616 | tf_op jit(solution)/shard_map/ppermute | solution.py:17
  203.1 4.6 %collective-permute-start.20 = (bf16[256,128]{1,0:T(8,128)(2,1)S(1)}, bf16[256,128]{1,0:T(8,128)(2,1)S(1)}, u32[]{:S(2)}, u32[]{:S(2)}) collective-permute-start(bf16[256,128]{1,0:T(8,128)(2,1)S(1)} %get-tuple-element.28), channel_id=1, source_target_pairs={{0,2},{2,4},{4,6},{6,8},{8,10},{10,12},{12,14},{14,16},{16,18},{18... | collective-permute-start | bytes 196616 | tf_op jit(solution)/shard_map/ppermute | solution.py:17
  207.7 4.8 %collective-permute-start.21 = (bf16[256,128]{1,0:T(8,128)(2,1)S(1)}, bf16[256,128]{1,0:T(8,128)(2,1)S(1)}, u32[]{:S(2)}, u32[]{:S(2)}) collective-permute-start(bf16[256,128]{1,0:T(8,128)(2,1)S(1)} %get-tuple-element.27), channel_id=1, source_target_pairs={{0,4},{2,6},{4,8},{6,10},{8,12},{10,14},{12,16},{14,18},{16,20},{1... | collective-permute-start | bytes 196616 | tf_op jit(solution)/shard_map/ppermute | solution.py:17
  212.6 7.8 %collective-permute-start.22 = (bf16[256,128]{1,0:T(8,128)(2,1)S(1)}, bf16[256,128]{1,0:T(8,128)(2,1)S(1)}, u32[]{:S(2)}, u32[]{:S(2)}) collective-permute-start(bf16[256,128]{1,0:T(8,128)(2,1)S(1)} %get-tuple-element.26), channel_id=1, source_target_pairs={{0,6},{2,8},{4,10},{6,12},{8,14},{10,16},{12,18},{14,20},{16,22},{... | collective-permute-start | bytes 196616 | tf_op jit(solution)/shard_map/ppermute | solution.py:17
  220.4 2.4 collective-permute-start.23
  224.6 8.9 %collective-permute-done.23 = bf16[256,128]{1,0:T(8,128)(2,1)S(1)} collective-permute-done((bf16[256,128]{1,0:T(8,128)(2,1)S(1)}, bf16[256,128]{1,0:T(8,128)(2,1)S(1)}, u32[]{:S(2)}, u32[]{:S(2)}) %collective-permute-start.23) | collective-permute-done | bytes 65568 | tf_op jit(solution)/shard_map/ppermute | solution.py:17
  (86 shorter events, 16.0 us)
Async XLA Ops:
  7.2 109.4 %copy-start = (bf16[256,512]{1,0:T(8,128)(2,1)S(1)}, bf16[256,512]{1,0:T(8,128)(2,1)}, u32[]{:S(2)}) copy-start(bf16[256,512]{1,0:T(8,128)(2,1)} %param.7) | copy-start | bytes 786436
  7.2 117.0 %all-gather.2.cloned.1.call-start = ((), (), s32[]{:S(2)}) async-start(), calls=%async_computation.2 | async-start | bytes 3145728 | tf_op jit(solution)/shard_map/all_gather | solution.py:103
  7.2 26.9 %collective-permute-start.8 = (bf16[256,128]{1,0:T(8,128)(2,1)}, bf16[256,128]{1,0:T(8,128)(2,1)S(1)}, u32[]{:S(2)}, u32[]{:S(2)}) collective-permute-start(bf16[256,128]{1,0:T(8,128)(2,1)} %param.8), channel_id=1, source_target_pairs={{0,8},{2,10},{4,12},{6,14},{8,16},{10,18},{12,20},{14,22},{16,24},... | collective-permute-start | bytes 196616 | tf_op jit(solution)/shard_map/ppermute | solution.py:17
  13.8 22.3 %collective-permute-start.9 = (bf16[256,128]{1,0:T(8,128)(2,1)}, bf16[256,128]{1,0:T(8,128)(2,1)S(1)}, u32[]{:S(2)}, u32[]{:S(2)}) collective-permute-start(bf16[256,128]{1,0:T(8,128)(2,1)} %param.8), channel_id=1, source_target_pairs={{0,6},{2,8},{4,10},{6,12},{8,14},{10,16},{12,18},{14,20},{16,22},{... | collective-permute-start | bytes 196616 | tf_op jit(solution)/shard_map/ppermute | solution.py:17
  16.7 26.8 %collective-permute-start.10 = (bf16[256,128]{1,0:T(8,128)(2,1)}, bf16[256,128]{1,0:T(8,128)(2,1)S(1)}, u32[]{:S(2)}, u32[]{:S(2)}) collective-permute-start(bf16[256,128]{1,0:T(8,128)(2,1)} %param.8), channel_id=1, source_target_pairs={{0,4},{2,6},{4,8},{6,10},{8,12},{10,14},{12,16},{14,18},{16,20},{1... | collective-permute-start | bytes 196616 | tf_op jit(solution)/shard_map/ppermute | solution.py:17
  23.1 24.9 %collective-permute-start.11 = (bf16[256,128]{1,0:T(8,128)(2,1)}, bf16[256,128]{1,0:T(8,128)(2,1)S(1)}, u32[]{:S(2)}, u32[]{:S(2)}) collective-permute-start(bf16[256,128]{1,0:T(8,128)(2,1)} %param.8), channel_id=1, source_target_pairs={{0,2},{2,4},{4,6},{6,8},{8,10},{10,12},{12,14},{14,16},{16,18},{18... | collective-permute-start | bytes 196616 | tf_op jit(solution)/shard_map/ppermute | solution.py:17
  26.0 69.7 %collective-permute-start.12 = (bf16[256,128]{1,0:T(8,128)(2,1)}, bf16[256,128]{1,0:T(8,128)(2,1)S(1)}, u32[]{:S(2)}, u32[]{:S(2)}) collective-permute-start(bf16[256,128]{1,0:T(8,128)(2,1)} %param.8), channel_id=1, source_target_pairs={{2,0},{4,2},{6,4},{8,6},{10,8},{12,10},{14,12},{16,14},{18,16},{20... | collective-permute-start | bytes 196616 | tf_op jit(solution)/shard_map/ppermute | solution.py:17
  29.0 205.2 %reduce-scatter.2.cloned.1.call-start = ((), (), s32[]{:S(2)}) async-start(), calls=%async_computation.1 | async-start | bytes 3145728 | tf_op jit(solution)/shard_map/reduce_scatter | solution.py:100
  34.1 69.8 %collective-permute-start.13 = (bf16[256,128]{1,0:T(8,128)(2,1)}, bf16[256,128]{1,0:T(8,128)(2,1)S(1)}, u32[]{:S(2)}, u32[]{:S(2)}) collective-permute-start(bf16[256,128]{1,0:T(8,128)(2,1)} %param.8), channel_id=1, source_target_pairs={{4,0},{6,2},{8,4},{10,6},{12,8},{14,10},{16,12},{18,14},{20,16},{2... | collective-permute-start | bytes 196616 | tf_op jit(solution)/shard_map/ppermute | solution.py:17
  36.1 69.8 %collective-permute-start.14 = (bf16[256,128]{1,0:T(8,128)(2,1)}, bf16[256,128]{1,0:T(8,128)(2,1)S(1)}, u32[]{:S(2)}, u32[]{:S(2)}) collective-permute-start(bf16[256,128]{1,0:T(8,128)(2,1)} %param.8), channel_id=1, source_target_pairs={{6,0},{8,2},{10,4},{12,6},{14,8},{16,10},{18,12},{20,14},{22,16},{... | collective-permute-start | bytes 196616 | tf_op jit(solution)/shard_map/ppermute | solution.py:17
  43.5 64.4 %collective-permute-start.15 = (bf16[256,128]{1,0:T(8,128)(2,1)}, bf16[256,128]{1,0:T(8,128)(2,1)S(1)}, u32[]{:S(2)}, u32[]{:S(2)}) collective-permute-start(bf16[256,128]{1,0:T(8,128)(2,1)} %param.8), channel_id=1, source_target_pairs={{8,0},{10,2},{12,4},{14,6},{16,8},{18,10},{20,12},{22,14},{24,16},... | collective-permute-start | bytes 196616 | tf_op jit(solution)/shard_map/ppermute | solution.py:17
  48.0 13.1 %collective-permute-start = (bf16[256,128]{0,1:T(8,128)(2,1)S(1)}, bf16[256,128]{0,1:T(8,128)(2,1)S(1)}, u32[]{:S(2)}, u32[]{:S(2)}) collective-permute-start(bf16[256,128]{0,1:T(8,128)(2,1)S(1)} %copy.53), channel_id=1, source_target_pairs={{0,8},{2,10},{4,12},{6,14},{8,16},{10,18},{12,20},{14,22},{16,24},... | collective-permute-start | bytes 196616 | tf_op jit(solution)/shard_map/ppermute | solution.py:17
  61.1 8.0 %collective-permute-start.1 = (bf16[256,128]{0,1:T(8,128)(2,1)S(1)}, bf16[256,128]{0,1:T(8,128)(2,1)S(1)}, u32[]{:S(2)}, u32[]{:S(2)}) collective-permute-start(bf16[256,128]{0,1:T(8,128)(2,1)S(1)} %copy.53), channel_id=1, source_target_pairs={{0,6},{2,8},{4,10},{6,12},{8,14},{10,16},{12,18},{14,20},{16,22},{... | collective-permute-start | bytes 196616 | tf_op jit(solution)/shard_map/ppermute | solution.py:17
  69.1 11.6 %collective-permute-start.2 = (bf16[256,128]{0,1:T(8,128)(2,1)S(1)}, bf16[256,128]{0,1:T(8,128)(2,1)S(1)}, u32[]{:S(2)}, u32[]{:S(2)}) collective-permute-start(bf16[256,128]{0,1:T(8,128)(2,1)S(1)} %copy.53), channel_id=1, source_target_pairs={{0,4},{2,6},{4,8},{6,10},{8,12},{10,14},{12,16},{14,18},{16,20},{1... | collective-permute-start | bytes 196616 | tf_op jit(solution)/shard_map/ppermute | solution.py:17
  80.7 6.1 %collective-permute-start.3 = (bf16[256,128]{0,1:T(8,128)(2,1)S(1)}, bf16[256,128]{0,1:T(8,128)(2,1)S(1)}, u32[]{:S(2)}, u32[]{:S(2)}) collective-permute-start(bf16[256,128]{0,1:T(8,128)(2,1)S(1)} %copy.53), channel_id=1, source_target_pairs={{0,2},{2,4},{4,6},{6,8},{8,10},{10,12},{12,14},{14,16},{16,18},{18... | collective-permute-start | bytes 196616 | tf_op jit(solution)/shard_map/ppermute | solution.py:17
  86.9 21.0 %collective-permute-start.4 = (bf16[256,128]{0,1:T(8,128)(2,1)S(1)}, bf16[256,128]{0,1:T(8,128)(2,1)S(1)}, u32[]{:S(2)}, u32[]{:S(2)}) collective-permute-start(bf16[256,128]{0,1:T(8,128)(2,1)S(1)} %copy.53), channel_id=1, source_target_pairs={{2,0},{4,2},{6,4},{8,6},{10,8},{12,10},{14,12},{16,14},{18,16},{20... | collective-permute-start | bytes 196616 | tf_op jit(solution)/shard_map/ppermute | solution.py:17
  95.8 12.8 %collective-permute-start.5 = (bf16[256,128]{0,1:T(8,128)(2,1)S(1)}, bf16[256,128]{0,1:T(8,128)(2,1)S(1)}, u32[]{:S(2)}, u32[]{:S(2)}) collective-permute-start(bf16[256,128]{0,1:T(8,128)(2,1)S(1)} %copy.53), channel_id=1, source_target_pairs={{4,0},{6,2},{8,4},{10,6},{12,8},{14,10},{16,12},{18,14},{20,16},{2... | collective-permute-start | bytes 196616 | tf_op jit(solution)/shard_map/ppermute | solution.py:17
  103.9 9.7 %collective-permute-start.6 = (bf16[256,128]{0,1:T(8,128)(2,1)S(1)}, bf16[256,128]{0,1:T(8,128)(2,1)S(1)}, u32[]{:S(2)}, u32[]{:S(2)}) collective-permute-start(bf16[256,128]{0,1:T(8,128)(2,1)S(1)} %copy.53), channel_id=1, source_target_pairs={{6,0},{8,2},{10,4},{12,6},{14,8},{16,10},{18,12},{20,14},{22,16},{... | collective-permute-start | bytes 196616 | tf_op jit(solution)/shard_map/ppermute | solution.py:17
  105.9 10.1 %collective-permute-start.7 = (bf16[256,128]{0,1:T(8,128)(2,1)S(1)}, bf16[256,128]{0,1:T(8,128)(2,1)S(1)}, u32[]{:S(2)}, u32[]{:S(2)}) collective-permute-start(bf16[256,128]{0,1:T(8,128)(2,1)S(1)} %copy.53), channel_id=1, source_target_pairs={{8,0},{10,2},{12,4},{14,6},{16,8},{18,10},{20,12},{22,14},{24,16},... | collective-permute-start | bytes 196616 | tf_op jit(solution)/shard_map/ppermute | solution.py:17
  118.2 3.7 %copy-start.1 = (f32[2304,256,4]{1,0,2:T(8,128)}, f32[2304,256,4]{1,0,2:T(8,128)S(1)}, u32[]{:S(2)}) copy-start(f32[2304,256,4]{1,0,2:T(8,128)S(1)} %get-tuple-element.33) | copy-start | bytes 28311556
  128.8 7.2 %copy-start.2 = (bf16[4096,512]{1,0:T(8,128)(2,1)S(1)}, bf16[4096,512]{1,0:T(8,128)(2,1)}, u32[]{:S(2)}) copy-start(bf16[4096,512]{1,0:T(8,128)(2,1)} %param.10) | copy-start | bytes 12582916
  138.6 24.4 %slice-start = ((s8[9437184]{0:T(1024)(128)(4,1)}), s8[1048576]{0:T(1024)(128)(4,1)S(1)}, s32[]{:S(2)}) async-start(s8[9437184]{0:T(1024)(128)(4,1)} %bitcast.196), calls=%async_computation.3 | async-start | bytes 2097152
  138.6 24.4 %slice-start.1 = ((s8[9437184]{0:T(1024)(128)(4,1)}), s8[4194304]{0:T(1024)(128)(4,1)S(1)}, s32[]{:S(2)}) async-start(s8[9437184]{0:T(1024)(128)(4,1)} %bitcast.196), calls=%async_computation.4 | async-start | bytes 8388608
  138.6 24.4 %slice-start.2 = ((s8[9437184]{0:T(1024)(128)(4,1)}), s8[4194304]{0:T(1024)(128)(4,1)S(1)}, s32[]{:S(2)}) async-start(s8[9437184]{0:T(1024)(128)(4,1)} %bitcast.196), calls=%async_computation.5 | async-start | bytes 8388608
  145.6 23.9 %collective-permute-start.24 = (bf16[256,128]{0,1:T(8,128)(2,1)S(1)}, bf16[256,128]{0,1:T(8,128)(2,1)S(1)}, u32[]{:S(2)}, u32[]{:S(2)}) collective-permute-start(bf16[256,128]{0,1:T(8,128)(2,1)S(1)} %get-tuple-element.16), channel_id=1, source_target_pairs={{8,0},{10,2},{12,4},{14,6},{16,8},{18,10},{20,12},{22,14},{24,16},... | collective-permute-start | bytes 196616 | tf_op jit(solution)/shard_map/ppermute | solution.py:17
  151.9 22.5 %collective-permute-start.25 = (bf16[256,128]{0,1:T(8,128)(2,1)S(1)}, bf16[256,128]{0,1:T(8,128)(2,1)S(1)}, u32[]{:S(2)}, u32[]{:S(2)}) collective-permute-start(bf16[256,128]{0,1:T(8,128)(2,1)S(1)} %get-tuple-element.23), channel_id=1, source_target_pairs={{6,0},{8,2},{10,4},{12,6},{14,8},{16,10},{18,12},{20,14},{22,16},{... | collective-permute-start | bytes 196616 | tf_op jit(solution)/shard_map/ppermute | solution.py:17
  153.9 28.4 %collective-permute-start.26 = (bf16[256,128]{0,1:T(8,128)(2,1)S(1)}, bf16[256,128]{0,1:T(8,128)(2,1)S(1)}, u32[]{:S(2)}, u32[]{:S(2)}) collective-permute-start(bf16[256,128]{0,1:T(8,128)(2,1)S(1)} %get-tuple-element.22), channel_id=1, source_target_pairs={{4,0},{6,2},{8,4},{10,6},{12,8},{14,10},{16,12},{18,14},{20,16},{2... | collective-permute-start | bytes 196616 | tf_op jit(solution)/shard_map/ppermute | solution.py:17
  155.8 30.9 %collective-permute-start.27 = (bf16[256,128]{0,1:T(8,128)(2,1)S(1)}, bf16[256,128]{0,1:T(8,128)(2,1)S(1)}, u32[]{:S(2)}, u32[]{:S(2)}) collective-permute-start(bf16[256,128]{0,1:T(8,128)(2,1)S(1)} %get-tuple-element.21), channel_id=1, source_target_pairs={{2,0},{4,2},{6,4},{8,6},{10,8},{12,10},{14,12},{16,14},{18,16},{20... | collective-permute-start | bytes 196616 | tf_op jit(solution)/shard_map/ppermute | solution.py:17
  158.3 36.8 %collective-permute-start.28 = (bf16[256,128]{0,1:T(8,128)(2,1)S(1)}, bf16[256,128]{0,1:T(8,128)(2,1)S(1)}, u32[]{:S(2)}, u32[]{:S(2)}) collective-permute-start(bf16[256,128]{0,1:T(8,128)(2,1)S(1)} %get-tuple-element.20), channel_id=1, source_target_pairs={{0,2},{2,4},{4,6},{6,8},{8,10},{10,12},{12,14},{14,16},{16,18},{18... | collective-permute-start | bytes 196616 | tf_op jit(solution)/shard_map/ppermute | solution.py:17
  169.5 27.5 %collective-permute-start.29 = (bf16[256,128]{0,1:T(8,128)(2,1)S(1)}, bf16[256,128]{0,1:T(8,128)(2,1)S(1)}, u32[]{:S(2)}, u32[]{:S(2)}) collective-permute-start(bf16[256,128]{0,1:T(8,128)(2,1)S(1)} %get-tuple-element.19), channel_id=1, source_target_pairs={{0,4},{2,6},{4,8},{6,10},{8,12},{10,14},{12,16},{14,18},{16,20},{1... | collective-permute-start | bytes 196616 | tf_op jit(solution)/shard_map/ppermute | solution.py:17
  174.4 26.2 %collective-permute-start.30 = (bf16[256,128]{0,1:T(8,128)(2,1)S(1)}, bf16[256,128]{0,1:T(8,128)(2,1)S(1)}, u32[]{:S(2)}, u32[]{:S(2)}) collective-permute-start(bf16[256,128]{0,1:T(8,128)(2,1)S(1)} %get-tuple-element.18), channel_id=1, source_target_pairs={{0,6},{2,8},{4,10},{6,12},{8,14},{10,16},{12,18},{14,20},{16,22},{... | collective-permute-start | bytes 196616 | tf_op jit(solution)/shard_map/ppermute | solution.py:17
  182.3 20.8 %collective-permute-start.31 = (bf16[256,128]{0,1:T(8,128)(2,1)S(1)}, bf16[256,128]{0,1:T(8,128)(2,1)}, u32[]{:S(2)}, u32[]{:S(2)}) collective-permute-start(bf16[256,128]{0,1:T(8,128)(2,1)S(1)} %get-tuple-element.17), channel_id=1, source_target_pairs={{0,8},{2,10},{4,12},{6,14},{8,16},{10,18},{12,20},{14,22},{16,24},... | collective-permute-start | bytes 196616 | tf_op jit(solution)/shard_map/ppermute | solution.py:17
  186.8 21.0 %collective-permute-start.16 = (bf16[256,128]{1,0:T(8,128)(2,1)S(1)}, bf16[256,128]{1,0:T(8,128)(2,1)S(1)}, u32[]{:S(2)}, u32[]{:S(2)}) collective-permute-start(bf16[256,128]{1,0:T(8,128)(2,1)S(1)} %get-tuple-element.24), channel_id=1, source_target_pairs={{8,0},{10,2},{12,4},{14,6},{16,8},{18,10},{20,12},{22,14},{24,16},... | collective-permute-start | bytes 196616 | tf_op jit(solution)/shard_map/ppermute | solution.py:17
  195.1 4.7 %copy-start.3 = (bf16[256,128]{0,1:T(8,128)(2,1)}, bf16[256,128]{0,1:T(8,128)(2,1)S(1)}, u32[]{:S(2)}) copy-start(bf16[256,128]{0,1:T(8,128)(2,1)S(1)} %collective-permute-done.28) | copy-start | bytes 196612
  195.1 17.5 %collective-permute-start.17 = (bf16[256,128]{1,0:T(8,128)(2,1)S(1)}, bf16[256,128]{1,0:T(8,128)(2,1)S(1)}, u32[]{:S(2)}, u32[]{:S(2)}) collective-permute-start(bf16[256,128]{1,0:T(8,128)(2,1)S(1)} %get-tuple-element.31), channel_id=1, source_target_pairs={{6,0},{8,2},{10,4},{12,6},{14,8},{16,10},{18,12},{20,14},{22,16},{... | collective-permute-start | bytes 196616 | tf_op jit(solution)/shard_map/ppermute | solution.py:17
  197.0 23.4 %collective-permute-start.18 = (bf16[256,128]{1,0:T(8,128)(2,1)S(1)}, bf16[256,128]{1,0:T(8,128)(2,1)S(1)}, u32[]{:S(2)}, u32[]{:S(2)}) collective-permute-start(bf16[256,128]{1,0:T(8,128)(2,1)S(1)} %get-tuple-element.30), channel_id=1, source_target_pairs={{4,0},{6,2},{8,4},{10,6},{12,8},{14,10},{16,12},{18,14},{20,16},{2... | collective-permute-start | bytes 196616 | tf_op jit(solution)/shard_map/ppermute | solution.py:17
  200.7 23.9 %collective-permute-start.19 = (bf16[256,128]{1,0:T(8,128)(2,1)S(1)}, bf16[256,128]{1,0:T(8,128)(2,1)S(1)}, u32[]{:S(2)}, u32[]{:S(2)}) collective-permute-start(bf16[256,128]{1,0:T(8,128)(2,1)S(1)} %get-tuple-element.29), channel_id=1, source_target_pairs={{2,0},{4,2},{6,4},{8,6},{10,8},{12,10},{14,12},{16,14},{18,16},{20... | collective-permute-start | bytes 196616 | tf_op jit(solution)/shard_map/ppermute | solution.py:17
  203.1 21.4 %collective-permute-start.20 = (bf16[256,128]{1,0:T(8,128)(2,1)S(1)}, bf16[256,128]{1,0:T(8,128)(2,1)S(1)}, u32[]{:S(2)}, u32[]{:S(2)}) collective-permute-start(bf16[256,128]{1,0:T(8,128)(2,1)S(1)} %get-tuple-element.28), channel_id=1, source_target_pairs={{0,2},{2,4},{4,6},{6,8},{8,10},{10,12},{12,14},{14,16},{16,18},{18... | collective-permute-start | bytes 196616 | tf_op jit(solution)/shard_map/ppermute | solution.py:17
  207.7 16.8 %collective-permute-start.21 = (bf16[256,128]{1,0:T(8,128)(2,1)S(1)}, bf16[256,128]{1,0:T(8,128)(2,1)S(1)}, u32[]{:S(2)}, u32[]{:S(2)}) collective-permute-start(bf16[256,128]{1,0:T(8,128)(2,1)S(1)} %get-tuple-element.27), channel_id=1, source_target_pairs={{0,4},{2,6},{4,8},{6,10},{8,12},{10,14},{12,16},{14,18},{16,20},{1... | collective-permute-start | bytes 196616 | tf_op jit(solution)/shard_map/ppermute | solution.py:17
  212.6 12.0 %collective-permute-start.22 = (bf16[256,128]{1,0:T(8,128)(2,1)S(1)}, bf16[256,128]{1,0:T(8,128)(2,1)S(1)}, u32[]{:S(2)}, u32[]{:S(2)}) collective-permute-start(bf16[256,128]{1,0:T(8,128)(2,1)S(1)} %get-tuple-element.26), channel_id=1, source_target_pairs={{0,6},{2,8},{4,10},{6,12},{8,14},{10,16},{12,18},{14,20},{16,22},{... | collective-permute-start | bytes 196616 | tf_op jit(solution)/shard_map/ppermute | solution.py:17
  220.4 13.1 %collective-permute-start.23 = (bf16[256,128]{1,0:T(8,128)(2,1)S(1)}, bf16[256,128]{1,0:T(8,128)(2,1)S(1)}, u32[]{:S(2)}, u32[]{:S(2)}) collective-permute-start(bf16[256,128]{1,0:T(8,128)(2,1)S(1)} %get-tuple-element.25), channel_id=1, source_target_pairs={{0,8},{2,10},{4,12},{6,14},{8,16},{10,18},{12,20},{14,22},{16,24},... | collective-permute-start | bytes 196616 | tf_op jit(solution)/shard_map/ppermute | solution.py:17
Sparse Core Ops, SparseCore 0:
  29.1 16.3 all-gather.1
  138.8 15.0 reduce-scatter.1
where the time goes:
time: 242 us; the launch traced here: 241 us
  starting transfers between devices  137 us (57%)
  waiting for transfers between devices  37.7 us (16%)
  matrix products  29.6 us (12%)
  between operations  14.7 us (6%)
  local copies, waits for them, and re-layouts  14.3 us (6%)
  other arithmetic  7.43 us (3%)
    ppermute x32, starting transfers between devices, passed_along(): return lax.ppermute(block, axis, route)  137 us
    ppermute x32, waiting for transfers between devices, passed_along(): return lax.ppermute(block, axis, route)  37.6 us
    unnamed x34, local copies, waits for them, and re-layouts  12.6 us
    dot_general x1, matrix products, on_device(): jnp.einsum('kgts,skd->tkgd', weights, v_heads, preferred_element_type=jnp...  7.13 us
    dot_general x1, matrix products, on_device(): jnp.einsum('kgts,tkgd->skd', weights, grad_heads, preferred_element_type=...  6.91 us
    dot_general x1, matrix products, on_device(): jnp.einsum('tkgd,skd->kgts', grad_heads, v_heads, preferred_element_type=...  5.04 us
  transfers between devices with their start and end apart: 34, of which 7 were waited for; matrix products, arithmetic and copies ran while one was open for 14% of the time, Pallas kernels for 0%

commit v1 on v0

v1 whole, which is shorter than its diff:
```python
import math

import jax
import jax.numpy as jnp
from jax import lax
from jax.experimental import pallas as pl
from jax.experimental.pallas import tpu as pltpu
from jax.sharding import PartitionSpec as P

HQ = 8
HK = 2
DH = 128
SPAN = 4
ROWS = 256
GROUPS = HQ // HK
WIDE = 2 * SPAN + 1
NEG = -1e30
SCALE = 1.0 / math.sqrt(DH)
SCALE2 = SCALE / math.log(2.0)
VMEM = pl.BlockSpec(memory_space=pltpu.VMEM)
HBM = pl.BlockSpec(memory_space=pltpu.HBM)
SMALL = pltpu.CompilerParams(vmem_limit_bytes=4 * 1024 * 1024)
SMEM = pl.BlockSpec(memory_space=pltpu.SMEM)


def dot_nn(a, b):
    return lax.dot_general(a, b, (((1,), (0,)), ((), ())), preferred_element_type=jnp.float32)


def dot_nt(a, b):
    return lax.dot_general(a, b, (((1,), (1,)), ((), ())), preferred_element_type=jnp.float32)


def limits(index, lengths_row, full_row):
    n = lengths_row.shape[1]
    row = lax.broadcasted_iota(jnp.int32, (n, n), 0)
    col = lax.broadcasted_iota(jnp.int32, (n, n), 1)
    ends = jnp.sum(jnp.where(col <= row, lengths_row, 0), axis=1, keepdims=True)
    starts = jnp.sum(jnp.where(col < row, lengths_row, 0), axis=1, keepdims=True)
    full = jnp.sum(jnp.where(col == row, full_row, 0), axis=1, keepdims=True)
    pos = index * ROWS + lax.broadcasted_iota(jnp.int32, (n, ROWS), 1)
    inside = (pos >= starts) & (pos < ends)
    low = jnp.sum(jnp.where(inside, starts, 0), axis=0, keepdims=True)
    high = jnp.sum(jnp.where(inside, jnp.where(full == 1, ends, pos + 1), 0), axis=0, keepdims=True)
    return low, high


def attention_kernel(
    place_ref, len_ref, full_ref, q_ref, own_ref, *refs,
):
    ring_refs = refs[0:SPAN]
    twin_refs = refs[SPAN : 2 * SPAN]
    do_ref, attn_ref, dq_ref, mid_ref, ahead_ref, across_ref = refs[2 * SPAN : 2 * SPAN + 6]
    win, s_scr, p_scr, q_st, do_st, qs_st, dos_st, acc, dq_acc = refs[2 * SPAN + 6 :]
    index = place_ref[0]
    way = 1 - 2 * place_ref[1]
    low, high = limits(index, len_ref[...], full_ref[...])
    first = jnp.min(low)
    last = jnp.max(high)
    base = index - SPAN
    r_low = jnp.maximum(first // ROWS - base, 0)
    r_high = jnp.minimum((last + ROWS - 1) // ROWS - base, WIDE)

    def rows_of(r):
        return pl.ds(pl.multiple_of(r * ROWS, ROWS), ROWS)

    def keys_of(r):
        return pl.ds(pl.multiple_of(r * 2 * ROWS, ROWS), ROWS)

    def vals_of(r):
        return pl.ds(pl.multiple_of(r * 2 * ROWS + ROWS, ROWS), ROWS)

    def pair_of(r):
        return pl.ds(pl.multiple_of(r * 2 * ROWS, ROWS), 2 * ROWS)

    for h in range(GROUPS):
        cols = slice(h * DH, (h + 1) * DH)
        rows = slice(h * ROWS, (h + 1) * ROWS)
        q_st[rows, :] = q_ref[:, cols]
        do_st[rows, :] = do_ref[:, cols]

    win[pair_of(SPAN), :] = own_ref[...]
    for k in range(1, SPAN + 1):
        win[pair_of(SPAN - k * way), :] = ring_refs[k - 1][0 : 2 * ROWS, :]
        win[pair_of(SPAN + k * way), :] = twin_refs[k - 1][...]

    def scores(r, top):
        keys = win[keys_of(r), :]
        key_pos = (base + r) * ROWS + lax.broadcasted_iota(jnp.int32, (ROWS, ROWS), 0)
        valid = (key_pos >= low) & (key_pos < high)
        out = []
        for h in range(GROUPS):
            rows = slice(h * ROWS, (h + 1) * ROWS)
            s = dot_nt(keys, q_st[rows, :]) * SCALE2
            s = jnp.where(valid, s, NEG)
            s_scr[rows_of(r), rows] = s
            out.append(jnp.maximum(top[h], jnp.max(s, axis=0, keepdims=True)))
        return tuple(out)

    none = jnp.full((1, ROWS), NEG, jnp.float32)
    top = lax.fori_loop(r_low, r_high, scores, (none,) * GROUPS)

    acc[...] = jnp.zeros_like(acc)

    def weigh(r, total):
        vals_t = win[vals_of(r), :].T
        out = []
        for h in range(GROUPS):
            rows = slice(h * ROWS, (h + 1) * ROWS)
            p = jnp.exp2(s_scr[rows_of(r), rows] - top[h])
            out.append(total[h] + jnp.sum(p, axis=0, keepdims=True))
            p = p.astype(jnp.bfloat16)
            p_scr[rows_of(r), rows] = p
            acc[:, rows] += dot_nn(vals_t, p)
        return tuple(out)

    zero = jnp.zeros((1, ROWS), jnp.float32)
    total = lax.fori_loop(r_low, r_high, weigh, (zero,) * GROUPS)

    deltas = []
    invs = []
    for h in range(GROUPS):
        cols = slice(h * DH, (h + 1) * DH)
        rows = slice(h * ROWS, (h + 1) * ROWS)
        inv = 1.0 / total[h]
        attn = (acc[:, rows] * inv).T.astype(jnp.bfloat16)
        attn_ref[:, cols] = attn
        grad = do_st[rows, :].astype(jnp.float32)
        prod = jnp.sum(attn.astype(jnp.float32) * grad, axis=1, keepdims=True)
        deltas.append(jnp.broadcast_to(prod, (ROWS, DH)).T[0:1, :])
        inv_col = jnp.broadcast_to(inv, (DH, ROWS)).T
        dos_st[rows, :] = (grad * inv_col).astype(jnp.bfloat16)
        qs_st[rows, :] = (q_st[rows, :].astype(jnp.float32) * (inv_col * SCALE)).astype(jnp.bfloat16)
        invs.append(inv)

    dq_acc[...] = jnp.zeros_like(dq_acc)
    ahead_ref[...] = jnp.zeros_like(ahead_ref)
    across_ref[...] = jnp.zeros_like(across_ref)

    def backward(r, carry):
        keys_t = win[keys_of(r), :].T
        vals = win[vals_of(r), :]
        dk = jnp.zeros((ROWS, DH), jnp.float32)
        dv = jnp.zeros((ROWS, DH), jnp.float32)
        for h in range(GROUPS):
            rows = slice(h * ROWS, (h + 1) * ROWS)
            p = p_scr[rows_of(r), rows]
            dp = dot_nt(vals, do_st[rows, :])
            ds = (p.astype(jnp.float32) * (dp - deltas[h])).astype(jnp.bfloat16)
            dq_acc[:, rows] += dot_nn(keys_t, ds)
            dk += dot_nn(ds, qs_st[rows, :])
            dv += dot_nn(p, dos_st[rows, :])
        off = (r - SPAN) * way
        at = jnp.abs(off) - 1
        dk = dk.astype(jnp.bfloat16)
        dv = dv.astype(jnp.bfloat16)

        @pl.when(off > 0)
        def _():
            ahead_ref[keys_of(at), :] = dk
            ahead_ref[vals_of(at), :] = dv

        @pl.when(off < 0)
        def _():
            across_ref[keys_of(at), :] = dk
            across_ref[vals_of(at), :] = dv

        @pl.when(off == 0)
        def _():
            mid_ref[0:ROWS, :] = dk
            mid_ref[ROWS : 2 * ROWS, :] = dv

        return carry

    lax.fori_loop(r_low, r_high, backward, 0)
    for h in range(GROUPS):
        cols = slice(h * DH, (h + 1) * DH)
        rows = slice(h * ROWS, (h + 1) * ROWS)
        dq_ref[:, cols] = (dq_acc[:, rows] * (invs[h] * SCALE)).T.astype(jnp.bfloat16)


def attention(place, lengths, full, q, own, ring, twins, do):
    wide = GROUPS * ROWS
    return pl.pallas_call(
        attention_kernel,
        out_shape=(
            jax.ShapeDtypeStruct(q.shape, jnp.bfloat16),
            jax.ShapeDtypeStruct(q.shape, jnp.bfloat16),
            jax.ShapeDtypeStruct((2 * ROWS, DH), jnp.bfloat16),
            jax.ShapeDtypeStruct((SPAN * 2 * ROWS, DH), jnp.bfloat16),
            jax.ShapeDtypeStruct((SPAN * 2 * ROWS, DH), jnp.bfloat16),
        ),
        in_specs=[SMEM] + [VMEM] * (5 + 2 * SPAN),
        out_specs=(VMEM,) * 5,
        scratch_shapes=[
            pltpu.VMEM((WIDE * 2 * ROWS, DH), jnp.bfloat16),
            pltpu.VMEM((WIDE * ROWS, wide), jnp.float32),
            pltpu.VMEM((WIDE * ROWS, wide), jnp.bfloat16),
            pltpu.VMEM((wide, DH), jnp.bfloat16),
            pltpu.VMEM((wide, DH), jnp.bfloat16),
            pltpu.VMEM((wide, DH), jnp.bfloat16),
            pltpu.VMEM((wide, DH), jnp.bfloat16),
            pltpu.VMEM((DH, wide), jnp.float32),
            pltpu.VMEM((DH, wide), jnp.float32),
        ],
        compiler_params=pltpu.CompilerParams(vmem_limit_bytes=28 * 1024 * 1024),
        cost_estimate=pl.CostEstimate(flops=3 * 10**9, bytes_accessed=6 * 10**6, transcendentals=10**6),
    )(place, lengths, full, q, own, *ring, *twins, do)


def small_call(body, out_rows, *args):
    shapes = [jax.ShapeDtypeStruct((rows, DH), jnp.bfloat16) for rows in out_rows]
    return pl.pallas_call(
        body,
        out_shape=shapes,
        in_specs=[VMEM] * len(args),
        out_specs=[VMEM] * len(shapes),
        compiler_params=SMALL,
        cost_estimate=pl.CostEstimate(flops=10**5, bytes_accessed=10**5, transcendentals=0),
    )(*args)


def stack_body(*refs):
    at = 0
    for ref in refs[:-1]:
        refs[-1][at : at + ref.shape[0], :] = ref[...]
        at += ref.shape[0]


def part_of(k):
    return slice((k - 1) * 2 * ROWS, k * 2 * ROWS)


def both_heads(ahead, across, which):
    n = 2 * ROWS

    def body(ahead_ref, across_ref, *out_refs):
        for k, out_ref in zip(which, out_refs):
            out_ref[0:n, :] = ahead_ref[part_of(k), :]
            out_ref[n : 2 * n, :] = across_ref[part_of(k), :]

    return small_call(body, [2 * n] * len(which), ahead, across)


def summed(ahead, across, k, *others):
    n = 2 * ROWS

    def body(ahead_ref, across_ref, *refs):
        for at, ref in ((0, ahead_ref), (n, across_ref)):
            total = ref[part_of(k), :].astype(jnp.float32)
            for other in refs[:-1]:
                total += other[at : at + n, :].astype(jnp.float32)
            refs[-1][at : at + n, :] = total.astype(jnp.bfloat16)

    return small_call(body, [2 * n], ahead, across, *others)[0]


def last_sum(mid, near, far, near_twin, far_twin):
    n = 2 * ROWS

    def body(*refs):
        for out_ref, rows in ((refs[-2], slice(0, ROWS)), (refs[-1], slice(ROWS, n))):
            total = refs[0][rows, :].astype(jnp.float32)
            for ref in refs[1:-2]:
                total += ref[rows, :].astype(jnp.float32)
            out_ref[...] = total.astype(jnp.bfloat16)

    return small_call(body, [ROWS, ROWS], mid, near, far, near_twin, far_twin)


def project_back(core, own, other, w):
    rows, depth = own.shape
    cols = w.shape[1]

    def body(core_ref, own_ref, other_ref, w_ref, out_ref, w_buf, sems):
        core = core_ref[0]
        copies = []
        for n, half in enumerate((core, 1 - core)):
            where = pl.ds(pl.multiple_of(half * depth, depth), depth)
            copies.append(pltpu.make_async_copy(w_ref.at[where, :], w_buf.at[n], sems.at[n]))
            copies[n].start()
        copies[0].wait()
        part = dot_nn(own_ref[...], w_buf[0])
        copies[1].wait()
        out_ref[...] = (part + dot_nn(other_ref[...], w_buf[1])).astype(jnp.bfloat16)

    return pl.pallas_call(
        body,
        out_shape=jax.ShapeDtypeStruct((rows, cols), jnp.bfloat16),
        in_specs=[SMEM, VMEM, VMEM, HBM],
        out_specs=VMEM,
        scratch_shapes=[pltpu.VMEM((2, depth, cols), jnp.bfloat16), pltpu.SemaphoreType.DMA((2,))],
        compiler_params=pltpu.CompilerParams(vmem_limit_bytes=12 * 1024 * 1024),
        cost_estimate=pl.CostEstimate(flops=4 * rows * depth * cols, bytes_accessed=6 * 10**6, transcendentals=0),
    )(core, own, other, w)


def project(half, attn, w, other=None):
    rows, depth = attn.shape
    cols = w.shape[0] // 2
    parts = 2
    wide = cols // parts
    more = () if other is None else (other,)

    def body(half_ref, a_ref, w_ref, *refs):
        out_ref, w_buf, sems = refs[-3:]
        copies = []
        for n in range(parts):
            where = pl.ds(pl.multiple_of(half_ref[0] * cols + n * wide, wide), wide)
            copies.append(pltpu.make_async_copy(w_ref.at[where, :], w_buf.at[n], sems.at[n]))
            copies[n].start()
        for n in range(parts):
            copies[n].wait()
            at = slice(n * wide, (n + 1) * wide)
            out = dot_nt(a_ref[...], w_buf[n])
            if more:
                out += refs[0][:, at].astype(jnp.float32)
            out_ref[:, at] = out.astype(jnp.bfloat16)

    return pl.pallas_call(
        body,
        out_shape=jax.ShapeDtypeStruct((rows, cols), jnp.bfloat16),
        in_specs=[SMEM, VMEM, HBM] + [VMEM] * len(more),
        out_specs=VMEM,
        scratch_shapes=[pltpu.VMEM((parts, wide, depth), jnp.bfloat16), pltpu.SemaphoreType.DMA((parts,))],
        compiler_params=pltpu.CompilerParams(vmem_limit_bytes=12 * 1024 * 1024),
        cost_estimate=pl.CostEstimate(flops=2 * rows * depth * cols, bytes_accessed=4 * 10**6, transcendentals=0),
    )(half, attn, w, *more)


def on_device(queries, keys, values, out_weight, doc_lengths, doc_full, out_grad):
    devices = lax.axis_size("cp")
    index = lax.axis_index("cp").astype(jnp.int32)
    core = lax.axis_index("hd").astype(jnp.int32)
    place = jnp.stack([index, core])
    core = core.reshape(1)
    half = 2 * ROWS

    def step(block, far):
        ways = [(2 * i, 2 * (i + far)) for i in range(devices - far)]
        ways += [(2 * (i + far) + 1, 2 * i + 1) for i in range(devices - far)]
        return lax.ppermute(block, ("cp", "hd"), ways)

    def twin(block):
        return lax.ppermute(block, "hd", [(0, 1), (1, 0)])

    block = small_call(stack_body, [2 * half], keys, values, twin(keys), twin(values))[0]
    other_grad = twin(out_grad)
    at2 = step(block, 2)
    at1 = step(block, 1)
    attn_grad = project_back(core, out_grad, other_grad, out_weight)
    at2, attn_grad = lax.optimization_barrier((at2, attn_grad))
    at4 = step(at2, 2)
    at3 = step(at2, 1)
    ring = (at1, at2, at3, at4)
    twins = [twin(got[half:]) for got in ring]

    attn, query_grad, mid, ahead, across = attention(
        place, doc_lengths.reshape(1, -1), doc_full.reshape(1, -1), queries, block[:half], ring, twins, attn_grad
    )
    across = twin(across)
    out4, out3, out1 = both_heads(ahead, across, (4, 3, 1))
    in4 = step(out4, 2)
    in3 = step(out3, 1)
    away = project(1 - core, attn, out_weight)
    near = step(out1, 1)
    far = step(summed(ahead, across, 2, in4, in3), 2)
    layer_out = project(core, attn, out_weight, twin(away))
    far, layer_out = lax.optimization_barrier((far, layer_out))
    key_grad, value_grad = last_sum(mid, near[:half], far[:half], twin(near[half:]), twin(far[half:]))
    return (layer_out, query_grad, key_grad, value_grad)


def solution(mesh):
    placed = (P("cp", "hd"), P("cp", "hd"), P("cp", "hd"), P(None, "hd"), P(), P(), P("cp", "hd"))
    return jax.shard_map(
        on_device,
        mesh=mesh,
        in_specs=placed,
        out_specs=(P("cp", "hd"), P("cp", "hd"), P("cp", "hd"), P("cp", "hd")),
        check_vma=False,
    )
```

time: 242 us -> 95.7 us (0.40)
  the two profiles are of different devices: /device:TPU:120 before, /device:TPU:25 now
where the time goes in v1:
time: 95.7 us
  starting transfers between devices  54.6 us (57%)
  Pallas kernels  18.8 us (20%)
  waiting for transfers between devices  16.2 us (17%)
  local copies, waits for them, and re-layouts  5.19 us (5%)
    ppermute x8, starting transfers between devices, step(): return lax.ppermute(block, ('cp', 'hd'), ways)  35.8 us
    ppermute x11, starting transfers between devices, twin(): return lax.ppermute(block, 'hd', [(0, 1), (1, 0)])  18.9 us
    pallas_call x1, Pallas kernels, attention(): pl.pallas_call(attention_kernel, out_shape=(jax.ShapeDtypeStruct(q.shape,...  12.9 us
    ppermute x8, waiting for transfers between devices, step(): return lax.ppermute(block, ('cp', 'hd'), ways)  9.24 us
    ppermute x11, waiting for transfers between devices, twin(): return lax.ppermute(block, 'hd', [(0, 1), (1, 0)])  6.94 us
    unnamed x16, local copies, waits for them, and re-layouts  5.1 us
    pallas_call x2, Pallas kernels, project(): pl.pallas_call(body, out_shape=jax.ShapeDtypeStruct((rows, cols), jnp.bfl...  3.19 us
  transfers between devices with their start and end apart: 19, of which 8 were waited for; matrix products, arithmetic and copies ran while one was open for 0% of the time, Pallas kernels for 4%

profile of v1, /device:TPU:25, one launch (start us, length us, event | category | flops | bytes accessed | tf_op | source)
XLA Modules:
  0.0 95.7 jit_solution(8867773598683019849)
XLA Ops:
  0.6 0.8 collective-permute-start.4
  1.4 0.1 collective-permute-start
  1.5 0.4 collective-permute-start.1
  1.9 2.1 %collective-permute-done.refs_2_ = bf16[256,128]{1,0:T(8,128)(2,1)S(1)} collective-permute-done((bf16[256,128]{1,0:T(8,128)(2,1)}, bf16[256,128]{1,0:T(8,128)(2,1)S(1)}, u32[]{:S(2)}, u32[]{:S(2)}) %collective-permute-start) | collective-permute-done | bytes 65568 | tf_op jit(solution)/shard_map/ppermute | solution.py:345
  4.0 0.1 collective-permute-done.1.refs_3_
  4.1 0.8 copy-done.3
  4.9 0.8 copy-done.4
  5.8 10.4 %collective-permute-start.3 = (bf16[1024,128]{1,0:T(8,128)(2,1)S(1)}, bf16[1024,128]{1,0:T(8,128)(2,1)S(1)}, u32[]{:S(2)}, u32[]{:S(2)}) collective-permute-start(bf16[1024,128]{1,0:T(8,128)(2,1)S(1)} %shard_map.102), channel_id=1, source_target_pairs={{0,4},{2,6},{4,8},{6,10},{8,12},{10,14},{12,16},{14,18},{16,20},{1... | collective-permute-start | bytes 786440 | tf_op jit(solution)/shard_map/ppermute | solution.py:342
  16.2 2.6 %collective-permute-start.2 = (bf16[1024,128]{1,0:T(8,128)(2,1)S(1)}, bf16[1024,128]{1,0:T(8,128)(2,1)S(1)}, u32[]{:S(2)}, u32[]{:S(2)}) collective-permute-start(bf16[1024,128]{1,0:T(8,128)(2,1)S(1)} %shard_map.102), channel_id=1, source_target_pairs={{0,2},{2,4},{4,6},{6,8},{8,10},{10,12},{12,14},{14,16},{16,18},{18... | collective-permute-start | bytes 786440 | tf_op jit(solution)/shard_map/ppermute | solution.py:342
  18.9 0.0 collective-permute-done.4.other_ref
  18.9 0.0 copy-start
  18.9 2.2 %copy-done = bf16[4096,512]{1,0:T(8,128)(2,1)S(1)} copy-done((bf16[4096,512]{1,0:T(8,128)(2,1)S(1)}, bf16[4096,512]{1,0:T(8,128)(2,1)}, u32[]{:S(2)}) %copy-start) | copy-done | bytes 4194328
  21.1 1.2 %copy-done.2 = bf16[256,2048]{1,0:T(8,128)(2,1)S(1)} copy-done((bf16[256,2048]{1,0:T(8,128)(2,1)S(1)}, bf16[256,2048]{1,0:T(8,128)(2,1)}, u32[]{:S(2)}) %copy-start.2) | copy-done | bytes 1048600
  22.3 1.7 %shard_map.103.refs_8_ = bf16[256,512]{1,0:T(8,128)(2,1)S(1)} custom-call(s32[1]{0:T(128)} %bitcast.1.core_ref.half_ref, bf16[256,2048]{1,0:T(8,128)(2,1)S(1)} %copy-done.2, bf16[256,2048]{1,0:T(8,128)(2,1)S(1)} %collective-permute-done.4.other_ref, bf16[4096,512]{1,0:T(8,128)(2,1)S(1)} %copy-done), custom_call_target="tpu_custom_call" | custom-call | flops 1073741824 | bytes 6000000 | tf_op jit(solution)/shard_map/pallas_call | solution.py:287
  24.1 0.0 collective-permute-done.3.refs_1_
  24.1 4.0 %collective-permute-start.5 = (bf16[1024,128]{1,0:T(8,128)(2,1)S(1)}, bf16[1024,128]{1,0:T(8,128)(2,1)S(1)}, u32[]{:S(2)}, u32[]{:S(2)}) collective-permute-start(bf16[1024,128]{1,0:T(8,128)(2,1)S(1)} %collective-permute-done.3.refs_1_), channel_id=1, source_target_pairs={{0,2},{2,4},{4,6},{6,8},{8,10},{10,12},{12,14},{14,16},{16,18},{18... | collective-permute-start | bytes 786440 | tf_op jit(solution)/shard_map/ppermute | solution.py:342
  28.1 5.1 %collective-permute-start.6 = (bf16[1024,128]{1,0:T(8,128)(2,1)S(1)}, bf16[1024,128]{1,0:T(8,128)(2,1)S(1)}, u32[]{:S(2)}, u32[]{:S(2)}) collective-permute-start(bf16[1024,128]{1,0:T(8,128)(2,1)S(1)} %collective-permute-done.3.refs_1_), channel_id=1, source_target_pairs={{0,4},{2,6},{4,8},{6,10},{8,12},{10,14},{12,16},{14,18},{16,20},{1... | collective-permute-start | bytes 786440 | tf_op jit(solution)/shard_map/ppermute | solution.py:342
  33.2 0.0 collective-permute-done.2.refs_0_
  33.2 0.1 collective-permute-start.7
  33.3 0.6 collective-permute-start.8
  33.9 0.0 collective-permute-done.5.refs_2_
  33.9 0.5 collective-permute-start.9
  34.4 3.9 %collective-permute-done.6.refs_3_ = bf16[1024,128]{1,0:T(8,128)(2,1)S(1)} collective-permute-done((bf16[1024,128]{1,0:T(8,128)(2,1)S(1)}, bf16[1024,128]{1,0:T(8,128)(2,1)S(1)}, u32[]{:S(2)}, u32[]{:S(2)}) %collective-permute-start.6) | collective-permute-done | bytes 262176 | tf_op jit(solution)/shard_map/ppermute | solution.py:342
  38.3 4.9 %collective-permute-start.10 = (bf16[512,128]{1,0:T(8,128)(2,1)S(1)}, bf16[512,128]{1,0:T(8,128)(2,1)S(1)}, u32[]{:S(2)}, u32[]{:S(2)}) collective-permute-start(bf16[512,128]{1,0:T(8,128)(2,1)S(1)} %slice.39), channel_id=1, source_target_pairs={{0,1},{1,0},{2,3},{3,2},{4,5},{5,4},{6,7},{7,6},{8,9},{9,8},{10,11... | collective-permute-start | bytes 393224 | tf_op jit(solution)/shard_map/ppermute | solution.py:345
  43.3 0.1 pad_add_fusion.place_ref
  43.3 0.0 collective-permute-done.7.refs_4_
  43.4 0.0 collective-permute-done.9.refs_6_
  43.4 0.9 collective-permute-done.10.refs_7_
  44.3 12.9 %shard_map.104 = (bf16[256,512]{1,0:T(8,128)(2,1)S(1)}, bf16[256,512]{1,0:T(8,128)(2,1)}, bf16[512,128]{1,0:T(8,128)(2,1)S(1)}, bf16[2048,128]{1,0:T(8,128)(2,1)S(1)}, bf16[2048,128]{1,0:T(8,128)(2,1)S(1)}) custom-call(s32[2]{0:T(128)S(1)} %pad_add_fusion.place_ref, s32[1,64]{1,0:T(1,128)S(1)} %bitcast.4, s32[1,64]{1,0:T(1,128)S(1)} %bitcast.5, ...), custom_call_target="tpu_custom_call" | custom-call | flops 3000000000 | bytes 6000000 | tf_op jit(solution)/shard_map/pallas_call | solution.py:184
  57.2 1.1 %shard_map.107 = bf16[256,2048]{1,0:T(8,128)(2,1)S(1)} custom-call(s32[1]{0:T(128)S(6)} %sub.3.half_ref, bf16[256,512]{1,0:T(8,128)(2,1)S(1)} %get-tuple-element.24.a_ref, bf16[4096,512]{1,0:T(8,128)(2,1)S(1)} %copy-done.1), custom_call_target="tpu_custom_call" | custom-call | flops 536870912 | bytes 4000000 | tf_op jit(solution)/shard_map/pallas_call | solution.py:320
  58.3 0.5 collective-permute-start.15
  58.8 0.1 collective-permute-start.11
  58.9 2.9 %collective-permute-done.11.across_ref = bf16[2048,128]{1,0:T(8,128)(2,1)S(1)} collective-permute-done((bf16[2048,128]{1,0:T(8,128)(2,1)S(1)}, bf16[2048,128]{1,0:T(8,128)(2,1)S(1)}, u32[]{:S(2)}, u32[]{:S(2)}) %collective-permute-start.11) | collective-permute-done | bytes 524320 | tf_op jit(solution)/shard_map/ppermute | solution.py:345
  61.8 0.1 shard_map.105
  61.9 1.9 %collective-permute-start.12 = (bf16[1024,128]{1,0:T(8,128)(2,1)S(1)}, bf16[1024,128]{1,0:T(8,128)(2,1)S(1)}, u32[]{:S(2)}, u32[]{:S(2)}) collective-permute-start(bf16[1024,128]{1,0:T(8,128)(2,1)S(1)} %get-tuple-element.22), channel_id=1, source_target_pairs={{0,4},{2,6},{4,8},{6,10},{8,12},{10,14},{12,16},{14,18},{16,20},{1... | collective-permute-start | bytes 786440 | tf_op jit(solution)/shard_map/ppermute | solution.py:342
  63.8 6.8 %collective-permute-start.13 = (bf16[1024,128]{1,0:T(8,128)(2,1)S(1)}, bf16[1024,128]{1,0:T(8,128)(2,1)S(1)}, u32[]{:S(2)}, u32[]{:S(2)}) collective-permute-start(bf16[1024,128]{1,0:T(8,128)(2,1)S(1)} %get-tuple-element.23), channel_id=1, source_target_pairs={{0,2},{2,4},{4,6},{6,8},{8,10},{10,12},{12,14},{14,16},{16,18},{18... | collective-permute-start | bytes 786440 | tf_op jit(solution)/shard_map/ppermute | solution.py:342
  70.7 1.9 %collective-permute-start.16 = (bf16[1024,128]{1,0:T(8,128)(2,1)S(1)}, bf16[1024,128]{1,0:T(8,128)(2,1)S(1)}, u32[]{:S(2)}, u32[]{:S(2)}) collective-permute-start(bf16[1024,128]{1,0:T(8,128)(2,1)S(1)} %get-tuple-element.28), channel_id=1, source_target_pairs={{0,2},{2,4},{4,6},{6,8},{8,10},{10,12},{12,14},{14,16},{16,18},{18... | collective-permute-start | bytes 786440 | tf_op jit(solution)/shard_map/ppermute | solution.py:342
  72.6 0.0 collective-permute-done.12.refs_0_
  72.6 3.2 %collective-permute-done.13.refs_1_ = bf16[1024,128]{1,0:T(8,128)(2,1)S(1)} collective-permute-done((bf16[1024,128]{1,0:T(8,128)(2,1)S(1)}, bf16[1024,128]{1,0:T(8,128)(2,1)S(1)}, u32[]{:S(2)}, u32[]{:S(2)}) %collective-permute-start.13) | collective-permute-done | bytes 262176 | tf_op jit(solution)/shard_map/ppermute | solution.py:342
  75.8 0.1 shard_map.106
  75.9 2.9 %collective-permute-start.14 = (bf16[1024,128]{1,0:T(8,128)(2,1)S(1)}, bf16[1024,128]{1,0:T(8,128)(2,1)S(1)}, u32[]{:S(2)}, u32[]{:S(2)}) collective-permute-start(bf16[1024,128]{1,0:T(8,128)(2,1)S(1)} %shard_map.106), channel_id=1, source_target_pairs={{0,4},{2,6},{4,8},{6,10},{8,12},{10,14},{12,16},{14,18},{16,20},{1... | collective-permute-start | bytes 786440 | tf_op jit(solution)/shard_map/ppermute | solution.py:342
  78.8 0.0 collective-permute-done.16
  78.8 3.1 %collective-permute-start.17 = (bf16[512,128]{1,0:T(8,128)(2,1)S(1)}, bf16[512,128]{1,0:T(8,128)(2,1)S(1)}, u32[]{:S(2)}, u32[]{:S(2)}) collective-permute-start(bf16[512,128]{1,0:T(8,128)(2,1)S(1)} %get-tuple-element.34), channel_id=1, source_target_pairs={{0,1},{1,0},{2,3},{3,2},{4,5},{5,4},{6,7},{7,6},{8,9},{9,8},{10,11... | collective-permute-start | bytes 393224 | tf_op jit(solution)/shard_map/ppermute | solution.py:345
  82.0 2.1 %shard_map.108 = bf16[256,2048]{1,0:T(8,128)(2,1)} custom-call(s32[1]{0:T(128)} %bitcast.1.core_ref.half_ref, bf16[256,512]{1,0:T(8,128)(2,1)S(1)} %get-tuple-element.24.a_ref, bf16[4096,512]{1,0:T(8,128)(2,1)S(1)} %copy-done.1, bf16[256,2048]{1,0:T(8,128)(2,1)S(1)} %collective-permute-done.15.refs_0_), custom_call_target="tpu_custom_call" | custom-call | flops 536870912 | bytes 4000000 | tf_op jit(solution)/shard_map/pallas_call | solution.py:320
  84.1 2.1 %collective-permute-done.14 = bf16[1024,128]{1,0:T(8,128)(2,1)S(1)} collective-permute-done((bf16[1024,128]{1,0:T(8,128)(2,1)S(1)}, bf16[1024,128]{1,0:T(8,128)(2,1)S(1)}, u32[]{:S(2)}, u32[]{:S(2)}) %collective-permute-start.14) | collective-permute-done | bytes 262176 | tf_op jit(solution)/shard_map/ppermute | solution.py:342
  86.2 7.8 %collective-permute-start.18 = (bf16[512,128]{1,0:T(8,128)(2,1)S(1)}, bf16[512,128]{1,0:T(8,128)(2,1)S(1)}, u32[]{:S(2)}, u32[]{:S(2)}) collective-permute-start(bf16[512,128]{1,0:T(8,128)(2,1)S(1)} %get-tuple-element.32), channel_id=1, source_target_pairs={{0,1},{1,0},{2,3},{3,2},{4,5},{5,4},{6,7},{7,6},{8,9},{9,8},{10,11... | collective-permute-start | bytes 393224 | tf_op jit(solution)/shard_map/ppermute | solution.py:345
  94.0 1.0 %collective-permute-done.18.refs_4_ = bf16[512,128]{1,0:T(8,128)(2,1)S(1)} collective-permute-done((bf16[512,128]{1,0:T(8,128)(2,1)S(1)}, bf16[512,128]{1,0:T(8,128)(2,1)S(1)}, u32[]{:S(2)}, u32[]{:S(2)}) %collective-permute-start.18) | collective-permute-done | bytes 131104 | tf_op jit(solution)/shard_map/ppermute | solution.py:345
  95.0 0.7 shard_map.109
  (22 shorter events, 0.1 us)
Async XLA Ops:
  0.6 18.2 %collective-permute-start.4 = (bf16[256,2048]{1,0:T(8,128)(2,1)}, bf16[256,2048]{1,0:T(8,128)(2,1)S(1)}, u32[]{:S(2)}, u32[]{:S(2)}) collective-permute-start(bf16[256,2048]{1,0:T(8,128)(2,1)} %own_ref.1), channel_id=1, source_target_pairs={{0,1},{1,0},{2,3},{3,2},{4,5},{5,4},{6,7},{7,6},{8,9},{9,8},{10,11... | collective-permute-start | bytes 3145736 | tf_op jit(solution)/shard_map/ppermute | solution.py:345
  1.4 2.6 %collective-permute-start = (bf16[256,128]{1,0:T(8,128)(2,1)}, bf16[256,128]{1,0:T(8,128)(2,1)S(1)}, u32[]{:S(2)}, u32[]{:S(2)}) collective-permute-start(bf16[256,128]{1,0:T(8,128)(2,1)} %refs_0_.1), channel_id=1, source_target_pairs={{0,1},{1,0},{2,3},{3,2},{4,5},{5,4},{6,7},{7,6},{8,9},{9,8},{10,11... | collective-permute-start | bytes 196616 | tf_op jit(solution)/shard_map/ppermute | solution.py:345
  1.5 2.6 %collective-permute-start.1 = (bf16[256,128]{1,0:T(8,128)(2,1)}, bf16[256,128]{1,0:T(8,128)(2,1)S(1)}, u32[]{:S(2)}, u32[]{:S(2)}) collective-permute-start(bf16[256,128]{1,0:T(8,128)(2,1)} %refs_1_.1), channel_id=1, source_target_pairs={{0,1},{1,0},{2,3},{3,2},{4,5},{5,4},{6,7},{7,6},{8,9},{9,8},{10,11... | collective-permute-start | bytes 196616 | tf_op jit(solution)/shard_map/ppermute | solution.py:345
  4.1 0.8 copy-start.3
  4.9 0.8 copy-start.4
  5.8 38.5 %copy-start.5 = (bf16[256,512]{1,0:T(8,128)(2,1)S(1)}, bf16[256,512]{1,0:T(8,128)(2,1)}, u32[]{:S(2)}) copy-start(bf16[256,512]{1,0:T(8,128)(2,1)} %q_ref.1) | copy-start | bytes 786436
  5.8 38.5 %copy-start.6 = (s32[64]{0:T(128)S(1)}, s32[64]{0:T(128)}, u32[]{:S(2)}) copy-start(s32[64]{0:T(128)} %param.11) | copy-start | bytes 772
  5.8 38.5 %copy-start.7 = (s32[64]{0:T(128)S(1)}, s32[64]{0:T(128)}, u32[]{:S(2)}) copy-start(s32[64]{0:T(128)} %param.12) | copy-start | bytes 772
  5.8 18.3 %collective-permute-start.3 = (bf16[1024,128]{1,0:T(8,128)(2,1)S(1)}, bf16[1024,128]{1,0:T(8,128)(2,1)S(1)}, u32[]{:S(2)}, u32[]{:S(2)}) collective-permute-start(bf16[1024,128]{1,0:T(8,128)(2,1)S(1)} %shard_map.102), channel_id=1, source_target_pairs={{0,4},{2,6},{4,8},{6,10},{8,12},{10,14},{12,16},{14,18},{16,20},{1... | collective-permute-start | bytes 786440 | tf_op jit(solution)/shard_map/ppermute | solution.py:342
  16.2 17.0 %collective-permute-start.2 = (bf16[1024,128]{1,0:T(8,128)(2,1)S(1)}, bf16[1024,128]{1,0:T(8,128)(2,1)S(1)}, u32[]{:S(2)}, u32[]{:S(2)}) collective-permute-start(bf16[1024,128]{1,0:T(8,128)(2,1)S(1)} %shard_map.102), channel_id=1, source_target_pairs={{0,2},{2,4},{4,6},{6,8},{8,10},{10,12},{12,14},{14,16},{16,18},{18... | collective-permute-start | bytes 786440 | tf_op jit(solution)/shard_map/ppermute | solution.py:342
  18.9 2.2 %copy-start = (bf16[4096,512]{1,0:T(8,128)(2,1)S(1)}, bf16[4096,512]{1,0:T(8,128)(2,1)}, u32[]{:S(2)}) copy-start(bf16[4096,512]{1,0:T(8,128)(2,1)} %w_ref.5) | copy-start | bytes 12582916
  21.1 1.2 %copy-start.2 = (bf16[256,2048]{1,0:T(8,128)(2,1)S(1)}, bf16[256,2048]{1,0:T(8,128)(2,1)}, u32[]{:S(2)}) copy-start(bf16[256,2048]{1,0:T(8,128)(2,1)} %own_ref.1) | copy-start | bytes 3145732
  24.1 9.9 %collective-permute-start.5 = (bf16[1024,128]{1,0:T(8,128)(2,1)S(1)}, bf16[1024,128]{1,0:T(8,128)(2,1)S(1)}, u32[]{:S(2)}, u32[]{:S(2)}) collective-permute-start(bf16[1024,128]{1,0:T(8,128)(2,1)S(1)} %collective-permute-done.3.refs_1_), channel_id=1, source_target_pairs={{0,2},{2,4},{4,6},{6,8},{8,10},{10,12},{12,14},{14,16},{16,18},{18... | collective-permute-start | bytes 786440 | tf_op jit(solution)/shard_map/ppermute | solution.py:342
  28.1 10.2 %collective-permute-start.6 = (bf16[1024,128]{1,0:T(8,128)(2,1)S(1)}, bf16[1024,128]{1,0:T(8,128)(2,1)S(1)}, u32[]{:S(2)}, u32[]{:S(2)}) collective-permute-start(bf16[1024,128]{1,0:T(8,128)(2,1)S(1)} %collective-permute-done.3.refs_1_), channel_id=1, source_target_pairs={{0,4},{2,6},{4,8},{6,10},{8,12},{10,14},{12,16},{14,18},{16,20},{1... | collective-permute-start | bytes 786440 | tf_op jit(solution)/shard_map/ppermute | solution.py:342
  33.2 10.1 %collective-permute-start.7 = (bf16[512,128]{1,0:T(8,128)(2,1)S(1)}, bf16[512,128]{1,0:T(8,128)(2,1)S(1)}, u32[]{:S(2)}, u32[]{:S(2)}) collective-permute-start(bf16[512,128]{1,0:T(8,128)(2,1)S(1)} %slice.37), channel_id=1, source_target_pairs={{0,1},{1,0},{2,3},{3,2},{4,5},{5,4},{6,7},{7,6},{8,9},{9,8},{10,11... | collective-permute-start | bytes 393224 | tf_op jit(solution)/shard_map/ppermute | solution.py:345
  33.3 10.0 %collective-permute-start.8 = (bf16[512,128]{1,0:T(8,128)(2,1)S(1)}, bf16[512,128]{1,0:T(8,128)(2,1)S(1)}, u32[]{:S(2)}, u32[]{:S(2)}) collective-permute-start(bf16[512,128]{1,0:T(8,128)(2,1)S(1)} %slice.29), channel_id=1, source_target_pairs={{0,1},{1,0},{2,3},{3,2},{4,5},{5,4},{6,7},{7,6},{8,9},{9,8},{10,11... | collective-permute-start | bytes 393224 | tf_op jit(solution)/shard_map/ppermute | solution.py:345
  33.9 9.4 %collective-permute-start.9 = (bf16[512,128]{1,0:T(8,128)(2,1)S(1)}, bf16[512,128]{1,0:T(8,128)(2,1)S(1)}, u32[]{:S(2)}, u32[]{:S(2)}) collective-permute-start(bf16[512,128]{1,0:T(8,128)(2,1)S(1)} %slice.38), channel_id=1, source_target_pairs={{0,1},{1,0},{2,3},{3,2},{4,5},{5,4},{6,7},{7,6},{8,9},{9,8},{10,11... | collective-permute-start | bytes 393224 | tf_op jit(solution)/shard_map/ppermute | solution.py:345
  38.3 5.9 %collective-permute-start.10 = (bf16[512,128]{1,0:T(8,128)(2,1)S(1)}, bf16[512,128]{1,0:T(8,128)(2,1)S(1)}, u32[]{:S(2)}, u32[]{:S(2)}) collective-permute-start(bf16[512,128]{1,0:T(8,128)(2,1)S(1)} %slice.39), channel_id=1, source_target_pairs={{0,1},{1,0},{2,3},{3,2},{4,5},{5,4},{6,7},{7,6},{8,9},{9,8},{10,11... | collective-permute-start | bytes 393224 | tf_op jit(solution)/shard_map/ppermute | solution.py:345
  44.2 13.0 %copy-start.1 = (bf16[4096,512]{1,0:T(8,128)(2,1)S(1)}, bf16[4096,512]{1,0:T(8,128)(2,1)}, u32[]{:S(2)}) copy-start(bf16[4096,512]{1,0:T(8,128)(2,1)} %w_ref.5) | copy-start | bytes 12582916
  58.3 23.7 %collective-permute-start.15 = (bf16[256,2048]{1,0:T(8,128)(2,1)S(1)}, bf16[256,2048]{1,0:T(8,128)(2,1)S(1)}, u32[]{:S(2)}, u32[]{:S(2)}) collective-permute-start(bf16[256,2048]{1,0:T(8,128)(2,1)S(1)} %shard_map.107), channel_id=1, source_target_pairs={{0,1},{1,0},{2,3},{3,2},{4,5},{5,4},{6,7},{7,6},{8,9},{9,8},{10,11... | collective-permute-start | bytes 3145736 | tf_op jit(solution)/shard_map/ppermute | solution.py:345
  58.8 3.0 %collective-permute-start.11 = (bf16[2048,128]{1,0:T(8,128)(2,1)S(1)}, bf16[2048,128]{1,0:T(8,128)(2,1)S(1)}, u32[]{:S(2)}, u32[]{:S(2)}) collective-permute-start(bf16[2048,128]{1,0:T(8,128)(2,1)S(1)} %get-tuple-element.21), channel_id=1, source_target_pairs={{0,1},{1,0},{2,3},{3,2},{4,5},{5,4},{6,7},{7,6},{8,9},{9,8},{10,11... | collective-permute-start | bytes 1572872 | tf_op jit(solution)/shard_map/ppermute | solution.py:345
  61.9 10.7 %collective-permute-start.12 = (bf16[1024,128]{1,0:T(8,128)(2,1)S(1)}, bf16[1024,128]{1,0:T(8,128)(2,1)S(1)}, u32[]{:S(2)}, u32[]{:S(2)}) collective-permute-start(bf16[1024,128]{1,0:T(8,128)(2,1)S(1)} %get-tuple-element.22), channel_id=1, source_target_pairs={{0,4},{2,6},{4,8},{6,10},{8,12},{10,14},{12,16},{14,18},{16,20},{1... | collective-permute-start | bytes 786440 | tf_op jit(solution)/shard_map/ppermute | solution.py:342
  63.8 12.0 %collective-permute-start.13 = (bf16[1024,128]{1,0:T(8,128)(2,1)S(1)}, bf16[1024,128]{1,0:T(8,128)(2,1)S(1)}, u32[]{:S(2)}, u32[]{:S(2)}) collective-permute-start(bf16[1024,128]{1,0:T(8,128)(2,1)S(1)} %get-tuple-element.23), channel_id=1, source_target_pairs={{0,2},{2,4},{4,6},{6,8},{8,10},{10,12},{12,14},{14,16},{16,18},{18... | collective-permute-start | bytes 786440 | tf_op jit(solution)/shard_map/ppermute | solution.py:342
  70.7 8.2 %collective-permute-start.16 = (bf16[1024,128]{1,0:T(8,128)(2,1)S(1)}, bf16[1024,128]{1,0:T(8,128)(2,1)S(1)}, u32[]{:S(2)}, u32[]{:S(2)}) collective-permute-start(bf16[1024,128]{1,0:T(8,128)(2,1)S(1)} %get-tuple-element.28), channel_id=1, source_target_pairs={{0,2},{2,4},{4,6},{6,8},{8,10},{10,12},{12,14},{14,16},{16,18},{18... | collective-permute-start | bytes 786440 | tf_op jit(solution)/shard_map/ppermute | solution.py:342
  75.9 10.3 %collective-permute-start.14 = (bf16[1024,128]{1,0:T(8,128)(2,1)S(1)}, bf16[1024,128]{1,0:T(8,128)(2,1)S(1)}, u32[]{:S(2)}, u32[]{:S(2)}) collective-permute-start(bf16[1024,128]{1,0:T(8,128)(2,1)S(1)} %shard_map.106), channel_id=1, source_target_pairs={{0,4},{2,6},{4,8},{6,10},{8,12},{10,14},{12,16},{14,18},{16,20},{1... | collective-permute-start | bytes 786440 | tf_op jit(solution)/shard_map/ppermute | solution.py:342
  78.8 15.2 %collective-permute-start.17 = (bf16[512,128]{1,0:T(8,128)(2,1)S(1)}, bf16[512,128]{1,0:T(8,128)(2,1)S(1)}, u32[]{:S(2)}, u32[]{:S(2)}) collective-permute-start(bf16[512,128]{1,0:T(8,128)(2,1)S(1)} %get-tuple-element.34), channel_id=1, source_target_pairs={{0,1},{1,0},{2,3},{3,2},{4,5},{5,4},{6,7},{7,6},{8,9},{9,8},{10,11... | collective-permute-start | bytes 393224 | tf_op jit(solution)/shard_map/ppermute | solution.py:345
  86.2 8.8 %collective-permute-start.18 = (bf16[512,128]{1,0:T(8,128)(2,1)S(1)}, bf16[512,128]{1,0:T(8,128)(2,1)S(1)}, u32[]{:S(2)}, u32[]{:S(2)}) collective-permute-start(bf16[512,128]{1,0:T(8,128)(2,1)S(1)} %get-tuple-element.32), channel_id=1, source_target_pairs={{0,1},{1,0},{2,3},{3,2},{4,5},{5,4},{6,7},{7,6},{8,9},{9,8},{10,11... | collective-permute-start | bytes 393224 | tf_op jit(solution)/shard_map/ppermute | solution.py:345

commit v2 on v1

v2 whole, which is shorter than its diff:
```python
import math

import jax
import jax.numpy as jnp
from jax import lax
from jax.experimental import pallas as pl
from jax.experimental.pallas import tpu as pltpu
from jax.sharding import PartitionSpec as P

HQ = 8
HK = 2
DH = 128
SPAN = 4
ROWS = 256
GROUPS = HQ // HK
WIDE = 2 * SPAN + 1
REACH = 2
NEAR = 2 * REACH + 1
FAR = WIDE - NEAR
SUB = 128
SUBS = ROWS // SUB
TILE = GROUPS * SUB
STACK = SUBS * TILE
CHUNK = 256
CHUNKS = TILE // CHUNK
NEG = -1e30
MASKED = -2e30
BIG = 60 * 1024 * 1024
SCALE = 1.0 / math.sqrt(DH)
SCALE2 = SCALE / math.log(2.0)
VMEM = pl.BlockSpec(memory_space=pltpu.VMEM)
ANY = pl.BlockSpec(memory_space=pl.ANY)
SMALL = pltpu.CompilerParams(vmem_limit_bytes=4 * 1024 * 1024)
SMEM = pl.BlockSpec(memory_space=pltpu.SMEM)


def dot_nn(a, b):
    return lax.dot_general(a, b, (((1,), (0,)), ((), ())), preferred_element_type=jnp.float32)


def dot_nt(a, b):
    return lax.dot_general(a, b, (((1,), (1,)), ((), ())), preferred_element_type=jnp.float32)


def limits(index, lengths_row, full_row):
    n = lengths_row.shape[1]
    row = lax.broadcasted_iota(jnp.int32, (n, n), 0)
    col = lax.broadcasted_iota(jnp.int32, (n, n), 1)
    ends = jnp.sum(jnp.where(col <= row, lengths_row, 0), axis=1, keepdims=True)
    starts = jnp.sum(jnp.where(col < row, lengths_row, 0), axis=1, keepdims=True)
    full = jnp.sum(jnp.where(col == row, full_row, 0), axis=1, keepdims=True)
    pos = index * ROWS + lax.broadcasted_iota(jnp.int32, (n, ROWS), 1)
    inside = (pos >= starts) & (pos < ends)
    low = jnp.sum(jnp.where(inside, starts, 0), axis=0, keepdims=True)
    high = jnp.sum(jnp.where(inside, jnp.where(full == 1, ends, pos + 1), 0), axis=0, keepdims=True)
    return low, high


def rows_of(r):
    return pl.ds(pl.multiple_of(r * ROWS, ROWS), ROWS)


def keys_of(r):
    return pl.ds(pl.multiple_of(r * 2 * ROWS, ROWS), ROWS)


def vals_of(r):
    return pl.ds(pl.multiple_of(r * 2 * ROWS + ROWS, ROWS), ROWS)


def pair_of(r):
    return pl.ds(pl.multiple_of(r * 2 * ROWS, ROWS), 2 * ROWS)


def tile_cols(sub, c):
    return slice(sub * TILE + c * CHUNK, sub * TILE + (c + 1) * CHUNK)


def staged(sub, h):
    return slice(sub * TILE + h * SUB, sub * TILE + (h + 1) * SUB)


def sub_rows(sub):
    return slice(sub * SUB, (sub + 1) * SUB)


def head_cols(h):
    return slice(h * DH, (h + 1) * DH)


def fold_block(sub, at, key_pos, low, high, win, q_st, acc, p_ref, tops, state):
    keys = win[keys_of(at), :]
    vals_t = win[vals_of(at), :].T
    valid = (key_pos >= low) & (key_pos < high)
    out = []
    for c in range(CHUNKS):
        cols = tile_cols(sub, c)
        top, total = state[c]
        s = jnp.where(valid, dot_nt(keys, q_st[cols, :]) * SCALE2, MASKED)
        new = jnp.maximum(top, jnp.max(s, axis=0, keepdims=True))
        p = jnp.exp2(s - new)
        fix = jnp.exp2(top - new)
        out.append((new, total * fix + jnp.sum(p, axis=0, keepdims=True)))
        p = p.astype(jnp.bfloat16)
        p_ref[rows_of(at), cols] = p
        tops[pl.ds(at, 1), cols] = new
        acc[:, cols] = acc[:, cols] * fix + dot_nn(vals_t, p)
    return tuple(out)


def back_block(sub, at, win, q_st, do_st, p_ref, tops, top, inv, delta, dq_acc, dkv):
    keys_t = win[keys_of(at), :].T
    vals = win[vals_of(at), :]
    dk = jnp.zeros((ROWS, DH), jnp.float32)
    dv = jnp.zeros((ROWS, DH), jnp.float32)
    for c in range(CHUNKS):
        cols = tile_cols(sub, c)
        share = jnp.exp2(tops[pl.ds(at, 1), cols] - top[:, cols]) * inv[:, cols]
        w = p_ref[rows_of(at), cols].astype(jnp.float32) * share
        dp = dot_nt(vals, do_st[cols, :])
        ds = (w * (dp - delta[:, cols])).astype(jnp.bfloat16)
        dq_acc[:, cols] += dot_nn(keys_t, ds)
        dk += dot_nn(ds, q_st[cols, :])
        dv += dot_nn(w.astype(jnp.bfloat16), do_st[cols, :])
    dkv[keys_of(at), :] += dk * SCALE
    dkv[vals_of(at), :] += dv


def key_positions(first):
    return first + lax.broadcasted_iota(jnp.int32, (ROWS, CHUNK), 0)


def near_forward_kernel(
    place_ref, len_ref, full_ref, q_ref, own_ref, at1, at2, twin1, twin2,
    range_ref, limit_ref, q_st, win, acc, p_ref, tops, state_ref,
):
    index = place_ref[0]
    way = 1 - 2 * place_ref[1]
    base = index - SPAN
    low, high = limits(index, len_ref[...], full_ref[...])
    for sub in range(SUBS):
        for h in range(GROUPS):
            q_st[staged(sub, h), :] = q_ref[sub_rows(sub), head_cols(h)]
    win[pair_of(REACH), :] = own_ref[0 : 2 * ROWS, :]
    for k, (ring, twin) in enumerate(((at1, twin1), (at2, twin2))):
        win[pair_of(REACH - (k + 1) * way), :] = ring[0 : 2 * ROWS, :]
        win[pair_of(REACH + (k + 1) * way), :] = twin[...]
    acc[...] = jnp.zeros_like(acc)
    limit_ref[...] = jnp.zeros_like(limit_ref)
    for sub in range(SUBS):
        cut = slice(sub * SUB, (sub + 1) * SUB)
        low_row = jnp.concatenate([low[:, cut]] * (CHUNK // SUB), axis=1)
        high_row = jnp.concatenate([high[:, cut]] * (CHUNK // SUB), axis=1)
        limit_ref[2 * sub : 2 * sub + 1, :] = low_row
        limit_ref[2 * sub + 1 : 2 * sub + 2, :] = high_row
        r_low = jnp.maximum(jnp.min(low[:, cut]) // ROWS - base, 0)
        r_high = jnp.minimum((jnp.max(high[:, cut]) + ROWS - 1) // ROWS - base, WIDE)
        range_ref[2 * sub] = r_low
        range_ref[2 * sub + 1] = r_high

        def body(at, state):
            key_pos = key_positions((base + SPAN - REACH + at) * ROWS)
            return fold_block(sub, at, key_pos, low_row, high_row, win, q_st, acc, p_ref, tops, state)

        none = (jnp.full((1, CHUNK), NEG, jnp.float32), jnp.zeros((1, CHUNK), jnp.float32))
        skip = SPAN - REACH
        state = lax.fori_loop(
            jnp.maximum(r_low - skip, 0), jnp.minimum(r_high - skip, NEAR), body, (none,) * CHUNKS
        )
        for c in range(CHUNKS):
            state_ref[0:1, tile_cols(sub, c)] = state[c][0]
            state_ref[1:2, tile_cols(sub, c)] = state[c][1]


def far_kernel(
    place_ref, range_ref, limit_ref, q_st, acc1, state_ref, at3, at4, twin3, twin4, do_ref,
    attn_ref, do_st, stats_ref, dq_acc, ahead_ref, across_ref,
    win, acc, p_ref, tops, dkv,
):
    index = place_ref[0]
    core = place_ref[1]
    base = index - SPAN

    def slot(n):
        return n + core * (FAR - 1 - 2 * n)

    for n, part in enumerate((at4, at3, twin3, twin4)):
        win[pair_of(slot(n)), :] = part[0 : 2 * ROWS, :]
    acc[...] = acc1[...]
    tops[...] = jnp.zeros_like(tops)
    dkv[...] = jnp.zeros_like(dkv)
    dq_acc[...] = jnp.zeros_like(dq_acc)
    stats_ref[...] = jnp.zeros_like(stats_ref)
    side = FAR // 2
    gap = WIDE - FAR
    spans = []
    for sub in range(SUBS):
        r_low = range_ref[2 * sub]
        r_high = range_ref[2 * sub + 1]
        spans.append(((r_low, jnp.minimum(r_high, side)), (jnp.maximum(r_low - gap, side), r_high - gap)))
        low_row = limit_ref[2 * sub : 2 * sub + 1, :]
        high_row = limit_ref[2 * sub + 1 : 2 * sub + 2, :]

        def body(at, state):
            r = jnp.where(at < side, at, at + gap)
            key_pos = key_positions((base + r) * ROWS)
            return fold_block(sub, at, key_pos, low_row, high_row, win, q_st, acc, p_ref, tops, state)

        state = tuple(
            (state_ref[0:1, tile_cols(sub, c)], state_ref[1:2, tile_cols(sub, c)]) for c in range(CHUNKS)
        )
        for lower, upper in spans[sub]:
            state = lax.fori_loop(lower, upper, body, state)
        for c in range(CHUNKS):
            cols = tile_cols(sub, c)
            stats_ref[0:1, cols] = state[c][0]
            stats_ref[1:2, cols] = 1.0 / state[c][1]
        for h in range(GROUPS):
            cols = staged(sub, h)
            attn_t = (acc[:, cols] * stats_ref[1:2, cols]).astype(jnp.bfloat16).astype(jnp.float32)
            attn_ref[sub_rows(sub), head_cols(h)] = attn_t.T.astype(jnp.bfloat16)
            grad = do_ref[sub_rows(sub), head_cols(h)]
            do_st[cols, :] = grad
            stats_ref[2:3, cols] = jnp.sum(attn_t * grad.astype(jnp.float32).T, axis=0, keepdims=True)
    for sub in range(SUBS):
        def back(at, carry):
            back_block(
                sub, at, win, q_st, do_st, p_ref, tops,
                stats_ref[0:1, :], stats_ref[1:2, :], stats_ref[2:3, :], dq_acc, dkv,
            )
            return carry

        for lower, upper in spans[sub]:
            lax.fori_loop(lower, upper, back, 0)
    for n in range(side):
        ahead_ref[pair_of(n), :] = dkv[pair_of(slot(side + n)), :].astype(jnp.bfloat16)
        across_ref[pair_of(n), :] = dkv[pair_of(slot(side - 1 - n)), :].astype(jnp.bfloat16)


def near_backward_kernel(
    place_ref, range_ref, q_st, do_st, win, p_ref, tops, stats_ref, dq_far,
    dq_ref, ahead_ref, across_ref, mid_ref,
    dq_acc, dkv,
):
    way = 1 - 2 * place_ref[1]
    skip = SPAN - REACH
    dkv[...] = jnp.zeros_like(dkv)
    dq_acc[...] = dq_far[...]
    for sub in range(SUBS):
        def back(at, carry):
            back_block(
                sub, at, win, q_st, do_st, p_ref, tops,
                stats_ref[0:1, :], stats_ref[1:2, :], stats_ref[2:3, :], dq_acc, dkv,
            )
            return carry

        lax.fori_loop(
            jnp.maximum(range_ref[2 * sub] - skip, 0), jnp.minimum(range_ref[2 * sub + 1] - skip, NEAR), back, 0
        )
    for sub in range(SUBS):
        for h in range(GROUPS):
            dq_ref[sub_rows(sub), head_cols(h)] = (dq_acc[:, staged(sub, h)] * SCALE).T.astype(jnp.bfloat16)
    mid_ref[...] = dkv[pair_of(REACH), :].astype(jnp.bfloat16)
    for k in range(1, REACH + 1):
        ahead_ref[pair_of(k - 1), :] = dkv[pair_of(REACH + k * way), :].astype(jnp.bfloat16)
        across_ref[pair_of(k - 1), :] = dkv[pair_of(REACH - k * way), :].astype(jnp.bfloat16)


def bf16(*shape):
    return jax.ShapeDtypeStruct(shape, jnp.bfloat16)


def f32(*shape):
    return jax.ShapeDtypeStruct(shape, jnp.float32)


def i32(*shape):
    return jax.ShapeDtypeStruct(shape, jnp.int32)


def near_forward(place, lengths, full, q, own, at1, at2, twin1, twin2):
    return pl.pallas_call(
        near_forward_kernel,
        out_shape=(
            i32(2 * SUBS), i32(8, CHUNK), bf16(STACK, DH), bf16(NEAR * 2 * ROWS, DH),
            f32(DH, STACK), bf16(NEAR * ROWS, STACK), f32(8, STACK), f32(8, STACK),
        ),
        in_specs=[SMEM] + [VMEM] * 8,
        out_specs=(SMEM,) + (VMEM,) * 7,
        compiler_params=pltpu.CompilerParams(vmem_limit_bytes=16 * 1024 * 1024),
        cost_estimate=pl.CostEstimate(flops=10**9, bytes_accessed=6 * 10**6, transcendentals=10**6),
    )(place, lengths, full, q, own, at1, at2, twin1, twin2)


def far_part(place, ranges, limit, q_st, acc, state, at3, at4, twin3, twin4, do):
    return pl.pallas_call(
        far_kernel,
        out_shape=(
            bf16(ROWS, GROUPS * DH), bf16(STACK, DH), f32(8, STACK), f32(DH, STACK),
            bf16(FAR * ROWS, DH), bf16(FAR * ROWS, DH),
        ),
        in_specs=[SMEM, SMEM] + [VMEM] * 9,
        out_specs=(VMEM,) * 6,
        scratch_shapes=[
            pltpu.VMEM((FAR * 2 * ROWS, DH), jnp.bfloat16),
            pltpu.VMEM((DH, STACK), jnp.float32),
            pltpu.VMEM((FAR * ROWS, STACK), jnp.bfloat16),
            pltpu.VMEM((8, STACK), jnp.float32),
            pltpu.VMEM((FAR * 2 * ROWS, DH), jnp.float32),
        ],
        compiler_params=pltpu.CompilerParams(vmem_limit_bytes=16 * 1024 * 1024),
        cost_estimate=pl.CostEstimate(flops=5 * 10**8, bytes_accessed=4 * 10**6, transcendentals=10**6),
    )(place, ranges, limit, q_st, acc, state, at3, at4, twin3, twin4, do)


def near_backward(place, ranges, q_st, do_st, win, p, tops, stats, dq_far):
    return pl.pallas_call(
        near_backward_kernel,
        out_shape=(
            bf16(ROWS, GROUPS * DH), bf16(REACH * 2 * ROWS, DH), bf16(REACH * 2 * ROWS, DH), bf16(2 * ROWS, DH),
        ),
        in_specs=[SMEM, SMEM] + [VMEM] * 7,
        out_specs=(VMEM,) * 4,
        scratch_shapes=[
            pltpu.VMEM((DH, STACK), jnp.float32),
            pltpu.VMEM((NEAR * 2 * ROWS, DH), jnp.float32),
        ],
        compiler_params=pltpu.CompilerParams(vmem_limit_bytes=16 * 1024 * 1024),
        cost_estimate=pl.CostEstimate(flops=2 * 10**9, bytes_accessed=6 * 10**6, transcendentals=10**6),
    )(place, ranges, q_st, do_st, win, p, tops, stats, dq_far)


def small_call(body, out_rows, *args):
    shapes = [jax.ShapeDtypeStruct((rows, DH), jnp.bfloat16) for rows in out_rows]
    return pl.pallas_call(
        body,
        out_shape=shapes,
        in_specs=[VMEM] * len(args),
        out_specs=[VMEM] * len(shapes),
        compiler_params=SMALL,
        cost_estimate=pl.CostEstimate(flops=10**5, bytes_accessed=10**5, transcendentals=0),
    )(*args)


def stacked(*parts):
    n = len(parts)
    total = sum(part.shape[0] for part in parts)

    def body(*refs):
        sems = refs[n + 1]
        copies = []
        at = 0
        for k in range(n):
            rows = parts[k].shape[0]
            copies.append(pltpu.make_async_copy(refs[k], refs[n].at[at : at + rows, :], sems.at[k]))
            copies[k].start()
            at += rows
        for copy in copies:
            copy.wait()

    return pl.pallas_call(
        body,
        out_shape=bf16(total, DH),
        in_specs=[ANY] * n,
        out_specs=ANY,
        scratch_shapes=[pltpu.SemaphoreType.DMA((n,))],
        compiler_params=pltpu.CompilerParams(vmem_limit_bytes=BIG),
        cost_estimate=pl.CostEstimate(flops=0, bytes_accessed=10**6, transcendentals=0),
    )(*parts)


def both_heads(ahead, across, which):
    n = 2 * ROWS

    def body(ahead_ref, across_ref, *out_refs):
        for k, out_ref in zip(which, out_refs):
            out_ref[0:n, :] = ahead_ref[k * n : (k + 1) * n, :]
            out_ref[n : 2 * n, :] = across_ref[k * n : (k + 1) * n, :]

    return small_call(body, [2 * n] * len(which), ahead, across)


def summed(ahead, across, k, *others):
    n = 2 * ROWS

    def body(ahead_ref, across_ref, *refs):
        for at, ref in ((0, ahead_ref), (n, across_ref)):
            total = ref[k * n : (k + 1) * n, :].astype(jnp.float32)
            for other in refs[:-1]:
                total += other[at : at + n, :].astype(jnp.float32)
            refs[-1][at : at + n, :] = total.astype(jnp.bfloat16)

    return small_call(body, [2 * n], ahead, across, *others)[0]


def last_sum(mid, near, far, near_twin, far_twin):
    n = 2 * ROWS

    def body(*refs):
        for out_ref, rows in ((refs[-2], slice(0, ROWS)), (refs[-1], slice(ROWS, n))):
            total = refs[0][rows, :].astype(jnp.float32)
            for ref in refs[1:-2]:
                total += ref[rows, :].astype(jnp.float32)
            out_ref[...] = total.astype(jnp.bfloat16)

    return small_call(body, [ROWS, ROWS], mid, near, far, near_twin, far_twin)


def project_back(core, own, other, w):
    rows, depth = own.shape
    cols = w.shape[1]

    def body(core_ref, own_ref, other_ref, w_ref, out_ref, a_buf, w_buf, sems):
        core = core_ref[0]
        copies = []
        for n, (a_ref, half) in enumerate(((own_ref, core), (other_ref, 1 - core))):
            where = pl.ds(pl.multiple_of(half * depth, depth), depth)
            copies.append(pltpu.make_async_copy(a_ref, a_buf.at[n], sems.at[0, n]))
            copies.append(pltpu.make_async_copy(w_ref.at[where, :], w_buf.at[n], sems.at[1, n]))
        for copy in copies:
            copy.start()
        copies[0].wait()
        copies[1].wait()
        part = dot_nn(a_buf[0], w_buf[0])
        copies[2].wait()
        copies[3].wait()
        out_ref[...] = (part + dot_nn(a_buf[1], w_buf[1])).astype(jnp.bfloat16)

    return pl.pallas_call(
        body,
        out_shape=bf16(rows, cols),
        in_specs=[SMEM, ANY, ANY, ANY],
        out_specs=VMEM,
        scratch_shapes=[
            pltpu.VMEM((2, rows, depth), jnp.bfloat16),
            pltpu.VMEM((2, depth, cols), jnp.bfloat16),
            pltpu.SemaphoreType.DMA((2, 2)),
        ],
        compiler_params=pltpu.CompilerParams(vmem_limit_bytes=BIG),
        cost_estimate=pl.CostEstimate(flops=4 * rows * depth * cols, bytes_accessed=6 * 10**6, transcendentals=0),
    )(core, own, other, w)


def project(half, attn, w, other=None):
    rows, depth = attn.shape
    cols = w.shape[0] // 2
    parts = 4
    wide = cols // parts
    more = () if other is None else (other,)

    def body(half_ref, a_ref, w_ref, *refs):
        out_ref, w_buf, sems = refs[-3:]
        copies = []
        for n in range(parts):
            where = pl.ds(pl.multiple_of(half_ref[0] * cols + n * wide, wide), wide)
            copies.append(pltpu.make_async_copy(w_ref.at[where, :], w_buf.at[n], sems.at[n]))
            copies[n].start()
        for n in range(parts):
            copies[n].wait()
            at = slice(n * wide, (n + 1) * wide)
            out = dot_nt(a_ref[...], w_buf[n])
            if more:
                out += refs[0][:, at].astype(jnp.float32)
            out_ref[:, at] = out.astype(jnp.bfloat16)

    return pl.pallas_call(
        body,
        out_shape=bf16(rows, cols),
        in_specs=[SMEM, VMEM, ANY] + [VMEM] * len(more),
        out_specs=VMEM,
        scratch_shapes=[pltpu.VMEM((parts, wide, depth), jnp.bfloat16), pltpu.SemaphoreType.DMA((parts,))],
        compiler_params=pltpu.CompilerParams(vmem_limit_bytes=BIG),
        cost_estimate=pl.CostEstimate(flops=2 * rows * depth * cols, bytes_accessed=4 * 10**6, transcendentals=0),
    )(half, attn, w, *more)


def on_device(queries, keys, values, out_weight, doc_lengths, doc_full, out_grad):
    devices = lax.axis_size("cp")
    index = lax.axis_index("cp").astype(jnp.int32)
    core = lax.axis_index("hd").astype(jnp.int32)
    place = jnp.stack([index, core])
    core = core.reshape(1)
    half = 2 * ROWS

    def step(block, far):
        ways = [(2 * i, 2 * (i + far)) for i in range(devices - far)]
        ways += [(2 * (i + far) + 1, 2 * i + 1) for i in range(devices - far)]
        return lax.ppermute(block, ("cp", "hd"), ways)

    def twin(block):
        return lax.ppermute(block, "hd", [(0, 1), (1, 0)])

    other_keys, other_values, late_grad = lax.optimization_barrier((twin(keys), twin(values), out_grad))
    block = stacked(keys, values, other_keys, other_values)
    other_grad = twin(late_grad)
    at2 = step(block, 2)
    at1 = step(block, 1)
    attn_grad = project_back(core, out_grad, other_grad, out_weight)
    at2, attn_grad = lax.optimization_barrier((at2, attn_grad))
    at4 = step(at2, 2)
    at3 = step(at2, 1)
    twin1, twin2 = twin(at1[half:]), twin(at2[half:])
    ranges, limit, q_st, win, acc, p, tops, state = near_forward(
        place, doc_lengths.reshape(1, -1), doc_full.reshape(1, -1), queries, block, at1, at2, twin1, twin2
    )
    at3, at4, state = lax.optimization_barrier((at3, at4, state))
    twin3, twin4 = twin(at3[half:]), twin(at4[half:])
    attn, do_st, stats, dq_far, ahead, across = far_part(
        place, ranges, limit, q_st, acc, state, at3, at4, twin3, twin4, attn_grad
    )
    out3, out4 = both_heads(ahead, twin(across), (0, 1))
    in4 = step(out4, 2)
    in3 = step(out3, 1)
    query_grad, ahead, across, mid = near_backward(place, ranges, q_st, do_st, win, p, tops, stats, dq_far)
    attn, across = lax.optimization_barrier((attn, twin(across)))
    far = step(summed(ahead, across, 1, in4, in3), 2)
    near = step(both_heads(ahead, across, (0,))[0], 1)
    away = project(1 - core, attn, out_weight)
    layer_out = project(core, attn, out_weight, twin(away))
    far, near, layer_out = lax.optimization_barrier((far, near, layer_out))
    key_grad, value_grad = last_sum(mid, near, far, twin(near[half:]), twin(far[half:]))
    return (layer_out, query_grad, key_grad, value_grad)


def solution(mesh):
    placed = (P("cp", "hd"), P("cp", "hd"), P("cp", "hd"), P(None, "hd"), P(), P(), P("cp", "hd"))
    return jax.shard_map(
        on_device,
        mesh=mesh,
        in_specs=placed,
        out_specs=(P("cp", "hd"), P("cp", "hd"), P("cp", "hd"), P("cp", "hd")),
        check_vma=False,
    )
```

time: 95.7 us -> 108 us (1.13); the launches traced: 95.7 us -> 106 us
  Pallas kernels: 18.8 us -> 37.1 us
  waiting for transfers between devices: 16.2 us -> 13 us
  starting transfers between devices: 54.6 us -> 51.8 us
  local copies, waits for them, and re-layouts: 5.19 us -> 3.19 us
    pallas_call x4 -> x7, Pallas kernels: 17.9 us -> 36.2 us  [the longest x1 9.08 us: stacked(): pl.pallas_call(body, out_shape=bf16(total, DH), in_specs=[ANY] * n, out_s...]
    ppermute x8, waiting for transfers between devices: 9.24 us -> 4.18 us  [step(): return lax.ppermute(block, ('cp', 'hd'), ways)]
    ppermute x11 -> x12, starting transfers between devices: 18.9 us -> 15.5 us  [twin(): return lax.ppermute(block, 'hd', [(0, 1), (1, 0)])]
    unnamed x16 -> x20, local copies, waits for them, and re-layouts: 5.1 us -> 3.13 us
    ppermute x11 -> x12, waiting for transfers between devices: 6.94 us -> 8.85 us  [twin(): return lax.ppermute(block, 'hd', [(0, 1), (1, 0)])]
  transfers between devices with their start and end apart: 19 -> 20, of which waited for: 8 -> 11; matrix products, arithmetic and copies ran while one was open for 0% -> 0% of each run, Pallas kernels for 4% -> 23%
where the time goes in v2:
time: 108 us; the launch traced here: 106 us
  starting transfers between devices  51.8 us (48%)
  Pallas kernels  37.1 us (34%)
  waiting for transfers between devices  13 us (12%)
  local copies, waits for them, and re-layouts  3.19 us (3%)
    ppermute x8, starting transfers between devices, step(): return lax.ppermute(block, ('cp', 'hd'), ways)  36.3 us
    ppermute x12, starting transfers between devices, twin(): return lax.ppermute(block, 'hd', [(0, 1), (1, 0)])  15.5 us
    pallas_call x1, Pallas kernels, stacked(): pl.pallas_call(body, out_shape=bf16(total, DH), in_specs=[ANY] * n, out_s...  9.08 us
    pallas_call x2, Pallas kernels, project(): pl.pallas_call(body, out_shape=bf16(rows, cols), in_specs=[SMEM, VMEM, AN...  9.04 us
    ppermute x12, waiting for transfers between devices, twin(): return lax.ppermute(block, 'hd', [(0, 1), (1, 0)])  8.85 us
    pallas_call x1, Pallas kernels, near_forward(): pl.pallas_call(near_forward_kernel, out_shape=(i32(2 * SUBS), i32(8, CHUN...  6.1 us
    pallas_call x1, Pallas kernels, near_backward(): pl.pallas_call(near_backward_kernel, out_shape=(bf16(ROWS, GROUPS * DH),...  6.09 us
    pallas_call x1, Pallas kernels, project_back(): pl.pallas_call(body, out_shape=bf16(rows, cols), in_specs=[SMEM, ANY, ANY...  4.84 us
  transfers between devices with their start and end apart: 20, of which 11 were waited for; matrix products, arithmetic and copies ran while one was open for 0% of the time, Pallas kernels for 23%

profile of v2, /device:TPU:25, one launch (start us, length us, event | category | flops | bytes accessed | tf_op | source)
XLA Modules:
  0.0 106.2 jit_solution(202886637919625039)
XLA Ops:
  0.7 0.8 collective-permute-start
  1.4 0.1 collective-permute-start.1
  1.5 1.0 collective-permute-done.refs_2_
  2.5 0.3 collective-permute-done.1.refs_3_
  2.9 0.2 collective-permute-start.4
  3.1 0.1 copy-done.8
  3.2 0.4 copy-done.9
  3.5 9.1 %shard_map.102.own_ref = bf16[1024,128]{1,0:T(8,128)(2,1)} custom-call(bf16[256,128]{1,0:T(8,128)(2,1)} %refs_0_.1, bf16[256,128]{1,0:T(8,128)(2,1)} %refs_1_.1, bf16[256,128]{1,0:T(8,128)(2,1)} %copy-done.8, bf16[256,128]{1,0:T(8,128)(2,1)} %copy-done.9), custom_call_target="tpu_custom_call" | custom-call | bytes 1000000 | tf_op jit(solution)/shard_map/pallas_call | solution.py:361
  12.6 0.0 copy-start.1
  12.6 10.4 %collective-permute-start.3 = (bf16[1024,128]{1,0:T(8,128)(2,1)}, bf16[1024,128]{1,0:T(8,128)(2,1)S(1)}, u32[]{:S(2)}, u32[]{:S(2)}) collective-permute-start(bf16[1024,128]{1,0:T(8,128)(2,1)} %shard_map.102.own_ref), channel_id=1, source_target_pairs={{0,4},{2,6},{4,8},{6,10},{8,12},{10,14},{12,16},{14,18},{16,20},{1... | collective-permute-start | bytes 786440 | tf_op jit(solution)/shard_map/ppermute | solution.py:488
  23.1 2.6 %collective-permute-start.2 = (bf16[1024,128]{1,0:T(8,128)(2,1)}, bf16[1024,128]{1,0:T(8,128)(2,1)S(1)}, u32[]{:S(2)}, u32[]{:S(2)}) collective-permute-start(bf16[1024,128]{1,0:T(8,128)(2,1)} %shard_map.102.own_ref), channel_id=1, source_target_pairs={{0,2},{2,4},{4,6},{6,8},{8,10},{10,12},{12,14},{14,16},{16,18},{18... | collective-permute-start | bytes 786440 | tf_op jit(solution)/shard_map/ppermute | solution.py:488
  25.7 0.0 copy-start.7
  25.7 1.0 copy-done.7
  26.7 4.8 %shard_map.103.do_ref = bf16[256,512]{1,0:T(8,128)(2,1)} custom-call(s32[1]{0:T(128)} %bitcast.1.core_ref.half_ref, bf16[256,2048]{1,0:T(8,128)(2,1)} %own_ref.1, bf16[256,2048]{1,0:T(8,128)(2,1)} %copy-done.7, bf16[4096,512]{1,0:T(8,128)(2,1)} %w_ref.5), custom_call_target="tpu_custom_call" | custom-call | flops 1073741824 | bytes 6000000 | tf_op jit(solution)/shard_map/pallas_call | solution.py:429
  31.6 3.6 %collective-permute-start.7 = (bf16[1024,128]{1,0:T(8,128)(2,1)S(1)}, bf16[1024,128]{1,0:T(8,128)(2,1)S(1)}, u32[]{:S(2)}, u32[]{:S(2)}) collective-permute-start(bf16[1024,128]{1,0:T(8,128)(2,1)S(1)} %collective-permute-done.3.at2), channel_id=1, source_target_pairs={{0,2},{2,4},{4,6},{6,8},{8,10},{10,12},{12,14},{14,16},{16,18},{18... | collective-permute-start | bytes 786440 | tf_op jit(solution)/shard_map/ppermute | solution.py:488
  35.1 5.1 %collective-permute-start.8 = (bf16[1024,128]{1,0:T(8,128)(2,1)S(1)}, bf16[1024,128]{1,0:T(8,128)(2,1)S(1)}, u32[]{:S(2)}, u32[]{:S(2)}) collective-permute-start(bf16[1024,128]{1,0:T(8,128)(2,1)S(1)} %collective-permute-done.3.at2), channel_id=1, source_target_pairs={{0,4},{2,6},{4,8},{6,10},{8,12},{10,14},{12,16},{14,18},{16,20},{1... | collective-permute-start | bytes 786440 | tf_op jit(solution)/shard_map/ppermute | solution.py:488
  40.3 0.1 collective-permute-start.5
  40.4 0.6 collective-permute-start.6
  41.0 0.1 pad_add_fusion.place_ref
  41.0 0.7 collective-permute-done.5.twin1
  41.7 0.2 collective-permute-done.6.twin2
  42.0 6.1 %shard_map.104 = (s32[4]{0:T(128)S(1)}, s32[8,256]{1,0:T(8,128)S(1)}, bf16[1024,128]{1,0:T(8,128)(2,1)S(1)}, bf16[2560,128]{1,0:T(8,128)(2,1)S(1)}, f32[128,1024...) custom-call(s32[2]{0:T(128)S(1)} %pad_add_fusion.place_ref, ...), custom_call_target="tpu_custom_call" | custom-call | flops 1000000000 | bytes 6000000 | tf_op jit(solution)/shard_map/pallas_call | solution.py:282
  48.1 2.0 %collective-permute-start.10 = (bf16[512,128]{1,0:T(8,128)(2,1)S(1)}, bf16[512,128]{1,0:T(8,128)(2,1)S(1)}, u32[]{:S(2)}, u32[]{:S(2)}) collective-permute-start(bf16[512,128]{1,0:T(8,128)(2,1)S(1)} %slice.21), channel_id=1, source_target_pairs={{0,1},{1,0},{2,3},{3,2},{4,5},{5,4},{6,7},{7,6},{8,9},{9,8},{10,11... | collective-permute-start | bytes 393224 | tf_op jit(solution)/shard_map/ppermute | solution.py:491
  50.1 0.1 collective-permute-start.9
  50.2 0.9 collective-permute-done.10.twin4
  51.1 0.5 collective-permute-done.9.twin3
  51.5 1.1 %shard_map.105 = (bf16[256,512]{1,0:T(8,128)(2,1)S(1)}, bf16[1024,128]{1,0:T(8,128)(2,1)S(1)}, f32[8,1024]{1,0:T(8,128)S(1)}, f32[128,1024]{1,0:T(8,128)S(1)}, b...) custom-call(s32[2]{0:T(128)S(1)} %pad_add_fusion.place_ref, s32[4]{0:T(128)S(1)} %get-tuple-element.43.range_ref, ...), custom_call_target="tpu_custom_call" | custom-call | flops 500000000 | bytes 4000000 | tf_op jit(solution)/shard_map/pallas_call | solution.py:296
  52.6 0.7 copy-done
  53.3 6.1 %shard_map.106 = (bf16[256,512]{1,0:T(8,128)(2,1)}, bf16[1024,128]{1,0:T(8,128)(2,1)S(1)}, bf16[1024,128]{1,0:T(8,128)(2,1)S(1)}, bf16[512,128]{1,0:T(8,128)(2,1)S(1)}) custom-call(s32[2]{0:T(128)S(1)} %pad_add_fusion.place_ref, s32[4]{0:T(128)S(1)} %get-tuple-element.43.range_ref, bf16[1024,128]{1,0:T(8,128)(2,1)S(1)} %get-tuple-element.44.q_st, ...), custom_call_target="tpu_custom_call" | custom-call | flops 2000000000 | bytes 6000000 | tf_op jit(solution)/shard_map/pallas_call | solution.py:317
  59.4 0.1 collective-permute-start.11
  59.6 1.4 %collective-permute-done.11.across_ref = bf16[1024,128]{1,0:T(8,128)(2,1)S(1)} collective-permute-done((bf16[1024,128]{1,0:T(8,128)(2,1)S(1)}, bf16[1024,128]{1,0:T(8,128)(2,1)S(1)}, u32[]{:S(2)}, u32[]{:S(2)}) %collective-permute-start.11) | collective-permute-done | bytes 262176 | tf_op jit(solution)/shard_map/ppermute | solution.py:491
  61.0 4.3 %shard_map.110 = bf16[256,2048]{1,0:T(8,128)(2,1)} custom-call(s32[1]{0:T(128)S(6)} %sub.3.half_ref, bf16[256,512]{1,0:T(8,128)(2,1)} %copy-done, bf16[4096,512]{1,0:T(8,128)(2,1)} %w_ref.5), custom_call_target="tpu_custom_call" | custom-call | flops 536870912 | bytes 4000000 | tf_op jit(solution)/shard_map/pallas_call | solution.py:466
  65.3 0.2 collective-permute-start.17
  65.5 0.4 collective-permute-start.12
  65.9 2.5 %collective-permute-done.12.across_ref = bf16[1024,128]{1,0:T(8,128)(2,1)S(1)} collective-permute-done((bf16[1024,128]{1,0:T(8,128)(2,1)S(1)}, bf16[1024,128]{1,0:T(8,128)(2,1)S(1)}, u32[]{:S(2)}, u32[]{:S(2)}) %collective-permute-start.12) | collective-permute-done | bytes 262176 | tf_op jit(solution)/shard_map/ppermute | solution.py:491
  68.5 3.6 %collective-permute-start.13 = (bf16[1024,128]{1,0:T(8,128)(2,1)S(1)}, bf16[1024,128]{1,0:T(8,128)(2,1)S(1)}, u32[]{:S(2)}, u32[]{:S(2)}) collective-permute-start(bf16[1024,128]{1,0:T(8,128)(2,1)S(1)} %get-tuple-element.64), channel_id=1, source_target_pairs={{0,4},{2,6},{4,8},{6,10},{8,12},{10,14},{12,16},{14,18},{16,20},{1... | collective-permute-start | bytes 786440 | tf_op jit(solution)/shard_map/ppermute | solution.py:488
  72.1 4.9 %collective-permute-start.14 = (bf16[1024,128]{1,0:T(8,128)(2,1)S(1)}, bf16[1024,128]{1,0:T(8,128)(2,1)S(1)}, u32[]{:S(2)}, u32[]{:S(2)}) collective-permute-start(bf16[1024,128]{1,0:T(8,128)(2,1)S(1)} %get-tuple-element.65), channel_id=1, source_target_pairs={{0,2},{2,4},{4,6},{6,8},{8,10},{10,12},{12,14},{14,16},{16,18},{18... | collective-permute-start | bytes 786440 | tf_op jit(solution)/shard_map/ppermute | solution.py:488
  77.0 1.9 %collective-permute-start.16 = (bf16[1024,128]{1,0:T(8,128)(2,1)S(1)}, bf16[1024,128]{1,0:T(8,128)(2,1)S(1)}, u32[]{:S(2)}, u32[]{:S(2)}) collective-permute-start(bf16[1024,128]{1,0:T(8,128)(2,1)S(1)} %shard_map.109), channel_id=1, source_target_pairs={{0,2},{2,4},{4,6},{6,8},{8,10},{10,12},{12,14},{14,16},{16,18},{18... | collective-permute-start | bytes 786440 | tf_op jit(solution)/shard_map/ppermute | solution.py:488
  78.9 4.2 %collective-permute-done.14.refs_1_ = bf16[1024,128]{1,0:T(8,128)(2,1)S(1)} collective-permute-done((bf16[1024,128]{1,0:T(8,128)(2,1)S(1)}, bf16[1024,128]{1,0:T(8,128)(2,1)S(1)}, u32[]{:S(2)}, u32[]{:S(2)}) %collective-permute-start.14) | collective-permute-done | bytes 262176 | tf_op jit(solution)/shard_map/ppermute | solution.py:488
  83.0 0.1 shard_map.108
  83.1 4.2 %collective-permute-start.15 = (bf16[1024,128]{1,0:T(8,128)(2,1)S(1)}, bf16[1024,128]{1,0:T(8,128)(2,1)S(1)}, u32[]{:S(2)}, u32[]{:S(2)}) collective-permute-start(bf16[1024,128]{1,0:T(8,128)(2,1)S(1)} %shard_map.108), channel_id=1, source_target_pairs={{0,4},{2,6},{4,8},{6,10},{8,12},{10,14},{12,16},{14,18},{16,20},{1... | collective-permute-start | bytes 786440 | tf_op jit(solution)/shard_map/ppermute | solution.py:488
  87.4 1.0 copy-done.6
  88.3 4.7 %shard_map.111 = bf16[256,2048]{1,0:T(8,128)(2,1)} custom-call(s32[1]{0:T(128)} %bitcast.1.core_ref.half_ref, bf16[256,512]{1,0:T(8,128)(2,1)} %copy-done, bf16[4096,512]{1,0:T(8,128)(2,1)} %w_ref.5, bf16[256,2048]{1,0:T(8,128)(2,1)} %copy-done.6), custom_call_target="tpu_custom_call" | custom-call | flops 536870912 | bytes 4000000 | tf_op jit(solution)/shard_map/pallas_call | solution.py:466
  93.1 10.9 %collective-permute-start.18 = (bf16[512,128]{1,0:T(8,128)(2,1)S(1)}, bf16[512,128]{1,0:T(8,128)(2,1)S(1)}, u32[]{:S(2)}, u32[]{:S(2)}) collective-permute-start(bf16[512,128]{1,0:T(8,128)(2,1)S(1)} %slice.22), channel_id=1, source_target_pairs={{0,1},{1,0},{2,3},{3,2},{4,5},{5,4},{6,7},{7,6},{8,9},{9,8},{10,11... | collective-permute-start | bytes 393224 | tf_op jit(solution)/shard_map/ppermute | solution.py:491
  104.0 0.1 collective-permute-start.19
  104.1 0.9 collective-permute-done.18.refs_3_
  105.0 0.5 collective-permute-done.19.refs_4_
  105.5 0.7 shard_map.112
  (30 shorter events, 0.2 us)
Async XLA Ops:
  0.6 41.3 %copy-start.4 = (s32[64]{0:T(128)S(1)}, s32[64]{0:T(128)}, u32[]{:S(2)}) copy-start(s32[64]{0:T(128)} %param.11) | copy-start | bytes 772
  0.6 41.3 %copy-start.5 = (s32[64]{0:T(128)S(1)}, s32[64]{0:T(128)}, u32[]{:S(2)}) copy-start(s32[64]{0:T(128)} %param.12) | copy-start | bytes 772
  0.7 41.3 %copy-start.3 = (bf16[256,512]{1,0:T(8,128)(2,1)S(1)}, bf16[256,512]{1,0:T(8,128)(2,1)}, u32[]{:S(2)}) copy-start(bf16[256,512]{1,0:T(8,128)(2,1)} %q_ref.1) | copy-start | bytes 786436
  0.7 1.9 %collective-permute-start = (bf16[256,128]{1,0:T(8,128)(2,1)}, bf16[256,128]{1,0:T(8,128)(2,1)S(1)}, u32[]{:S(2)}, u32[]{:S(2)}) collective-permute-start(bf16[256,128]{1,0:T(8,128)(2,1)} %refs_0_.1), channel_id=1, source_target_pairs={{0,1},{1,0},{2,3},{3,2},{4,5},{5,4},{6,7},{7,6},{8,9},{9,8},{10,11... | collective-permute-start | bytes 196616 | tf_op jit(solution)/shard_map/ppermute | solution.py:491
  1.4 1.5 %collective-permute-start.1 = (bf16[256,128]{1,0:T(8,128)(2,1)}, bf16[256,128]{1,0:T(8,128)(2,1)S(1)}, u32[]{:S(2)}, u32[]{:S(2)}) collective-permute-start(bf16[256,128]{1,0:T(8,128)(2,1)} %refs_1_.1), channel_id=1, source_target_pairs={{0,1},{1,0},{2,3},{3,2},{4,5},{5,4},{6,7},{7,6},{8,9},{9,8},{10,11... | collective-permute-start | bytes 196616 | tf_op jit(solution)/shard_map/ppermute | solution.py:491
  2.5 0.6 copy-start.8
  2.9 0.6 copy-start.9
  2.9 22.8 %collective-permute-start.4 = (bf16[256,2048]{1,0:T(8,128)(2,1)}, bf16[256,2048]{1,0:T(8,128)(2,1)S(1)}, u32[]{:S(2)}, u32[]{:S(2)}) collective-permute-start(bf16[256,2048]{1,0:T(8,128)(2,1)} %own_ref.1), channel_id=1, source_target_pairs={{0,1},{1,0},{2,3},{3,2},{4,5},{5,4},{6,7},{7,6},{8,9},{9,8},{10,11... | collective-permute-start | bytes 3145736 | tf_op jit(solution)/shard_map/ppermute | solution.py:491
  12.6 29.3 %copy-start.1 = (bf16[1024,128]{1,0:T(8,128)(2,1)S(1)}, bf16[1024,128]{1,0:T(8,128)(2,1)}, u32[]{:S(2)}) copy-start(bf16[1024,128]{1,0:T(8,128)(2,1)} %shard_map.102.own_ref) | copy-start | bytes 786436
  12.6 18.9 %collective-permute-start.3 = (bf16[1024,128]{1,0:T(8,128)(2,1)}, bf16[1024,128]{1,0:T(8,128)(2,1)S(1)}, u32[]{:S(2)}, u32[]{:S(2)}) collective-permute-start(bf16[1024,128]{1,0:T(8,128)(2,1)} %shard_map.102.own_ref), channel_id=1, source_target_pairs={{0,4},{2,6},{4,8},{6,10},{8,12},{10,14},{12,16},{14,18},{16,20},{1... | collective-permute-start | bytes 786440 | tf_op jit(solution)/shard_map/ppermute | solution.py:488
  23.1 17.2 %collective-permute-start.2 = (bf16[1024,128]{1,0:T(8,128)(2,1)}, bf16[1024,128]{1,0:T(8,128)(2,1)S(1)}, u32[]{:S(2)}, u32[]{:S(2)}) collective-permute-start(bf16[1024,128]{1,0:T(8,128)(2,1)} %shard_map.102.own_ref), channel_id=1, source_target_pairs={{0,2},{2,4},{4,6},{6,8},{8,10},{10,12},{12,14},{14,16},{16,18},{18... | collective-permute-start | bytes 786440 | tf_op jit(solution)/shard_map/ppermute | solution.py:488
  25.7 1.0 copy-start.7
  31.5 20.0 %copy-start.2 = (bf16[256,512]{1,0:T(8,128)(2,1)S(1)}, bf16[256,512]{1,0:T(8,128)(2,1)}, u32[]{:S(2)}) copy-start(bf16[256,512]{1,0:T(8,128)(2,1)} %shard_map.103.do_ref) | copy-start | bytes 786436
  31.6 16.5 %collective-permute-start.7 = (bf16[1024,128]{1,0:T(8,128)(2,1)S(1)}, bf16[1024,128]{1,0:T(8,128)(2,1)S(1)}, u32[]{:S(2)}, u32[]{:S(2)}) collective-permute-start(bf16[1024,128]{1,0:T(8,128)(2,1)S(1)} %collective-permute-done.3.at2), channel_id=1, source_target_pairs={{0,2},{2,4},{4,6},{6,8},{8,10},{10,12},{12,14},{14,16},{16,18},{18... | collective-permute-start | bytes 786440 | tf_op jit(solution)/shard_map/ppermute | solution.py:488
  35.1 12.9 %collective-permute-start.8 = (bf16[1024,128]{1,0:T(8,128)(2,1)S(1)}, bf16[1024,128]{1,0:T(8,128)(2,1)S(1)}, u32[]{:S(2)}, u32[]{:S(2)}) collective-permute-start(bf16[1024,128]{1,0:T(8,128)(2,1)S(1)} %collective-permute-done.3.at2), channel_id=1, source_target_pairs={{0,4},{2,6},{4,8},{6,10},{8,12},{10,14},{12,16},{14,18},{16,20},{1... | collective-permute-start | bytes 786440 | tf_op jit(solution)/shard_map/ppermute | solution.py:488
  40.3 1.4 %collective-permute-start.5 = (bf16[512,128]{1,0:T(8,128)(2,1)S(1)}, bf16[512,128]{1,0:T(8,128)(2,1)S(1)}, u32[]{:S(2)}, u32[]{:S(2)}) collective-permute-start(bf16[512,128]{1,0:T(8,128)(2,1)S(1)} %slice.24), channel_id=1, source_target_pairs={{0,1},{1,0},{2,3},{3,2},{4,5},{5,4},{6,7},{7,6},{8,9},{9,8},{10,11... | collective-permute-start | bytes 393224 | tf_op jit(solution)/shard_map/ppermute | solution.py:491
  40.4 1.6 %collective-permute-start.6 = (bf16[512,128]{1,0:T(8,128)(2,1)S(1)}, bf16[512,128]{1,0:T(8,128)(2,1)S(1)}, u32[]{:S(2)}, u32[]{:S(2)}) collective-permute-start(bf16[512,128]{1,0:T(8,128)(2,1)S(1)} %slice.19), channel_id=1, source_target_pairs={{0,1},{1,0},{2,3},{3,2},{4,5},{5,4},{6,7},{7,6},{8,9},{9,8},{10,11... | collective-permute-start | bytes 393224 | tf_op jit(solution)/shard_map/ppermute | solution.py:491
  48.1 3.0 %collective-permute-start.10 = (bf16[512,128]{1,0:T(8,128)(2,1)S(1)}, bf16[512,128]{1,0:T(8,128)(2,1)S(1)}, u32[]{:S(2)}, u32[]{:S(2)}) collective-permute-start(bf16[512,128]{1,0:T(8,128)(2,1)S(1)} %slice.21), channel_id=1, source_target_pairs={{0,1},{1,0},{2,3},{3,2},{4,5},{5,4},{6,7},{7,6},{8,9},{9,8},{10,11... | collective-permute-start | bytes 393224 | tf_op jit(solution)/shard_map/ppermute | solution.py:491
  50.1 1.4 %collective-permute-start.9 = (bf16[512,128]{1,0:T(8,128)(2,1)S(1)}, bf16[512,128]{1,0:T(8,128)(2,1)S(1)}, u32[]{:S(2)}, u32[]{:S(2)}) collective-permute-start(bf16[512,128]{1,0:T(8,128)(2,1)S(1)} %slice.20), channel_id=1, source_target_pairs={{0,1},{1,0},{2,3},{3,2},{4,5},{5,4},{6,7},{7,6},{8,9},{9,8},{10,11... | collective-permute-start | bytes 393224 | tf_op jit(solution)/shard_map/ppermute | solution.py:491
  52.6 0.7 copy-start
  59.4 1.5 %collective-permute-start.11 = (bf16[1024,128]{1,0:T(8,128)(2,1)S(1)}, bf16[1024,128]{1,0:T(8,128)(2,1)S(1)}, u32[]{:S(2)}, u32[]{:S(2)}) collective-permute-start(bf16[1024,128]{1,0:T(8,128)(2,1)S(1)} %get-tuple-element.60), channel_id=1, source_target_pairs={{0,1},{1,0},{2,3},{3,2},{4,5},{5,4},{6,7},{7,6},{8,9},{9,8},{10,11... | collective-permute-start | bytes 786440 | tf_op jit(solution)/shard_map/ppermute | solution.py:491
  65.3 22.0 %collective-permute-start.17 = (bf16[256,2048]{1,0:T(8,128)(2,1)}, bf16[256,2048]{1,0:T(8,128)(2,1)S(1)}, u32[]{:S(2)}, u32[]{:S(2)}) collective-permute-start(bf16[256,2048]{1,0:T(8,128)(2,1)} %shard_map.110), channel_id=1, source_target_pairs={{0,1},{1,0},{2,3},{3,2},{4,5},{5,4},{6,7},{7,6},{8,9},{9,8},{10,11... | collective-permute-start | bytes 3145736 | tf_op jit(solution)/shard_map/ppermute | solution.py:491
  65.5 2.9 %collective-permute-start.12 = (bf16[1024,128]{1,0:T(8,128)(2,1)S(1)}, bf16[1024,128]{1,0:T(8,128)(2,1)S(1)}, u32[]{:S(2)}, u32[]{:S(2)}) collective-permute-start(bf16[1024,128]{1,0:T(8,128)(2,1)S(1)} %get-tuple-element.63), channel_id=1, source_target_pairs={{0,1},{1,0},{2,3},{3,2},{4,5},{5,4},{6,7},{7,6},{8,9},{9,8},{10,11... | collective-permute-start | bytes 786440 | tf_op jit(solution)/shard_map/ppermute | solution.py:491
  68.5 10.4 %collective-permute-start.13 = (bf16[1024,128]{1,0:T(8,128)(2,1)S(1)}, bf16[1024,128]{1,0:T(8,128)(2,1)S(1)}, u32[]{:S(2)}, u32[]{:S(2)}) collective-permute-start(bf16[1024,128]{1,0:T(8,128)(2,1)S(1)} %get-tuple-element.64), channel_id=1, source_target_pairs={{0,4},{2,6},{4,8},{6,10},{8,12},{10,14},{12,16},{14,18},{16,20},{1... | collective-permute-start | bytes 786440 | tf_op jit(solution)/shard_map/ppermute | solution.py:488
  72.1 11.0 %collective-permute-start.14 = (bf16[1024,128]{1,0:T(8,128)(2,1)S(1)}, bf16[1024,128]{1,0:T(8,128)(2,1)S(1)}, u32[]{:S(2)}, u32[]{:S(2)}) collective-permute-start(bf16[1024,128]{1,0:T(8,128)(2,1)S(1)} %get-tuple-element.65), channel_id=1, source_target_pairs={{0,2},{2,4},{4,6},{6,8},{8,10},{10,12},{12,14},{14,16},{16,18},{18... | collective-permute-start | bytes 786440 | tf_op jit(solution)/shard_map/ppermute | solution.py:488
  77.0 16.1 %collective-permute-start.16 = (bf16[1024,128]{1,0:T(8,128)(2,1)S(1)}, bf16[1024,128]{1,0:T(8,128)(2,1)S(1)}, u32[]{:S(2)}, u32[]{:S(2)}) collective-permute-start(bf16[1024,128]{1,0:T(8,128)(2,1)S(1)} %shard_map.109), channel_id=1, source_target_pairs={{0,2},{2,4},{4,6},{6,8},{8,10},{10,12},{12,14},{14,16},{16,18},{18... | collective-permute-start | bytes 786440 | tf_op jit(solution)/shard_map/ppermute | solution.py:488
  83.1 9.9 %collective-permute-start.15 = (bf16[1024,128]{1,0:T(8,128)(2,1)S(1)}, bf16[1024,128]{1,0:T(8,128)(2,1)S(1)}, u32[]{:S(2)}, u32[]{:S(2)}) collective-permute-start(bf16[1024,128]{1,0:T(8,128)(2,1)S(1)} %shard_map.108), channel_id=1, source_target_pairs={{0,4},{2,6},{4,8},{6,10},{8,12},{10,14},{12,16},{14,18},{16,20},{1... | collective-permute-start | bytes 786440 | tf_op jit(solution)/shard_map/ppermute | solution.py:488
  87.3 1.0 copy-start.6
  93.1 11.9 %collective-permute-start.18 = (bf16[512,128]{1,0:T(8,128)(2,1)S(1)}, bf16[512,128]{1,0:T(8,128)(2,1)S(1)}, u32[]{:S(2)}, u32[]{:S(2)}) collective-permute-start(bf16[512,128]{1,0:T(8,128)(2,1)S(1)} %slice.22), channel_id=1, source_target_pairs={{0,1},{1,0},{2,3},{3,2},{4,5},{5,4},{6,7},{7,6},{8,9},{9,8},{10,11... | collective-permute-start | bytes 393224 | tf_op jit(solution)/shard_map/ppermute | solution.py:491
  104.0 1.4 %collective-permute-start.19 = (bf16[512,128]{1,0:T(8,128)(2,1)S(1)}, bf16[512,128]{1,0:T(8,128)(2,1)S(1)}, u32[]{:S(2)}, u32[]{:S(2)}) collective-permute-start(bf16[512,128]{1,0:T(8,128)(2,1)S(1)} %slice.23), channel_id=1, source_target_pairs={{0,1},{1,0},{2,3},{3,2},{4,5},{5,4},{6,7},{7,6},{8,9},{9,8},{10,11... | collective-permute-start | bytes 393224 | tf_op jit(solution)/shard_map/ppermute | solution.py:491

commit v3 on v2

v3 whole, which is shorter than its diff:
```python
import math

import jax
import jax.numpy as jnp
from jax import lax
from jax.experimental import pallas as pl
from jax.experimental.pallas import tpu as pltpu
from jax.sharding import PartitionSpec as P

HQ = 8
HK = 2
DH = 128
SPAN = 4
ROWS = 256
GROUPS = HQ // HK
WIDE = 2 * SPAN + 1
PAIR = 2 * ROWS
REACH = 2
NEAR = 2 * REACH + 1
FAR = WIDE - NEAR
SIDE = FAR // 2
SUB = 128
SUBS = ROWS // SUB
TILE = GROUPS * SUB
CHUNK = 256
CHUNKS = TILE // CHUNK
STACK = SUBS * TILE
NEG = -1e30
BIG = 60 * 1024 * 1024
SCALE = 1.0 / math.sqrt(DH)
SCALE2 = SCALE / math.log(2.0)
VMEM = pl.BlockSpec(memory_space=pltpu.VMEM)
ANY = pl.BlockSpec(memory_space=pl.ANY)
SMALL = pltpu.CompilerParams(vmem_limit_bytes=4 * 1024 * 1024)
SMEM = pl.BlockSpec(memory_space=pltpu.SMEM)


def dot_nn(a, b):
    return lax.dot_general(a, b, (((1,), (0,)), ((), ())), preferred_element_type=jnp.float32)


def dot_nt(a, b):
    return lax.dot_general(a, b, (((1,), (1,)), ((), ())), preferred_element_type=jnp.float32)


def limits(index, lengths_row, full_row):
    n = lengths_row.shape[1]
    row = lax.broadcasted_iota(jnp.int32, (n, n), 0)
    col = lax.broadcasted_iota(jnp.int32, (n, n), 1)
    ends = jnp.sum(jnp.where(col <= row, lengths_row, 0), axis=1, keepdims=True)
    starts = jnp.sum(jnp.where(col < row, lengths_row, 0), axis=1, keepdims=True)
    full = jnp.sum(jnp.where(col == row, full_row, 0), axis=1, keepdims=True)
    pos = index * ROWS + lax.broadcasted_iota(jnp.int32, (n, ROWS), 1)
    inside = (pos >= starts) & (pos < ends)
    low = jnp.sum(jnp.where(inside, starts, 0), axis=0, keepdims=True)
    high = jnp.sum(jnp.where(inside, jnp.where(full == 1, ends, pos + 1), 0), axis=0, keepdims=True)
    return low, high


def rows_of(r):
    return pl.ds(pl.multiple_of(r * ROWS, ROWS), ROWS)


def keys_of(r):
    return pl.ds(pl.multiple_of(r * 2 * ROWS, ROWS), ROWS)


def vals_of(r):
    return pl.ds(pl.multiple_of(r * 2 * ROWS + ROWS, ROWS), ROWS)


def pair_of(r):
    return pl.ds(pl.multiple_of(r * PAIR, ROWS), PAIR)


def staged(sub, h):
    return slice(sub * TILE + h * SUB, sub * TILE + (h + 1) * SUB)


def sub_rows(sub):
    return slice(sub * SUB, (sub + 1) * SUB)


def head_cols(h):
    return slice(h * DH, (h + 1) * DH)


def chunks_of(subs):
    return range(subs[0] * CHUNKS, (subs[-1] + 1) * CHUNKS)


def chunk_cols(c):
    return slice(c * CHUNK, (c + 1) * CHUNK)


def segments_of(range_ref):
    low0, high0, low1, high1 = [range_ref[n] for n in range(4)]
    return (
        ((0,), low0, jnp.minimum(low1, high0)),
        ((0, 1), low1, high0),
        ((1,), jnp.maximum(low1, high0), high1),
    )


def every_near(range_ref, make, state):
    skip = SPAN - REACH
    for subs, lower, upper in segments_of(range_ref):
        state = lax.fori_loop(jnp.maximum(lower - skip, 0), jnp.minimum(upper - skip, NEAR), make(subs), state)
    return state


def every_far(range_ref, make, state):
    end = SPAN + REACH + 1
    for subs, lower, upper in segments_of(range_ref):
        first = jnp.where(lower < SIDE, lower, jnp.maximum(lower, end) - NEAR)
        last = jnp.where(upper > end, upper - NEAR, jnp.minimum(upper, SIDE))
        state = lax.fori_loop(first, last, make(subs), state)
    return state


def score_block(subs, at, first_key, limit_ref, win, q_st, s_ref, top):
    keys = win[keys_of(at), :]
    key_pos = first_key + lax.broadcasted_iota(jnp.int32, (ROWS, CHUNK), 0)
    valid = {
        sub: (key_pos >= limit_ref[2 * sub : 2 * sub + 1, :]) & (key_pos < limit_ref[2 * sub + 1 : 2 * sub + 2, :])
        for sub in subs
    }
    out = list(top)
    for c in chunks_of(subs):
        s = dot_nt(keys, q_st[chunk_cols(c), :]) * SCALE2
        s = jnp.where(valid[c // CHUNKS], s, NEG)
        s_ref[rows_of(at), chunk_cols(c)] = s
        out[c] = jnp.maximum(top[c], jnp.max(s, axis=0, keepdims=True))
    return tuple(out)


def weigh_block(subs, at, win, s_ref, p_ref, acc, top, total):
    vals_t = win[vals_of(at), :].T
    out = list(total)
    for c in chunks_of(subs):
        cols = chunk_cols(c)
        p = jnp.exp2(s_ref[rows_of(at), cols] - top[c])
        out[c] = total[c] + jnp.sum(p, axis=0, keepdims=True)
        p = p.astype(jnp.bfloat16)
        p_ref[rows_of(at), cols] = p
        acc[:, cols] += dot_nn(vals_t, p)
    return tuple(out)


def back_block(subs, at, win, p_ref, do_st, qs_st, dos_st, stats_ref, ds_scr, dq_acc, out_win):
    keys_t = win[keys_of(at), :].T
    vals = win[vals_of(at), :]
    for c in chunks_of(subs):
        cols = chunk_cols(c)
        dp = dot_nt(vals, do_st[cols, :])
        ds = (p_ref[rows_of(at), cols].astype(jnp.float32) * (dp - stats_ref[1:2, cols])).astype(jnp.bfloat16)
        ds_scr[:, cols] = ds
        dq_acc[:, cols] += dot_nn(keys_t, ds)
    cols = slice(subs[0] * TILE, (subs[-1] + 1) * TILE)
    out_win[keys_of(at), :] = dot_nn(ds_scr[:, cols], qs_st[cols, :]).astype(jnp.bfloat16)
    out_win[vals_of(at), :] = dot_nn(p_ref[rows_of(at), cols], dos_st[cols, :]).astype(jnp.bfloat16)


def near_scores_kernel(
    place_ref, len_ref, full_ref, q_ref, own_ref, at1_ref, at2_ref, twin1_ref, twin2_ref,
    range_ref, limit_ref, q_st, win, s_ref, top_ref,
):
    way = 1 - 2 * place_ref[1]
    base = place_ref[0] - SPAN
    low, high = limits(place_ref[0], len_ref[...], full_ref[...])
    for sub in range(SUBS):
        cut = sub_rows(sub)
        limit_ref[2 * sub : 2 * sub + 1, :] = jnp.concatenate([low[:, cut]] * (CHUNK // SUB), axis=1)
        limit_ref[2 * sub + 1 : 2 * sub + 2, :] = jnp.concatenate([high[:, cut]] * (CHUNK // SUB), axis=1)
        range_ref[2 * sub] = jnp.maximum(jnp.min(low[:, cut]) // ROWS - base, 0)
        range_ref[2 * sub + 1] = jnp.minimum((jnp.max(high[:, cut]) + ROWS - 1) // ROWS - base, WIDE)
        for h in range(GROUPS):
            q_st[staged(sub, h), :] = q_ref[cut, head_cols(h)]
    win[pair_of(REACH), :] = own_ref[0:PAIR, :]
    for k, ring, twin in ((1, at1_ref, twin1_ref), (2, at2_ref, twin2_ref)):
        win[pair_of(REACH - k * way), :] = ring[0:PAIR, :]
        win[pair_of(REACH + k * way), :] = twin[...]

    def scores(subs):
        def body(at, top):
            first_key = (base + SPAN - REACH + at) * ROWS
            return score_block(subs, at, first_key, limit_ref, win, q_st, s_ref, top)

        return body

    none = jnp.full((1, CHUNK), NEG, jnp.float32)
    top = every_near(range_ref, scores, (none,) * (SUBS * CHUNKS))
    for c in range(SUBS * CHUNKS):
        top_ref[0:1, chunk_cols(c)] = top[c]


def middle_kernel(
    place_ref, range_ref, limit_ref, q_st, near_win, near_s, top_ref, at3_ref, at4_ref, twin3_ref, twin4_ref, do_ref,
    attn_ref, do_st, qs_st, dos_st, near_p, stats_ref, dq_acc, ahead_ref, across_ref,
    win, out_win, s_scr, p_scr, ds_scr, acc,
):
    core = place_ref[1]
    base = place_ref[0] - SPAN

    def slot(n):
        return n + core * (FAR - 1 - 2 * n)

    for n, ref in enumerate((at4_ref, at3_ref, twin3_ref, twin4_ref)):
        win[pair_of(slot(n)), :] = ref[0:PAIR, :]
    for sub in range(SUBS):
        for h in range(GROUPS):
            do_st[staged(sub, h), :] = do_ref[sub_rows(sub), head_cols(h)]

    def scores(subs):
        def body(at, top):
            first_key = (base + jnp.where(at < SIDE, at, at + NEAR)) * ROWS
            return score_block(subs, at, first_key, limit_ref, win, q_st, s_scr, top)

        return body

    top = tuple(top_ref[0:1, chunk_cols(c)] for c in range(SUBS * CHUNKS))
    top = every_far(range_ref, scores, top)
    acc[...] = jnp.zeros_like(acc)

    def weigh(subs):
        return lambda at, total: weigh_block(subs, at, near_win, near_s, near_p, acc, top, total)

    def weigh_far(subs):
        return lambda at, total: weigh_block(subs, at, win, s_scr, p_scr, acc, top, total)

    total = every_near(range_ref, weigh, (jnp.zeros((1, CHUNK), jnp.float32),) * (SUBS * CHUNKS))
    total = every_far(range_ref, weigh_far, total)
    for c in range(SUBS * CHUNKS):
        stats_ref[0:1, chunk_cols(c)] = 1.0 / total[c]
    for sub in range(SUBS):
        for h in range(GROUPS):
            cols = staged(sub, h)
            inv = stats_ref[0:1, cols]
            attn_t = (acc[:, cols] * inv).astype(jnp.bfloat16).astype(jnp.float32)
            attn_ref[sub_rows(sub), head_cols(h)] = attn_t.T.astype(jnp.bfloat16)
            grad = do_st[cols, :].astype(jnp.float32)
            stats_ref[1:2, cols] = jnp.sum(attn_t * grad.T, axis=0, keepdims=True)
            inv_col = jnp.broadcast_to(inv, (DH, SUB)).T
            dos_st[cols, :] = (grad * inv_col).astype(jnp.bfloat16)
            qs_st[cols, :] = (q_st[cols, :].astype(jnp.float32) * (inv_col * SCALE)).astype(jnp.bfloat16)
    dq_acc[...] = jnp.zeros_like(dq_acc)
    out_win[...] = jnp.zeros_like(out_win)

    def back(subs):
        def body(at, carry):
            back_block(subs, at, win, p_scr, do_st, qs_st, dos_st, stats_ref, ds_scr, dq_acc, out_win)
            return carry

        return body

    every_far(range_ref, back, 0)
    for n in range(SIDE):
        ahead_ref[n * PAIR : (n + 1) * PAIR, :] = out_win[pair_of(slot(FAR - 1 - n)), :]
        across_ref[n * PAIR : (n + 1) * PAIR, :] = out_win[pair_of(slot(n)), :]


def near_back_kernel(
    place_ref, range_ref, win, p_ref, do_st, qs_st, dos_st, stats_ref, dq_far,
    dq_ref, ahead_ref, across_ref, mid_ref,
    out_win, ds_scr, dq_acc,
):
    way = 1 - 2 * place_ref[1]
    dq_acc[...] = dq_far[...]
    out_win[...] = jnp.zeros_like(out_win)

    def back(subs):
        def body(at, carry):
            back_block(subs, at, win, p_ref, do_st, qs_st, dos_st, stats_ref, ds_scr, dq_acc, out_win)
            return carry

        return body

    every_near(range_ref, back, 0)
    mid_ref[...] = out_win[pair_of(REACH), :]
    for n in range(REACH):
        k = REACH - n
        ahead_ref[n * PAIR : (n + 1) * PAIR, :] = out_win[pair_of(REACH + k * way), :]
        across_ref[n * PAIR : (n + 1) * PAIR, :] = out_win[pair_of(REACH - k * way), :]
    for sub in range(SUBS):
        for h in range(GROUPS):
            cols = staged(sub, h)
            dq = dq_acc[:, cols] * (stats_ref[0:1, cols] * SCALE)
            dq_ref[sub_rows(sub), head_cols(h)] = dq.T.astype(jnp.bfloat16)


def bf16(*shape):
    return jax.ShapeDtypeStruct(shape, jnp.bfloat16)


def f32(*shape):
    return jax.ShapeDtypeStruct(shape, jnp.float32)


def i32(*shape):
    return jax.ShapeDtypeStruct(shape, jnp.int32)


def near_scores(*args):
    return pl.pallas_call(
        near_scores_kernel,
        out_shape=(
            i32(4), i32(8, CHUNK), bf16(STACK, DH), bf16(NEAR * PAIR, DH), f32(NEAR * ROWS, STACK), f32(8, STACK),
        ),
        in_specs=[SMEM] + [VMEM] * 8,
        out_specs=(SMEM,) + (VMEM,) * 5,
        compiler_params=pltpu.CompilerParams(vmem_limit_bytes=16 * 1024 * 1024),
        cost_estimate=pl.CostEstimate(flops=10**9, bytes_accessed=6 * 10**6, transcendentals=0),
    )(*args)


def middle(*args):
    return pl.pallas_call(
        middle_kernel,
        out_shape=(
            bf16(ROWS, GROUPS * DH), bf16(STACK, DH), bf16(STACK, DH), bf16(STACK, DH), bf16(NEAR * ROWS, STACK),
            f32(8, STACK), f32(DH, STACK), bf16(SIDE * PAIR, DH), bf16(SIDE * PAIR, DH),
        ),
        in_specs=[SMEM, SMEM] + [VMEM] * 10,
        out_specs=(VMEM,) * 9,
        scratch_shapes=[
            pltpu.VMEM((FAR * PAIR, DH), jnp.bfloat16),
            pltpu.VMEM((FAR * PAIR, DH), jnp.bfloat16),
            pltpu.VMEM((FAR * ROWS, STACK), jnp.float32),
            pltpu.VMEM((FAR * ROWS, STACK), jnp.bfloat16),
            pltpu.VMEM((ROWS, STACK), jnp.bfloat16),
            pltpu.VMEM((DH, STACK), jnp.float32),
        ],
        compiler_params=pltpu.CompilerParams(vmem_limit_bytes=26 * 1024 * 1024),
        cost_estimate=pl.CostEstimate(flops=10**9, bytes_accessed=6 * 10**6, transcendentals=10**6),
    )(*args)


def near_back(*args):
    return pl.pallas_call(
        near_back_kernel,
        out_shape=(bf16(ROWS, GROUPS * DH), bf16(REACH * PAIR, DH), bf16(REACH * PAIR, DH), bf16(PAIR, DH)),
        in_specs=[SMEM, SMEM] + [VMEM] * 7,
        out_specs=(VMEM,) * 4,
        scratch_shapes=[
            pltpu.VMEM((NEAR * PAIR, DH), jnp.bfloat16),
            pltpu.VMEM((ROWS, STACK), jnp.bfloat16),
            pltpu.VMEM((DH, STACK), jnp.float32),
        ],
        compiler_params=pltpu.CompilerParams(vmem_limit_bytes=16 * 1024 * 1024),
        cost_estimate=pl.CostEstimate(flops=2 * 10**10, bytes_accessed=3 * 10**7, transcendentals=0),
    )(*args)


def small_call(body, out_rows, *args):
    shapes = [jax.ShapeDtypeStruct((rows, DH), jnp.bfloat16) for rows in out_rows]
    return pl.pallas_call(
        body,
        out_shape=shapes,
        in_specs=[VMEM] * len(args),
        out_specs=[VMEM] * len(shapes),
        compiler_params=SMALL,
        cost_estimate=pl.CostEstimate(flops=10**5, bytes_accessed=10**5, transcendentals=0),
    )(*args)


def stacked(*parts):
    def body(*refs):
        at = 0
        for ref in refs[:-1]:
            refs[-1][at : at + ref.shape[0], :] = ref[...]
            at += ref.shape[0]

    return small_call(body, [sum(part.shape[0] for part in parts)], *parts)[0]


def far_and_near(ahead, across, came):
    def body(ahead_ref, across_ref, came_ref, far_ref, near_ref):
        for n, ref in enumerate((ahead_ref, across_ref)):
            at = slice(n * PAIR, (n + 1) * PAIR)
            far_ref[at, :] = (ref[0:PAIR, :].astype(jnp.float32) + came_ref[at, :].astype(jnp.float32)).astype(jnp.bfloat16)
            near_ref[at, :] = ref[PAIR : 2 * PAIR, :]

    return small_call(body, [2 * PAIR] * 2, ahead, across, came)


def packed(*parts):
    n = len(parts)
    rows = parts[0].shape[0]

    def body(*refs):
        copies = [
            pltpu.make_async_copy(refs[k], refs[n].at[k * rows : (k + 1) * rows, :], refs[n + 1].at[k]) for k in range(n)
        ]
        for copy in copies:
            copy.start()
        for copy in copies:
            copy.wait()

    return pl.pallas_call(
        body,
        out_shape=bf16(n * rows, DH),
        in_specs=[ANY] * n,
        out_specs=VMEM,
        scratch_shapes=[pltpu.SemaphoreType.DMA((n,))],
        compiler_params=pltpu.CompilerParams(vmem_limit_bytes=BIG),
        cost_estimate=pl.CostEstimate(flops=0, bytes_accessed=10**6, transcendentals=0),
    )(*parts)


def both_heads(ahead, across):
    def body(ahead_ref, across_ref, *out_refs):
        for n, out_ref in enumerate(out_refs):
            out_ref[0:PAIR, :] = ahead_ref[n * PAIR : (n + 1) * PAIR, :]
            out_ref[PAIR : 2 * PAIR, :] = across_ref[n * PAIR : (n + 1) * PAIR, :]

    return small_call(body, [2 * PAIR] * 2, ahead, across)


def summed(*parts):
    def body(*refs):
        total = refs[0][...].astype(jnp.float32)
        for ref in refs[1:-1]:
            total += ref[...].astype(jnp.float32)
        refs[-1][...] = total.astype(jnp.bfloat16)

    return small_call(body, [parts[0].shape[0]], *parts)[0]


def last_sum(*parts):
    def body(*refs):
        for at, out_ref in ((0, refs[-2]), (ROWS, refs[-1])):
            total = refs[0][at : at + ROWS, :].astype(jnp.float32)
            for ref in refs[1:-2]:
                total += ref[at : at + ROWS, :].astype(jnp.float32)
            out_ref[...] = total.astype(jnp.bfloat16)

    return small_call(body, [ROWS, ROWS], *parts)


def half_of(core, size):
    return pl.ds(pl.multiple_of(core * size, size), size)


def project_back(core, own, other, w):
    rows, depth = own.shape
    cols = w.shape[1]

    def body(core_ref, own_ref, other_ref, w_ref, out_ref):
        core = core_ref[0]
        part = dot_nn(own_ref[...], w_ref[half_of(core, depth), :])
        out_ref[...] = (part + dot_nn(other_ref[...], w_ref[half_of(1 - core, depth), :])).astype(jnp.bfloat16)

    return pl.pallas_call(
        body,
        out_shape=bf16(rows, cols),
        in_specs=[SMEM, VMEM, VMEM, VMEM],
        out_specs=VMEM,
        compiler_params=pltpu.CompilerParams(vmem_limit_bytes=12 * 1024 * 1024),
        cost_estimate=pl.CostEstimate(flops=4 * rows * depth * cols, bytes_accessed=6 * 10**6, transcendentals=0),
    )(core, own, other, w)


def project(half, attn, w, other=None):
    rows, depth = attn.shape
    cols = w.shape[0] // 2
    more = () if other is None else (other,)

    def body(half_ref, a_ref, w_ref, *refs):
        out = dot_nt(a_ref[...], w_ref[half_of(half_ref[0], cols), :])
        if more:
            out += refs[0][...].astype(jnp.float32)
        refs[-1][...] = out.astype(jnp.bfloat16)

    return pl.pallas_call(
        body,
        out_shape=bf16(rows, cols),
        in_specs=[SMEM, VMEM, VMEM] + [VMEM] * len(more),
        out_specs=VMEM,
        compiler_params=pltpu.CompilerParams(vmem_limit_bytes=12 * 1024 * 1024),
        cost_estimate=pl.CostEstimate(flops=2 * rows * depth * cols, bytes_accessed=4 * 10**6, transcendentals=0),
    )(half, attn, w, *more)


def on_device(queries, keys, values, out_weight, doc_lengths, doc_full, out_grad):
    devices = lax.axis_size("cp")
    index = lax.axis_index("cp").astype(jnp.int32)
    core = lax.axis_index("hd").astype(jnp.int32)
    place = jnp.stack([index, core])
    core = core.reshape(1)

    def step(block, far):
        ways = [(2 * i, 2 * (i + far)) for i in range(devices - far)]
        ways += [(2 * (i + far) + 1, 2 * i + 1) for i in range(devices - far)]
        return lax.ppermute(block, ("cp", "hd"), ways)

    def twin(block):
        return lax.ppermute(block, "hd", [(0, 1), (1, 0)])

    own = packed(keys, values)
    other_keys, other_values, late_grad, own = lax.optimization_barrier((twin(keys), twin(values), out_grad, own))
    block = stacked(own, other_keys, other_values)
    other_grad = twin(late_grad)
    at2 = step(block, 2)
    at1 = step(block, 1)
    attn_grad = project_back(core, out_grad, other_grad, out_weight)
    at2, attn_grad = lax.optimization_barrier((at2, attn_grad))
    at4 = step(at2, 2)
    at3 = step(at2, 1)
    ranges, limit, q_st, win, s, top = near_scores(
        place, doc_lengths.reshape(1, -1), doc_full.reshape(1, -1), queries,
        own, at1, at2, twin(at1[PAIR:]), twin(at2[PAIR:]),
    )
    at4, top = lax.optimization_barrier((at4, top))
    at3, twin4 = lax.optimization_barrier((at3, twin(at4[PAIR:])))
    attn, do_st, qs_st, dos_st, p, stats, dq_far, ahead, across = middle(
        place, ranges, limit, q_st, win, s, top, at3, at4, twin(at3[PAIR:]), twin4, attn_grad
    )
    away = project(1 - core, attn, out_weight)
    across, away = lax.optimization_barrier((twin(across), away))
    out4, out3 = both_heads(ahead, across)
    out4, out3, stats = lax.optimization_barrier((out4, out3, stats))
    in4 = step(out4, 2)
    in3 = step(out3, 1)
    query_grad, ahead, across, mid = near_back(place, ranges, win, p, do_st, qs_st, dos_st, stats, dq_far)
    came = summed(in4, in3)
    came, across = lax.optimization_barrier((came, twin(across)))
    far_out, near_out = far_and_near(ahead, across, came)
    far_out, away = lax.optimization_barrier((far_out, away))
    far = step(far_out, 2)
    near = step(near_out, 1)
    layer_out = project(core, attn, out_weight, twin(away))
    near, layer_out = lax.optimization_barrier((near, layer_out))
    far, near_twin = lax.optimization_barrier((far, twin(near[PAIR:])))
    key_grad, value_grad = last_sum(mid, near, far, near_twin, twin(far[PAIR:]))
    return (layer_out, query_grad, key_grad, value_grad)


def solution(mesh):
    placed = (P("cp", "hd"), P("cp", "hd"), P("cp", "hd"), P(None, "hd"), P(), P(), P("cp", "hd"))
    return jax.shard_map(
        on_device,
        mesh=mesh,
        in_specs=placed,
        out_specs=(P("cp", "hd"), P("cp", "hd"), P("cp", "hd"), P("cp", "hd")),
        check_vma=False,
    )
```

time: 108 us -> 87.4 us (0.81)
  the two profiles are of different devices: /device:TPU:25 before, /device:TPU:49 now
where the time goes in v3:
time: 87.4 us; the launch traced here: 86.4 us
  starting transfers between devices  53.9 us (62%)
  Pallas kernels  17.4 us (20%)
  waiting for transfers between devices  9.67 us (11%)
  local copies, waits for them, and re-layouts  4.39 us (5%)
  between operations  0.93 us (1%)
    ppermute x8, starting transfers between devices, step(): return lax.ppermute(block, ('cp', 'hd'), ways)  43 us
    ppermute x12, starting transfers between devices, twin(): return lax.ppermute(block, 'hd', [(0, 1), (1, 0)])  10.9 us
    ppermute x8, waiting for transfers between devices, step(): return lax.ppermute(block, ('cp', 'hd'), ways)  6.27 us
    pallas_call x1, Pallas kernels, near_back(): pl.pallas_call(near_back_kernel, out_shape=(bf16(ROWS, GROUPS * DH), bf16...  4.47 us
    pallas_call x1, Pallas kernels, middle(): pl.pallas_call(middle_kernel, out_shape=(bf16(ROWS, GROUPS * DH), bf16(ST...  4.46 us
    unnamed x16, local copies, waits for them, and re-layouts  4.33 us
    ppermute x12, waiting for transfers between devices, twin(): return lax.ppermute(block, 'hd', [(0, 1), (1, 0)])  3.4 us
    pallas_call x2, Pallas kernels, project(): pl.pallas_call(body, out_shape=bf16(rows, cols), in_specs=[SMEM, VMEM, VM...  2.49 us
  transfers between devices with their start and end apart: 20, of which 6 were waited for; matrix products, arithmetic and copies ran while one was open for 0% of the time, Pallas kernels for 14%

profile of v3, /device:TPU:49, one launch (start us, length us, event | category | flops | bytes accessed | tf_op | source)
XLA Modules:
  0.0 86.4 jit_solution(3577306226116190289)
XLA Ops:
  0.6 0.8 collective-permute-start
  1.4 0.1 collective-permute-start.1
  1.5 1.5 %shard_map.102.refs_0_.own_ref = bf16[512,128]{1,0:T(8,128)(2,1)} custom-call(bf16[256,128]{1,0:T(8,128)(2,1)} %refs_0_.1, bf16[256,128]{1,0:T(8,128)(2,1)} %refs_1_.1), custom_call_target="tpu_custom_call" | custom-call | bytes 1000000 | tf_op jit(solution)/shard_map/pallas_call | solution.py:399
  3.1 0.0 collective-permute-done.refs_1_
  3.1 0.0 collective-permute-done.1.refs_2_
  3.1 0.5 collective-permute-start.4
  3.6 0.9 %copy-done.3 = bf16[512,128]{1,0:T(8,128)(2,1)S(1)} copy-done((bf16[512,128]{1,0:T(8,128)(2,1)S(1)}, bf16[512,128]{1,0:T(8,128)(2,1)}, u32[]{:S(2)}) %copy-start.3) | copy-done | bytes 131096
  4.5 9.2 %collective-permute-start.3 = (bf16[1024,128]{1,0:T(8,128)(2,1)S(1)}, bf16[1024,128]{1,0:T(8,128)(2,1)S(1)}, u32[]{:S(2)}, u32[]{:S(2)}) collective-permute-start(bf16[1024,128]{1,0:T(8,128)(2,1)S(1)} %shard_map.103), channel_id=1, source_target_pairs={{0,4},{2,6},{4,8},{6,10},{8,12},{10,14},{12,16},{14,18},{16,20},{1... | collective-permute-start | bytes 786440 | tf_op jit(solution)/shard_map/ppermute | solution.py:494
  13.8 2.6 %collective-permute-start.2 = (bf16[1024,128]{1,0:T(8,128)(2,1)S(1)}, bf16[1024,128]{1,0:T(8,128)(2,1)S(1)}, u32[]{:S(2)}, u32[]{:S(2)}) collective-permute-start(bf16[1024,128]{1,0:T(8,128)(2,1)S(1)} %shard_map.103), channel_id=1, source_target_pairs={{0,2},{2,4},{4,6},{6,8},{8,10},{10,12},{12,14},{14,16},{16,18},{18... | collective-permute-start | bytes 786440 | tf_op jit(solution)/shard_map/ppermute | solution.py:494
  16.4 0.0 collective-permute-done.4.other_ref
  16.4 0.0 copy-start
  16.4 2.2 %copy-done = bf16[4096,512]{1,0:T(8,128)(2,1)S(1)} copy-done((bf16[4096,512]{1,0:T(8,128)(2,1)S(1)}, bf16[4096,512]{1,0:T(8,128)(2,1)}, u32[]{:S(2)}) %copy-start) | copy-done | bytes 4194328
  18.6 1.2 %copy-done.2 = bf16[256,2048]{1,0:T(8,128)(2,1)S(1)} copy-done((bf16[256,2048]{1,0:T(8,128)(2,1)S(1)}, bf16[256,2048]{1,0:T(8,128)(2,1)}, u32[]{:S(2)}) %copy-start.2) | copy-done | bytes 1048600
  19.8 1.3 %shard_map.104.do_ref = bf16[256,512]{1,0:T(8,128)(2,1)S(1)} custom-call(s32[1]{0:T(128)} %bitcast.1.core_ref.half_ref, bf16[256,2048]{1,0:T(8,128)(2,1)S(1)} %copy-done.2, bf16[256,2048]{1,0:T(8,128)(2,1)S(1)} %collective-permute-done.4.other_ref, bf16[4096,512]{1,0:T(8,128)(2,1)S(1)} %copy-done), custom_call_target="tpu_custom_call" | custom-call | flops 1073741824 | bytes 6000000 | tf_op jit(solution)/shard_map/pallas_call | solution.py:453
  21.1 5.0 %collective-permute-start.7 = (bf16[1024,128]{1,0:T(8,128)(2,1)S(1)}, bf16[1024,128]{1,0:T(8,128)(2,1)S(1)}, u32[]{:S(2)}, u32[]{:S(2)}) collective-permute-start(bf16[1024,128]{1,0:T(8,128)(2,1)S(1)} %collective-permute-done.3.at2_ref), channel_id=1, source_target_pairs={{0,4},{2,6},{4,8},{6,10},{8,12},{10,14},{12,16},{14,18},{16,20},{1... | collective-permute-start | bytes 786440 | tf_op jit(solution)/shard_map/ppermute | solution.py:494
  26.1 0.1 collective-permute-start.5
  26.2 0.6 collective-permute-start.6
  26.8 5.3 %collective-permute-start.8 = (bf16[1024,128]{1,0:T(8,128)(2,1)S(1)}, bf16[1024,128]{1,0:T(8,128)(2,1)S(1)}, u32[]{:S(2)}, u32[]{:S(2)}) collective-permute-start(bf16[1024,128]{1,0:T(8,128)(2,1)S(1)} %collective-permute-done.3.at2_ref), channel_id=1, source_target_pairs={{0,2},{2,4},{4,6},{6,8},{8,10},{10,12},{12,14},{14,16},{16,18},{18... | collective-permute-start | bytes 786440 | tf_op jit(solution)/shard_map/ppermute | solution.py:494
  32.1 0.1 pad_add_fusion.place_ref
  32.2 0.0 collective-permute-done.6.twin2_ref
  32.3 2.3 %shard_map.105 = (s32[4]{0:T(128)S(1)}, s32[8,256]{1,0:T(8,128)S(1)}, bf16[1024,128]{1,0:T(8,128)(2,1)S(1)}, bf16[2560,128]{1,0:T(8,128)(2,1)S(1)}, f32[1280,1024]{1,0:T(8,128)S(1)}, /*index=5*/f32[8,1024]{1,0:T(8,128)S(1)}) custom-call(s32[2]{0:T(128)S(1)} %pad_add_fusion.place_ref, s32[1,64]{1,0:T(1,128)S(1)} %bitcast.4, s32[1,64]{1,0:T(1,128)S(1)} %bitcast.5, ...), custom_call_target="tpu_custom_call" | custom-call | flops 1000000000 | bytes 6000000 | tf_op jit(solution)/shard_map/pallas_call | solution.py:304
  34.6 0.0 copy-start.1
  34.6 0.0 collective-permute-done.7.at4_ref
  34.6 2.1 %collective-permute-start.9 = (bf16[512,128]{1,0:T(8,128)(2,1)S(1)}, bf16[512,128]{1,0:T(8,128)(2,1)S(1)}, u32[]{:S(2)}, u32[]{:S(2)}) collective-permute-start(bf16[512,128]{1,0:T(8,128)(2,1)S(1)} %slice.20), channel_id=1, source_target_pairs={{0,1},{1,0},{2,3},{3,2},{4,5},{5,4},{6,7},{7,6},{8,9},{9,8},{10,11... | collective-permute-start | bytes 393224 | tf_op jit(solution)/shard_map/ppermute | solution.py:497
  36.8 1.0 %collective-permute-done.9.twin4_ref = bf16[512,128]{1,0:T(8,128)(2,1)S(1)} collective-permute-done((bf16[512,128]{1,0:T(8,128)(2,1)S(1)}, bf16[512,128]{1,0:T(8,128)(2,1)S(1)}, u32[]{:S(2)}, u32[]{:S(2)}) %collective-permute-start.9) | collective-permute-done | bytes 131104 | tf_op jit(solution)/shard_map/ppermute | solution.py:497
  37.8 0.4 collective-permute-start.10
  38.2 1.0 %collective-permute-done.10.twin3_ref = bf16[512,128]{1,0:T(8,128)(2,1)S(1)} collective-permute-done((bf16[512,128]{1,0:T(8,128)(2,1)S(1)}, bf16[512,128]{1,0:T(8,128)(2,1)S(1)}, u32[]{:S(2)}, u32[]{:S(2)}) %collective-permute-start.10) | collective-permute-done | bytes 131104 | tf_op jit(solution)/shard_map/ppermute | solution.py:497
  39.2 4.5 %shard_map.106 = (bf16[256,512]{1,0:T(8,128)(2,1)S(1)}, bf16[1024,128]{1,0:T(8,128)(2,1)S(1)}, bf16[1024,128]{1,0:T(8,128)(2,1)S(1)}, bf16[1024,128]{1,0:T(8,128...) custom-call(s32[2]{0:T(128)S(1)} %pad_add_fusion.place_ref, ...), custom_call_target="tpu_custom_call" | custom-call | flops 1000000000 | bytes 6000000 | tf_op jit(solution)/shard_map/pallas_call | solution.py:317
  43.7 0.4 collective-permute-start.11
  44.1 0.7 shard_map.107
  44.9 0.4 collective-permute-done.11.across_ref
  45.3 5.9 %collective-permute-start.12 = (bf16[1024,128]{1,0:T(8,128)(2,1)S(1)}, bf16[1024,128]{1,0:T(8,128)(2,1)S(1)}, u32[]{:S(2)}, u32[]{:S(2)}) collective-permute-start(bf16[1024,128]{1,0:T(8,128)(2,1)S(1)} %get-tuple-element.82), channel_id=1, source_target_pairs={{0,4},{2,6},{4,8},{6,10},{8,12},{10,14},{12,16},{14,18},{16,20},{1... | collective-permute-start | bytes 786440 | tf_op jit(solution)/shard_map/ppermute | solution.py:494
  51.2 3.3 %collective-permute-start.13 = (bf16[1024,128]{1,0:T(8,128)(2,1)S(1)}, bf16[1024,128]{1,0:T(8,128)(2,1)S(1)}, u32[]{:S(2)}, u32[]{:S(2)}) collective-permute-start(bf16[1024,128]{1,0:T(8,128)(2,1)S(1)} %get-tuple-element.83), channel_id=1, source_target_pairs={{0,2},{2,4},{4,6},{6,8},{8,10},{10,12},{12,14},{14,16},{16,18},{18... | collective-permute-start | bytes 786440 | tf_op jit(solution)/shard_map/ppermute | solution.py:494
  54.6 4.5 %shard_map.109 = (bf16[256,512]{1,0:T(8,128)(2,1)}, bf16[1024,128]{1,0:T(8,128)(2,1)S(1)}, bf16[1024,128]{1,0:T(8,128)(2,1)S(1)}, bf16[512,128]{1,0:T(8,128)(2,1)S(1)}) custom-call(s32[2]{0:T(128)S(1)} %pad_add_fusion.place_ref, s32[4]{0:T(128)S(1)} %get-tuple-element.57.range_ref, bf16[2560,128]{1,0:T(8,128)(2,1)S(1)} %get-tuple-element.58.near_win.win, ...), custom_call_target="tpu_custom_call" | custom-call | flops 20000000000 | bytes 30000000 | tf_op jit(solution)/shard_map/pallas_call | solution.py:339
  59.1 0.0 collective-permute-start.14
  59.1 2.7 %collective-permute-done.13.refs_1_ = bf16[1024,128]{1,0:T(8,128)(2,1)S(1)} collective-permute-done((bf16[1024,128]{1,0:T(8,128)(2,1)S(1)}, bf16[1024,128]{1,0:T(8,128)(2,1)S(1)}, u32[]{:S(2)}, u32[]{:S(2)}) %collective-permute-start.13) | collective-permute-done | bytes 262176 | tf_op jit(solution)/shard_map/ppermute | solution.py:494
  61.8 0.1 shard_map.110.came_ref
  61.8 0.1 shard_map.111
  61.9 0.1 collective-permute-start.16
  62.0 6.7 %collective-permute-start.15 = (bf16[1024,128]{1,0:T(8,128)(2,1)S(1)}, bf16[1024,128]{1,0:T(8,128)(2,1)S(1)}, u32[]{:S(2)}, u32[]{:S(2)}) collective-permute-start(bf16[1024,128]{1,0:T(8,128)(2,1)S(1)} %get-tuple-element.87), channel_id=1, source_target_pairs={{0,2},{2,4},{4,6},{6,8},{8,10},{10,12},{12,14},{14,16},{16,18},{18... | collective-permute-start | bytes 786440 | tf_op jit(solution)/shard_map/ppermute | solution.py:494
  68.7 5.0 %collective-permute-start.17 = (bf16[1024,128]{1,0:T(8,128)(2,1)S(1)}, bf16[1024,128]{1,0:T(8,128)(2,1)S(1)}, u32[]{:S(2)}, u32[]{:S(2)}) collective-permute-start(bf16[1024,128]{1,0:T(8,128)(2,1)S(1)} %get-tuple-element.95), channel_id=1, source_target_pairs={{0,4},{2,6},{4,8},{6,10},{8,12},{10,14},{12,16},{14,18},{16,20},{1... | collective-permute-start | bytes 786440 | tf_op jit(solution)/shard_map/ppermute | solution.py:494
  73.7 0.0 collective-permute-done.16.refs_0_
  73.7 1.8 %shard_map.112 = bf16[256,2048]{1,0:T(8,128)(2,1)} custom-call(s32[1]{0:T(128)} %bitcast.1.core_ref.half_ref, bf16[256,512]{1,0:T(8,128)(2,1)S(1)} %get-tuple-element.74.a_ref, bf16[4096,512]{1,0:T(8,128)(2,1)S(1)} %copy-done.1, bf16[256,2048]{1,0:T(8,128)(2,1)S(1)} %collective-permute-done.16.refs_0_), custom_call_target="tpu_custom_call" | custom-call | flops 536870912 | bytes 4000000 | tf_op jit(solution)/shard_map/pallas_call | solution.py:474
  75.5 0.7 collective-permute-start.18
  76.1 3.5 %collective-permute-done.17.refs_2_ = bf16[1024,128]{1,0:T(8,128)(2,1)S(1)} collective-permute-done((bf16[1024,128]{1,0:T(8,128)(2,1)S(1)}, bf16[1024,128]{1,0:T(8,128)(2,1)S(1)}, u32[]{:S(2)}, u32[]{:S(2)}) %collective-permute-start.17) | collective-permute-done | bytes 262176 | tf_op jit(solution)/shard_map/ppermute | solution.py:494
  79.7 5.0 %collective-permute-start.19 = (bf16[512,128]{1,0:T(8,128)(2,1)S(1)}, bf16[512,128]{1,0:T(8,128)(2,1)S(1)}, u32[]{:S(2)}, u32[]{:S(2)}) collective-permute-start(bf16[512,128]{1,0:T(8,128)(2,1)S(1)} %slice.23), channel_id=1, source_target_pairs={{0,1},{1,0},{2,3},{3,2},{4,5},{5,4},{6,7},{7,6},{8,9},{9,8},{10,11... | collective-permute-start | bytes 393224 | tf_op jit(solution)/shard_map/ppermute | solution.py:497
  84.7 1.0 %collective-permute-done.19.refs_4_ = bf16[512,128]{1,0:T(8,128)(2,1)S(1)} collective-permute-done((bf16[512,128]{1,0:T(8,128)(2,1)S(1)}, bf16[512,128]{1,0:T(8,128)(2,1)S(1)}, u32[]{:S(2)}, u32[]{:S(2)}) %collective-permute-start.19) | collective-permute-done | bytes 131104 | tf_op jit(solution)/shard_map/ppermute | solution.py:497
  85.7 0.7 shard_map.113
  (27 shorter events, 0.2 us)
Async XLA Ops:
  0.6 31.6 %copy-start.5 = (bf16[256,512]{1,0:T(8,128)(2,1)S(1)}, bf16[256,512]{1,0:T(8,128)(2,1)}, u32[]{:S(2)}) copy-start(bf16[256,512]{1,0:T(8,128)(2,1)} %q_ref.1) | copy-start | bytes 786436
  0.6 2.4 %collective-permute-start = (bf16[256,128]{1,0:T(8,128)(2,1)}, bf16[256,128]{1,0:T(8,128)(2,1)S(1)}, u32[]{:S(2)}, u32[]{:S(2)}) collective-permute-start(bf16[256,128]{1,0:T(8,128)(2,1)} %refs_0_.1), channel_id=1, source_target_pairs={{0,1},{1,0},{2,3},{3,2},{4,5},{5,4},{6,7},{7,6},{8,9},{9,8},{10,11... | collective-permute-start | bytes 196616 | tf_op jit(solution)/shard_map/ppermute | solution.py:497
  1.4 1.7 %collective-permute-start.1 = (bf16[256,128]{1,0:T(8,128)(2,1)}, bf16[256,128]{1,0:T(8,128)(2,1)S(1)}, u32[]{:S(2)}, u32[]{:S(2)}) collective-permute-start(bf16[256,128]{1,0:T(8,128)(2,1)} %refs_1_.1), channel_id=1, source_target_pairs={{0,1},{1,0},{2,3},{3,2},{4,5},{5,4},{6,7},{7,6},{8,9},{9,8},{10,11... | collective-permute-start | bytes 196616 | tf_op jit(solution)/shard_map/ppermute | solution.py:497
  3.1 13.3 %collective-permute-start.4 = (bf16[256,2048]{1,0:T(8,128)(2,1)}, bf16[256,2048]{1,0:T(8,128)(2,1)S(1)}, u32[]{:S(2)}, u32[]{:S(2)}) collective-permute-start(bf16[256,2048]{1,0:T(8,128)(2,1)} %own_ref.1), channel_id=1, source_target_pairs={{0,1},{1,0},{2,3},{3,2},{4,5},{5,4},{6,7},{7,6},{8,9},{9,8},{10,11... | collective-permute-start | bytes 3145736 | tf_op jit(solution)/shard_map/ppermute | solution.py:497
  3.6 0.9 %copy-start.3 = (bf16[512,128]{1,0:T(8,128)(2,1)S(1)}, bf16[512,128]{1,0:T(8,128)(2,1)}, u32[]{:S(2)}) copy-start(bf16[512,128]{1,0:T(8,128)(2,1)} %shard_map.102.refs_0_.own_ref) | copy-start | bytes 393220
  4.5 27.8 %copy-start.4 = (bf16[512,128]{1,0:T(8,128)(2,1)S(1)}, bf16[512,128]{1,0:T(8,128)(2,1)}, u32[]{:S(2)}) copy-start(bf16[512,128]{1,0:T(8,128)(2,1)} %shard_map.102.refs_0_.own_ref) | copy-start | bytes 393220
  4.5 27.8 %copy-start.6 = (s32[64]{0:T(128)S(1)}, s32[64]{0:T(128)}, u32[]{:S(2)}) copy-start(s32[64]{0:T(128)} %param.11) | copy-start | bytes 772
  4.5 27.8 %copy-start.7 = (s32[64]{0:T(128)S(1)}, s32[64]{0:T(128)}, u32[]{:S(2)}) copy-start(s32[64]{0:T(128)} %param.12) | copy-start | bytes 772
  4.5 16.6 %collective-permute-start.3 = (bf16[1024,128]{1,0:T(8,128)(2,1)S(1)}, bf16[1024,128]{1,0:T(8,128)(2,1)S(1)}, u32[]{:S(2)}, u32[]{:S(2)}) collective-permute-start(bf16[1024,128]{1,0:T(8,128)(2,1)S(1)} %shard_map.103), channel_id=1, source_target_pairs={{0,4},{2,6},{4,8},{6,10},{8,12},{10,14},{12,16},{14,18},{16,20},{1... | collective-permute-start | bytes 786440 | tf_op jit(solution)/shard_map/ppermute | solution.py:494
  13.8 12.3 %collective-permute-start.2 = (bf16[1024,128]{1,0:T(8,128)(2,1)S(1)}, bf16[1024,128]{1,0:T(8,128)(2,1)S(1)}, u32[]{:S(2)}, u32[]{:S(2)}) collective-permute-start(bf16[1024,128]{1,0:T(8,128)(2,1)S(1)} %shard_map.103), channel_id=1, source_target_pairs={{0,2},{2,4},{4,6},{6,8},{8,10},{10,12},{12,14},{14,16},{16,18},{18... | collective-permute-start | bytes 786440 | tf_op jit(solution)/shard_map/ppermute | solution.py:494
  16.4 2.2 %copy-start = (bf16[4096,512]{1,0:T(8,128)(2,1)S(1)}, bf16[4096,512]{1,0:T(8,128)(2,1)}, u32[]{:S(2)}) copy-start(bf16[4096,512]{1,0:T(8,128)(2,1)} %w_ref.5) | copy-start | bytes 12582916
  18.6 1.2 %copy-start.2 = (bf16[256,2048]{1,0:T(8,128)(2,1)S(1)}, bf16[256,2048]{1,0:T(8,128)(2,1)}, u32[]{:S(2)}) copy-start(bf16[256,2048]{1,0:T(8,128)(2,1)} %own_ref.1) | copy-start | bytes 3145732
  21.1 13.5 %collective-permute-start.7 = (bf16[1024,128]{1,0:T(8,128)(2,1)S(1)}, bf16[1024,128]{1,0:T(8,128)(2,1)S(1)}, u32[]{:S(2)}, u32[]{:S(2)}) collective-permute-start(bf16[1024,128]{1,0:T(8,128)(2,1)S(1)} %collective-permute-done.3.at2_ref), channel_id=1, source_target_pairs={{0,4},{2,6},{4,8},{6,10},{8,12},{10,14},{12,16},{14,18},{16,20},{1... | collective-permute-start | bytes 786440 | tf_op jit(solution)/shard_map/ppermute | solution.py:494
  26.1 6.1 %collective-permute-start.5 = (bf16[512,128]{1,0:T(8,128)(2,1)S(1)}, bf16[512,128]{1,0:T(8,128)(2,1)S(1)}, u32[]{:S(2)}, u32[]{:S(2)}) collective-permute-start(bf16[512,128]{1,0:T(8,128)(2,1)S(1)} %slice.24), channel_id=1, source_target_pairs={{0,1},{1,0},{2,3},{3,2},{4,5},{5,4},{6,7},{7,6},{8,9},{9,8},{10,11... | collective-permute-start | bytes 393224 | tf_op jit(solution)/shard_map/ppermute | solution.py:497
  26.2 6.0 %collective-permute-start.6 = (bf16[512,128]{1,0:T(8,128)(2,1)S(1)}, bf16[512,128]{1,0:T(8,128)(2,1)S(1)}, u32[]{:S(2)}, u32[]{:S(2)}) collective-permute-start(bf16[512,128]{1,0:T(8,128)(2,1)S(1)} %slice.19), channel_id=1, source_target_pairs={{0,1},{1,0},{2,3},{3,2},{4,5},{5,4},{6,7},{7,6},{8,9},{9,8},{10,11... | collective-permute-start | bytes 393224 | tf_op jit(solution)/shard_map/ppermute | solution.py:497
  26.8 10.0 %collective-permute-start.8 = (bf16[1024,128]{1,0:T(8,128)(2,1)S(1)}, bf16[1024,128]{1,0:T(8,128)(2,1)S(1)}, u32[]{:S(2)}, u32[]{:S(2)}) collective-permute-start(bf16[1024,128]{1,0:T(8,128)(2,1)S(1)} %collective-permute-done.3.at2_ref), channel_id=1, source_target_pairs={{0,2},{2,4},{4,6},{6,8},{8,10},{10,12},{12,14},{14,16},{16,18},{18... | collective-permute-start | bytes 786440 | tf_op jit(solution)/shard_map/ppermute | solution.py:494
  34.6 9.5 %copy-start.1 = (bf16[4096,512]{1,0:T(8,128)(2,1)S(1)}, bf16[4096,512]{1,0:T(8,128)(2,1)}, u32[]{:S(2)}) copy-start(bf16[4096,512]{1,0:T(8,128)(2,1)} %w_ref.5) | copy-start | bytes 12582916
  34.6 3.1 %collective-permute-start.9 = (bf16[512,128]{1,0:T(8,128)(2,1)S(1)}, bf16[512,128]{1,0:T(8,128)(2,1)S(1)}, u32[]{:S(2)}, u32[]{:S(2)}) collective-permute-start(bf16[512,128]{1,0:T(8,128)(2,1)S(1)} %slice.20), channel_id=1, source_target_pairs={{0,1},{1,0},{2,3},{3,2},{4,5},{5,4},{6,7},{7,6},{8,9},{9,8},{10,11... | collective-permute-start | bytes 393224 | tf_op jit(solution)/shard_map/ppermute | solution.py:497
  37.8 1.4 %collective-permute-start.10 = (bf16[512,128]{1,0:T(8,128)(2,1)S(1)}, bf16[512,128]{1,0:T(8,128)(2,1)S(1)}, u32[]{:S(2)}, u32[]{:S(2)}) collective-permute-start(bf16[512,128]{1,0:T(8,128)(2,1)S(1)} %slice.21), channel_id=1, source_target_pairs={{0,1},{1,0},{2,3},{3,2},{4,5},{5,4},{6,7},{7,6},{8,9},{9,8},{10,11... | collective-permute-start | bytes 393224 | tf_op jit(solution)/shard_map/ppermute | solution.py:497
  43.7 1.6 %collective-permute-start.11 = (bf16[1024,128]{1,0:T(8,128)(2,1)S(1)}, bf16[1024,128]{1,0:T(8,128)(2,1)S(1)}, u32[]{:S(2)}, u32[]{:S(2)}) collective-permute-start(bf16[1024,128]{1,0:T(8,128)(2,1)S(1)} %get-tuple-element.73), channel_id=1, source_target_pairs={{0,1},{1,0},{2,3},{3,2},{4,5},{5,4},{6,7},{7,6},{8,9},{9,8},{10,11... | collective-permute-start | bytes 786440 | tf_op jit(solution)/shard_map/ppermute | solution.py:497
  45.3 13.7 %collective-permute-start.12 = (bf16[1024,128]{1,0:T(8,128)(2,1)S(1)}, bf16[1024,128]{1,0:T(8,128)(2,1)S(1)}, u32[]{:S(2)}, u32[]{:S(2)}) collective-permute-start(bf16[1024,128]{1,0:T(8,128)(2,1)S(1)} %get-tuple-element.82), channel_id=1, source_target_pairs={{0,4},{2,6},{4,8},{6,10},{8,12},{10,14},{12,16},{14,18},{16,20},{1... | collective-permute-start | bytes 786440 | tf_op jit(solution)/shard_map/ppermute | solution.py:494
  51.2 10.5 %collective-permute-start.13 = (bf16[1024,128]{1,0:T(8,128)(2,1)S(1)}, bf16[1024,128]{1,0:T(8,128)(2,1)S(1)}, u32[]{:S(2)}, u32[]{:S(2)}) collective-permute-start(bf16[1024,128]{1,0:T(8,128)(2,1)S(1)} %get-tuple-element.83), channel_id=1, source_target_pairs={{0,2},{2,4},{4,6},{6,8},{8,10},{10,12},{12,14},{14,16},{16,18},{18... | collective-permute-start | bytes 786440 | tf_op jit(solution)/shard_map/ppermute | solution.py:494
  59.1 2.8 %collective-permute-start.14 = (bf16[1024,128]{1,0:T(8,128)(2,1)S(1)}, bf16[1024,128]{1,0:T(8,128)(2,1)S(1)}, u32[]{:S(2)}, u32[]{:S(2)}) collective-permute-start(bf16[1024,128]{1,0:T(8,128)(2,1)S(1)} %get-tuple-element.84), channel_id=1, source_target_pairs={{0,1},{1,0},{2,3},{3,2},{4,5},{5,4},{6,7},{7,6},{8,9},{9,8},{10,11... | collective-permute-start | bytes 786440 | tf_op jit(solution)/shard_map/ppermute | solution.py:497
  61.9 11.8 %collective-permute-start.16 = (bf16[256,2048]{1,0:T(8,128)(2,1)S(1)}, bf16[256,2048]{1,0:T(8,128)(2,1)S(1)}, u32[]{:S(2)}, u32[]{:S(2)}) collective-permute-start(bf16[256,2048]{1,0:T(8,128)(2,1)S(1)} %shard_map.107), channel_id=1, source_target_pairs={{0,1},{1,0},{2,3},{3,2},{4,5},{5,4},{6,7},{7,6},{8,9},{9,8},{10,11... | collective-permute-start | bytes 3145736 | tf_op jit(solution)/shard_map/ppermute | solution.py:497
  62.0 13.4 %collective-permute-start.15 = (bf16[1024,128]{1,0:T(8,128)(2,1)S(1)}, bf16[1024,128]{1,0:T(8,128)(2,1)S(1)}, u32[]{:S(2)}, u32[]{:S(2)}) collective-permute-start(bf16[1024,128]{1,0:T(8,128)(2,1)S(1)} %get-tuple-element.87), channel_id=1, source_target_pairs={{0,2},{2,4},{4,6},{6,8},{8,10},{10,12},{12,14},{14,16},{16,18},{18... | collective-permute-start | bytes 786440 | tf_op jit(solution)/shard_map/ppermute | solution.py:494
  68.7 11.0 %collective-permute-start.17 = (bf16[1024,128]{1,0:T(8,128)(2,1)S(1)}, bf16[1024,128]{1,0:T(8,128)(2,1)S(1)}, u32[]{:S(2)}, u32[]{:S(2)}) collective-permute-start(bf16[1024,128]{1,0:T(8,128)(2,1)S(1)} %get-tuple-element.95), channel_id=1, source_target_pairs={{0,4},{2,6},{4,8},{6,10},{8,12},{10,14},{12,16},{14,18},{16,20},{1... | collective-permute-start | bytes 786440 | tf_op jit(solution)/shard_map/ppermute | solution.py:494
  75.5 4.2 %collective-permute-start.18 = (bf16[512,128]{1,0:T(8,128)(2,1)S(1)}, bf16[512,128]{1,0:T(8,128)(2,1)S(1)}, u32[]{:S(2)}, u32[]{:S(2)}) collective-permute-start(bf16[512,128]{1,0:T(8,128)(2,1)S(1)} %slice.22), channel_id=1, source_target_pairs={{0,1},{1,0},{2,3},{3,2},{4,5},{5,4},{6,7},{7,6},{8,9},{9,8},{10,11... | collective-permute-start | bytes 393224 | tf_op jit(solution)/shard_map/ppermute | solution.py:497
  79.7 6.0 %collective-permute-start.19 = (bf16[512,128]{1,0:T(8,128)(2,1)S(1)}, bf16[512,128]{1,0:T(8,128)(2,1)S(1)}, u32[]{:S(2)}, u32[]{:S(2)}) collective-permute-start(bf16[512,128]{1,0:T(8,128)(2,1)S(1)} %slice.23), channel_id=1, source_target_pairs={{0,1},{1,0},{2,3},{3,2},{4,5},{5,4},{6,7},{7,6},{8,9},{9,8},{10,11... | collective-permute-start | bytes 393224 | tf_op jit(solution)/shard_map/ppermute | solution.py:497

commit v4 on v3

--- a/solution.py
+++ b/solution.py
@@ -162,7 +162,7 @@
 
 
 def near_scores_kernel(
-    place_ref, len_ref, full_ref, q_ref, own_ref, at1_ref, at2_ref, twin1_ref, twin2_ref,
+    place_ref, len_ref, full_ref, q_ref, own_ref, at1_ref, twin1_ref, at2_ref, other2_ref,
     range_ref, limit_ref, q_st, win, s_ref, top_ref,
 ):
     way = 1 - 2 * place_ref[1]
@@ -177,9 +177,10 @@
         for h in range(GROUPS):
             q_st[staged(sub, h), :] = q_ref[cut, head_cols(h)]
     win[pair_of(REACH), :] = own_ref[0:PAIR, :]
-    for k, ring, twin in ((1, at1_ref, twin1_ref), (2, at2_ref, twin2_ref)):
-        win[pair_of(REACH - k * way), :] = ring[0:PAIR, :]
-        win[pair_of(REACH + k * way), :] = twin[...]
+    win[pair_of(REACH - way), :] = at1_ref[0:PAIR, :]
+    win[pair_of(REACH + way), :] = twin1_ref[...]
+    win[pair_of(REACH + 2 * way), :] = at2_ref[PAIR : 2 * PAIR, :]
+    win[pair_of(REACH - 2 * way), :] = other2_ref[0:PAIR, :]
 
     def scores(subs):
         def body(at, top):
@@ -205,8 +206,8 @@
     def slot(n):
         return n + core * (FAR - 1 - 2 * n)
 
-    for n, ref in enumerate((at4_ref, at3_ref, twin3_ref, twin4_ref)):
-        win[pair_of(slot(n)), :] = ref[0:PAIR, :]
+    for n, part in enumerate((twin4_ref[...], at3_ref[0:PAIR, :], twin3_ref[...], at4_ref[PAIR : 2 * PAIR, :])):
+        win[pair_of(slot(n)), :] = part
     for sub in range(SUBS):
         for h in range(GROUPS):
             do_st[staged(sub, h), :] = do_ref[sub_rows(sub), head_cols(h)]
@@ -426,15 +427,16 @@
     return small_call(body, [parts[0].shape[0]], *parts)[0]
 
 
-def last_sum(*parts):
-    def body(*refs):
-        for at, out_ref in ((0, refs[-2]), (ROWS, refs[-1])):
-            total = refs[0][at : at + ROWS, :].astype(jnp.float32)
-            for ref in refs[1:-2]:
-                total += ref[at : at + ROWS, :].astype(jnp.float32)
+def last_sum(mid, near, far, near_twin, far_twin):
+    def body(mid_ref, near_ref, far_ref, near_twin_ref, far_twin_ref, key_ref, val_ref):
+        for at, out_ref in ((0, key_ref), (ROWS, val_ref)):
+            rows = slice(at, at + ROWS)
+            total = mid_ref[rows, :].astype(jnp.float32) + near_ref[rows, :].astype(jnp.float32)
+            total += far_ref[PAIR + at : PAIR + at + ROWS, :].astype(jnp.float32)
+            total += near_twin_ref[rows, :].astype(jnp.float32) + far_twin_ref[rows, :].astype(jnp.float32)
             out_ref[...] = total.astype(jnp.bfloat16)
 
-    return small_call(body, [ROWS, ROWS], *parts)
+    return small_call(body, [ROWS, ROWS], mid, near, far, near_twin, far_twin)
 
 
 def half_of(core, size):
@@ -488,10 +490,15 @@
     place = jnp.stack([index, core])
     core = core.reshape(1)
 
-    def step(block, far):
-        ways = [(2 * i, 2 * (i + far)) for i in range(devices - far)]
-        ways += [(2 * (i + far) + 1, 2 * i + 1) for i in range(devices - far)]
+    def onward(block):
+        ways = [(2 * i, 2 * (i + 1) if i + 1 < devices else 2 * i + 1) for i in range(devices)]
+        ways += [(2 * i + 1, 2 * (i - 1) + 1 if i >= 1 else 2 * i) for i in range(devices)]
         return lax.ppermute(block, ("cp", "hd"), ways)
+
+    def traded(block):
+        pairs = [(2 * i, 2 * (i + 2) + 1) for i in range(devices - 2)]
+        pairs += [(1, 3), (2 * devices - 4, 2 * devices - 2)]
+        return lax.ppermute(block, ("cp", "hd"), pairs + [(b, a) for a, b in pairs])
 
     def twin(block):
         return lax.ppermute(block, "hd", [(0, 1), (1, 0)])
@@ -500,18 +507,19 @@
     other_keys, other_values, late_grad, own = lax.optimization_barrier((twin(keys), twin(values), out_grad, own))
     block = stacked(own, other_keys, other_values)
     other_grad = twin(late_grad)
-    at2 = step(block, 2)
-    at1 = step(block, 1)
+    at2 = traded(block)
+    at1 = onward(block)
     attn_grad = project_back(core, out_grad, other_grad, out_weight)
     at2, attn_grad = lax.optimization_barrier((at2, attn_grad))
-    at4 = step(at2, 2)
-    at3 = step(at2, 1)
+    other2 = twin(at2)
+    at4 = traded(other2)
+    at3 = onward(other2)
     ranges, limit, q_st, win, s, top = near_scores(
         place, doc_lengths.reshape(1, -1), doc_full.reshape(1, -1), queries,
-        own, at1, at2, twin(at1[PAIR:]), twin(at2[PAIR:]),
+        own, at1, twin(at1[PAIR:]), at2, other2,
     )
     at4, top = lax.optimization_barrier((at4, top))
-    at3, twin4 = lax.optimization_barrier((at3, twin(at4[PAIR:])))
+    at3, twin4 = lax.optimization_barrier((at3, twin(at4[:PAIR])))
     attn, do_st, qs_st, dos_st, p, stats, dq_far, ahead, across = middle(
         place, ranges, limit, q_st, win, s, top, at3, at4, twin(at3[PAIR:]), twin4, attn_grad
     )
@@ -519,19 +527,19 @@
     across, away = lax.optimization_barrier((twin(across), away))
     out4, out3 = both_heads(ahead, across)
     out4, out3, stats = lax.optimization_barrier((out4, out3, stats))
-    in4 = step(out4, 2)
-    in3 = step(out3, 1)
+    in4 = traded(out4)
+    in3 = onward(out3)
     query_grad, ahead, across, mid = near_back(place, ranges, win, p, do_st, qs_st, dos_st, stats, dq_far)
-    came = summed(in4, in3)
+    came = summed(in3, twin(in4))
     came, across = lax.optimization_barrier((came, twin(across)))
     far_out, near_out = far_and_near(ahead, across, came)
     far_out, away = lax.optimization_barrier((far_out, away))
-    far = step(far_out, 2)
-    near = step(near_out, 1)
+    far = traded(far_out)
+    near = onward(near_out)
     layer_out = project(core, attn, out_weight, twin(away))
     near, layer_out = lax.optimization_barrier((near, layer_out))
     far, near_twin = lax.optimization_barrier((far, twin(near[PAIR:])))
-    key_grad, value_grad = last_sum(mid, near, far, near_twin, twin(far[PAIR:]))
+    key_grad, value_grad = last_sum(mid, near, far, near_twin, twin(far[:PAIR]))
     return (layer_out, query_grad, key_grad, value_grad)
 
 

time: 87.4 us -> 81.3 us (0.930)
  the two profiles are of different devices: /device:TPU:49 before, /device:TPU:25 now
where the time goes in v4:
time: 81.3 us
  starting transfers between devices  38 us (47%)
  Pallas kernels  20.4 us (25%)
  waiting for transfers between devices  17.6 us (22%)
  local copies, waits for them, and re-layouts  4.39 us (5%)
  between operations  0.82 us (1%)
    ppermute x4, starting transfers between devices, traded(): return lax.ppermute(block, ('cp', 'hd'), pairs + [(b, a) for a, b in pairs])  14.6 us
    ppermute x4, starting transfers between devices, onward(): return lax.ppermute(block, ('cp', 'hd'), ways)  12.8 us
    ppermute x13, starting transfers between devices, twin(): return lax.ppermute(block, 'hd', [(0, 1), (1, 0)])  10.7 us
    ppermute x4, waiting for transfers between devices, traded(): return lax.ppermute(block, ('cp', 'hd'), pairs + [(b, a) for a, b in pairs])  8.88 us
    pallas_call x1, Pallas kernels, near_back(): pl.pallas_call(near_back_kernel, out_shape=(bf16(ROWS, GROUPS * DH), bf16...  6.77 us
    ppermute x13, waiting for transfers between devices, twin(): return lax.ppermute(block, 'hd', [(0, 1), (1, 0)])  5.14 us
    pallas_call x1, Pallas kernels, middle(): pl.pallas_call(middle_kernel, out_shape=(bf16(ROWS, GROUPS * DH), bf16(ST...  4.68 us
    unnamed x16, local copies, waits for them, and re-layouts  4.34 us
  transfers between devices with their start and end apart: 21, of which 11 were waited for; matrix products, arithmetic and copies ran while one was open for 0% of the time, Pallas kernels for 18%

profile of v4, /device:TPU:25, one launch (start us, length us, event | category | flops | bytes accessed | tf_op | source)
XLA Modules:
  0.0 81.3 jit_solution(1753133283979712529)
XLA Ops:
  0.6 0.8 collective-permute-start
  1.4 0.1 collective-permute-start.1
  1.5 1.5 %shard_map.102.refs_0_.own_ref = bf16[512,128]{1,0:T(8,128)(2,1)} custom-call(bf16[256,128]{1,0:T(8,128)(2,1)} %refs_0_.1, bf16[256,128]{1,0:T(8,128)(2,1)} %refs_1_.1), custom_call_target="tpu_custom_call" | custom-call | bytes 1000000 | tf_op jit(solution)/shard_map/pallas_call | solution.py:400
  3.1 0.0 collective-permute-done.refs_1_
  3.1 0.5 collective-permute-start.5
  3.6 0.9 %copy-done.3 = bf16[512,128]{1,0:T(8,128)(2,1)S(1)} copy-done((bf16[512,128]{1,0:T(8,128)(2,1)S(1)}, bf16[512,128]{1,0:T(8,128)(2,1)}, u32[]{:S(2)}) %copy-start.3) | copy-done | bytes 131096
  4.5 8.5 %collective-permute-start.4 = (bf16[1024,128]{1,0:T(8,128)(2,1)S(1)}, bf16[1024,128]{1,0:T(8,128)(2,1)S(1)}, u32[]{:S(2)}, u32[]{:S(2)}) collective-permute-start(bf16[1024,128]{1,0:T(8,128)(2,1)S(1)} %shard_map.103), channel_id=1, source_target_pairs={{0,5},{2,7},{4,9},{6,11},{8,13},{10,15},{12,17},{14,19},{16,21},{1... | collective-permute-start | bytes 786440 | tf_op jit(solution)/shard_map/ppermute | solution.py:501
  13.0 0.0 collective-permute-done.5.other_ref
  13.0 2.2 %copy-done = bf16[4096,512]{1,0:T(8,128)(2,1)S(1)} copy-done((bf16[4096,512]{1,0:T(8,128)(2,1)S(1)}, bf16[4096,512]{1,0:T(8,128)(2,1)}, u32[]{:S(2)}) %copy-start) | copy-done | bytes 4194328
  15.2 1.2 %copy-done.2 = bf16[256,2048]{1,0:T(8,128)(2,1)S(1)} copy-done((bf16[256,2048]{1,0:T(8,128)(2,1)S(1)}, bf16[256,2048]{1,0:T(8,128)(2,1)}, u32[]{:S(2)}) %copy-start.2) | copy-done | bytes 1048600
  16.4 1.3 %shard_map.104.do_ref = bf16[256,512]{1,0:T(8,128)(2,1)S(1)} custom-call(s32[1]{0:T(128)} %bitcast.1.core_ref.half_ref, bf16[256,2048]{1,0:T(8,128)(2,1)S(1)} %copy-done.2, bf16[256,2048]{1,0:T(8,128)(2,1)S(1)} %collective-permute-done.5.other_ref, bf16[4096,512]{1,0:T(8,128)(2,1)S(1)} %copy-done), custom_call_target="tpu_custom_call" | custom-call | flops 1073741824 | bytes 6000000 | tf_op jit(solution)/shard_map/pallas_call | solution.py:455
  17.7 1.4 %collective-permute-done.4.at2_ref = bf16[1024,128]{1,0:T(8,128)(2,1)S(1)} collective-permute-done((bf16[1024,128]{1,0:T(8,128)(2,1)S(1)}, bf16[1024,128]{1,0:T(8,128)(2,1)S(1)}, u32[]{:S(2)}, u32[]{:S(2)}) %collective-permute-start.4) | collective-permute-done | bytes 262176 | tf_op jit(solution)/shard_map/ppermute | solution.py:501
  19.1 4.6 %collective-permute-start.2 = (bf16[1024,128]{1,0:T(8,128)(2,1)S(1)}, bf16[1024,128]{1,0:T(8,128)(2,1)S(1)}, u32[]{:S(2)}, u32[]{:S(2)}) collective-permute-start(bf16[1024,128]{1,0:T(8,128)(2,1)S(1)} %shard_map.103), channel_id=1, source_target_pairs={{0,2},{2,4},{4,6},{6,8},{8,10},{10,12},{12,14},{14,16},{16,18},{18... | collective-permute-start | bytes 786440 | tf_op jit(solution)/shard_map/ppermute | solution.py:496
  23.7 4.6 %collective-permute-start.7 = (bf16[1024,128]{1,0:T(8,128)(2,1)S(1)}, bf16[1024,128]{1,0:T(8,128)(2,1)S(1)}, u32[]{:S(2)}, u32[]{:S(2)}) collective-permute-start(bf16[1024,128]{1,0:T(8,128)(2,1)S(1)} %collective-permute-done.6.other2_ref), channel_id=1, source_target_pairs={{0,5},{2,7},{4,9},{6,11},{8,13},{10,15},{12,17},{14,19},{16,21},{1... | collective-permute-start | bytes 786440 | tf_op jit(solution)/shard_map/ppermute | solution.py:501
  28.2 2.1 %collective-permute-start.3 = (bf16[512,128]{1,0:T(8,128)(2,1)S(1)}, bf16[512,128]{1,0:T(8,128)(2,1)S(1)}, u32[]{:S(2)}, u32[]{:S(2)}) collective-permute-start(bf16[512,128]{1,0:T(8,128)(2,1)S(1)} %slice.20), channel_id=1, source_target_pairs={{0,1},{1,0},{2,3},{3,2},{4,5},{5,4},{6,7},{7,6},{8,9},{9,8},{10,11... | collective-permute-start | bytes 393224 | tf_op jit(solution)/shard_map/ppermute | solution.py:504
  30.3 3.3 %collective-permute-start.8 = (bf16[1024,128]{1,0:T(8,128)(2,1)S(1)}, bf16[1024,128]{1,0:T(8,128)(2,1)S(1)}, u32[]{:S(2)}, u32[]{:S(2)}) collective-permute-start(bf16[1024,128]{1,0:T(8,128)(2,1)S(1)} %collective-permute-done.6.other2_ref), channel_id=1, source_target_pairs={{0,2},{2,4},{4,6},{6,8},{8,10},{10,12},{12,14},{14,16},{16,18},{18... | collective-permute-start | bytes 786440 | tf_op jit(solution)/shard_map/ppermute | solution.py:496
  33.6 0.1 pad_add_fusion.place_ref
  33.7 2.8 %shard_map.105 = (s32[4]{0:T(128)S(1)}, s32[8,256]{1,0:T(8,128)S(1)}, bf16[1024,128]{1,0:T(8,128)(2,1)S(1)}, bf16[2560,128]{1,0:T(8,128)(2,1)S(1)}, f32[1280,1024]{1,0:T(8,128)S(1)}, /*index=5*/f32[8,1024]{1,0:T(8,128)S(1)}) custom-call(s32[2]{0:T(128)S(1)} %pad_add_fusion.place_ref, s32[1,64]{1,0:T(1,128)S(1)} %bitcast.4, s32[1,64]{1,0:T(1,128)S(1)} %bitcast.5, ...), custom_call_target="tpu_custom_call" | custom-call | flops 1000000000 | bytes 6000000 | tf_op jit(solution)/shard_map/pallas_call | solution.py:305
  36.5 0.0 copy-start.1
  36.5 0.1 collective-permute-start.9
  36.6 0.3 collective-permute-done.8.at3_ref
  36.9 1.0 %collective-permute-done.9.twin4_ref = bf16[512,128]{1,0:T(8,128)(2,1)S(1)} collective-permute-done((bf16[512,128]{1,0:T(8,128)(2,1)S(1)}, bf16[512,128]{1,0:T(8,128)(2,1)S(1)}, u32[]{:S(2)}, u32[]{:S(2)}) %collective-permute-start.9) | collective-permute-done | bytes 131104 | tf_op jit(solution)/shard_map/ppermute | solution.py:504
  38.0 3.1 %collective-permute-start.10 = (bf16[512,128]{1,0:T(8,128)(2,1)S(1)}, bf16[512,128]{1,0:T(8,128)(2,1)S(1)}, u32[]{:S(2)}, u32[]{:S(2)}) collective-permute-start(bf16[512,128]{1,0:T(8,128)(2,1)S(1)} %slice.17), channel_id=1, source_target_pairs={{0,1},{1,0},{2,3},{3,2},{4,5},{5,4},{6,7},{7,6},{8,9},{9,8},{10,11... | collective-permute-start | bytes 393224 | tf_op jit(solution)/shard_map/ppermute | solution.py:504
  41.1 1.0 %collective-permute-done.10.twin3_ref = bf16[512,128]{1,0:T(8,128)(2,1)S(1)} collective-permute-done((bf16[512,128]{1,0:T(8,128)(2,1)S(1)}, bf16[512,128]{1,0:T(8,128)(2,1)S(1)}, u32[]{:S(2)}, u32[]{:S(2)}) %collective-permute-start.10) | collective-permute-done | bytes 131104 | tf_op jit(solution)/shard_map/ppermute | solution.py:504
  42.1 4.7 %shard_map.106 = (bf16[256,512]{1,0:T(8,128)(2,1)S(1)}, bf16[1024,128]{1,0:T(8,128)(2,1)S(1)}, bf16[1024,128]{1,0:T(8,128)(2,1)S(1)}, bf16[1024,128]{1,0:T(8,128...) custom-call(s32[2]{0:T(128)S(1)} %pad_add_fusion.place_ref, ...), custom_call_target="tpu_custom_call" | custom-call | flops 1000000000 | bytes 6000000 | tf_op jit(solution)/shard_map/pallas_call | solution.py:318
  46.8 0.4 collective-permute-start.11
  47.2 0.7 shard_map.107
  48.0 0.4 collective-permute-done.11.across_ref
  48.4 0.1 collective-permute-start.13
  48.5 3.1 %collective-permute-start.12 = (bf16[1024,128]{1,0:T(8,128)(2,1)S(1)}, bf16[1024,128]{1,0:T(8,128)(2,1)S(1)}, u32[]{:S(2)}, u32[]{:S(2)}) collective-permute-start(bf16[1024,128]{1,0:T(8,128)(2,1)S(1)} %get-tuple-element.82), channel_id=1, source_target_pairs={{0,2},{2,4},{4,6},{6,8},{8,10},{10,12},{12,14},{14,16},{16,18},{18... | collective-permute-start | bytes 786440 | tf_op jit(solution)/shard_map/ppermute | solution.py:496
  51.6 6.8 %shard_map.109 = (bf16[256,512]{1,0:T(8,128)(2,1)}, bf16[1024,128]{1,0:T(8,128)(2,1)S(1)}, bf16[1024,128]{1,0:T(8,128)(2,1)S(1)}, bf16[512,128]{1,0:T(8,128)(2,1)S(1)}) custom-call(s32[2]{0:T(128)S(1)} %pad_add_fusion.place_ref, s32[4]{0:T(128)S(1)} %get-tuple-element.57.range_ref, bf16[2560,128]{1,0:T(8,128)(2,1)S(1)} %get-tuple-element.58.near_win.win, ...), custom_call_target="tpu_custom_call" | custom-call | flops 20000000000 | bytes 30000000 | tf_op jit(solution)/shard_map/pallas_call | solution.py:340
  58.4 3.7 %collective-permute-done.13 = bf16[1024,128]{1,0:T(8,128)(2,1)S(1)} collective-permute-done((bf16[1024,128]{1,0:T(8,128)(2,1)S(1)}, bf16[1024,128]{1,0:T(8,128)(2,1)S(1)}, u32[]{:S(2)}, u32[]{:S(2)}) %collective-permute-start.13) | collective-permute-done | bytes 262176 | tf_op jit(solution)/shard_map/ppermute | solution.py:501
  62.1 0.5 collective-permute-start.15
  62.7 0.0 collective-permute-done.12.refs_0_
  62.7 1.0 %collective-permute-done.14.refs_1_ = bf16[1024,128]{1,0:T(8,128)(2,1)S(1)} collective-permute-done((bf16[1024,128]{1,0:T(8,128)(2,1)S(1)}, bf16[1024,128]{1,0:T(8,128)(2,1)S(1)}, u32[]{:S(2)}, u32[]{:S(2)}) %collective-permute-start.14) | collective-permute-done | bytes 262176 | tf_op jit(solution)/shard_map/ppermute | solution.py:504
  63.7 0.1 shard_map.110.came_ref
  63.7 0.3 collective-permute-done.15.across_ref
  64.1 0.1 shard_map.111
  64.1 0.2 collective-permute-start.17
  64.3 1.8 %collective-permute-start.16 = (bf16[1024,128]{1,0:T(8,128)(2,1)S(1)}, bf16[1024,128]{1,0:T(8,128)(2,1)S(1)}, u32[]{:S(2)}, u32[]{:S(2)}) collective-permute-start(bf16[1024,128]{1,0:T(8,128)(2,1)S(1)} %get-tuple-element.87), channel_id=1, source_target_pairs={{0,2},{2,4},{4,6},{6,8},{8,10},{10,12},{12,14},{14,16},{16,18},{18... | collective-permute-start | bytes 786440 | tf_op jit(solution)/shard_map/ppermute | solution.py:496
  66.2 1.4 %collective-permute-start.18 = (bf16[1024,128]{1,0:T(8,128)(2,1)S(1)}, bf16[1024,128]{1,0:T(8,128)(2,1)S(1)}, u32[]{:S(2)}, u32[]{:S(2)}) collective-permute-start(bf16[1024,128]{1,0:T(8,128)(2,1)S(1)} %get-tuple-element.95), channel_id=1, source_target_pairs={{0,5},{2,7},{4,9},{6,11},{8,13},{10,15},{12,17},{14,19},{16,21},{1... | collective-permute-start | bytes 786440 | tf_op jit(solution)/shard_map/ppermute | solution.py:501
  67.6 1.7 %shard_map.112 = bf16[256,2048]{1,0:T(8,128)(2,1)} custom-call(s32[1]{0:T(128)} %bitcast.1.core_ref.half_ref, bf16[256,512]{1,0:T(8,128)(2,1)S(1)} %get-tuple-element.74.a_ref, bf16[4096,512]{1,0:T(8,128)(2,1)S(1)} %copy-done.1, bf16[256,2048]{1,0:T(8,128)(2,1)S(1)} %collective-permute-done.17.refs_0_), custom_call_target="tpu_custom_call" | custom-call | flops 536870912 | bytes 4000000 | tf_op jit(solution)/shard_map/pallas_call | solution.py:476
  69.3 3.3 %collective-permute-done.16.near_ref = bf16[1024,128]{1,0:T(8,128)(2,1)S(1)} collective-permute-done((bf16[1024,128]{1,0:T(8,128)(2,1)S(1)}, bf16[1024,128]{1,0:T(8,128)(2,1)S(1)}, u32[]{:S(2)}, u32[]{:S(2)}) %collective-permute-start.16) | collective-permute-done | bytes 262176 | tf_op jit(solution)/shard_map/ppermute | solution.py:496
  72.7 2.8 %collective-permute-start.19 = (bf16[512,128]{1,0:T(8,128)(2,1)S(1)}, bf16[512,128]{1,0:T(8,128)(2,1)S(1)}, u32[]{:S(2)}, u32[]{:S(2)}) collective-permute-start(bf16[512,128]{1,0:T(8,128)(2,1)S(1)} %slice.18), channel_id=1, source_target_pairs={{0,1},{1,0},{2,3},{3,2},{4,5},{5,4},{6,7},{7,6},{8,9},{9,8},{10,11... | collective-permute-start | bytes 393224 | tf_op jit(solution)/shard_map/ppermute | solution.py:504
  75.4 3.7 %collective-permute-done.18.far_ref = bf16[1024,128]{1,0:T(8,128)(2,1)S(1)} collective-permute-done((bf16[1024,128]{1,0:T(8,128)(2,1)S(1)}, bf16[1024,128]{1,0:T(8,128)(2,1)S(1)}, u32[]{:S(2)}, u32[]{:S(2)}) %collective-permute-start.18) | collective-permute-done | bytes 262176 | tf_op jit(solution)/shard_map/ppermute | solution.py:501
  79.2 0.1 collective-permute-start.20
  79.3 1.3 %collective-permute-done.20.far_twin_ref = bf16[512,128]{1,0:T(8,128)(2,1)S(1)} collective-permute-done((bf16[512,128]{1,0:T(8,128)(2,1)S(1)}, bf16[512,128]{1,0:T(8,128)(2,1)S(1)}, u32[]{:S(2)}, u32[]{:S(2)}) %collective-permute-start.20) | collective-permute-done | bytes 131104 | tf_op jit(solution)/shard_map/ppermute | solution.py:504
  80.6 0.7 shard_map.113
  (28 shorter events, 0.1 us)
Async XLA Ops:
  0.6 33.0 %copy-start.5 = (bf16[256,512]{1,0:T(8,128)(2,1)S(1)}, bf16[256,512]{1,0:T(8,128)(2,1)}, u32[]{:S(2)}) copy-start(bf16[256,512]{1,0:T(8,128)(2,1)} %q_ref.1) | copy-start | bytes 786436
  0.6 2.4 %collective-permute-start = (bf16[256,128]{1,0:T(8,128)(2,1)}, bf16[256,128]{1,0:T(8,128)(2,1)S(1)}, u32[]{:S(2)}, u32[]{:S(2)}) collective-permute-start(bf16[256,128]{1,0:T(8,128)(2,1)} %refs_0_.1), channel_id=1, source_target_pairs={{0,1},{1,0},{2,3},{3,2},{4,5},{5,4},{6,7},{7,6},{8,9},{9,8},{10,11... | collective-permute-start | bytes 196616 | tf_op jit(solution)/shard_map/ppermute | solution.py:504
  1.4 1.7 %collective-permute-start.1 = (bf16[256,128]{1,0:T(8,128)(2,1)}, bf16[256,128]{1,0:T(8,128)(2,1)S(1)}, u32[]{:S(2)}, u32[]{:S(2)}) collective-permute-start(bf16[256,128]{1,0:T(8,128)(2,1)} %refs_1_.1), channel_id=1, source_target_pairs={{0,1},{1,0},{2,3},{3,2},{4,5},{5,4},{6,7},{7,6},{8,9},{9,8},{10,11... | collective-permute-start | bytes 196616 | tf_op jit(solution)/shard_map/ppermute | solution.py:504
  3.1 9.9 %collective-permute-start.5 = (bf16[256,2048]{1,0:T(8,128)(2,1)}, bf16[256,2048]{1,0:T(8,128)(2,1)S(1)}, u32[]{:S(2)}, u32[]{:S(2)}) collective-permute-start(bf16[256,2048]{1,0:T(8,128)(2,1)} %own_ref.1), channel_id=1, source_target_pairs={{0,1},{1,0},{2,3},{3,2},{4,5},{5,4},{6,7},{7,6},{8,9},{9,8},{10,11... | collective-permute-start | bytes 3145736 | tf_op jit(solution)/shard_map/ppermute | solution.py:504
  3.6 0.9 %copy-start.3 = (bf16[512,128]{1,0:T(8,128)(2,1)S(1)}, bf16[512,128]{1,0:T(8,128)(2,1)}, u32[]{:S(2)}) copy-start(bf16[512,128]{1,0:T(8,128)(2,1)} %shard_map.102.refs_0_.own_ref) | copy-start | bytes 393220
  4.5 29.2 %copy-start.4 = (bf16[512,128]{1,0:T(8,128)(2,1)S(1)}, bf16[512,128]{1,0:T(8,128)(2,1)}, u32[]{:S(2)}) copy-start(bf16[512,128]{1,0:T(8,128)(2,1)} %shard_map.102.refs_0_.own_ref) | copy-start | bytes 393220
  4.5 29.2 %copy-start.6 = (s32[64]{0:T(128)S(1)}, s32[64]{0:T(128)}, u32[]{:S(2)}) copy-start(s32[64]{0:T(128)} %param.11) | copy-start | bytes 772
  4.5 29.2 %copy-start.7 = (s32[64]{0:T(128)S(1)}, s32[64]{0:T(128)}, u32[]{:S(2)}) copy-start(s32[64]{0:T(128)} %param.12) | copy-start | bytes 772
  4.5 14.6 %collective-permute-start.4 = (bf16[1024,128]{1,0:T(8,128)(2,1)S(1)}, bf16[1024,128]{1,0:T(8,128)(2,1)S(1)}, u32[]{:S(2)}, u32[]{:S(2)}) collective-permute-start(bf16[1024,128]{1,0:T(8,128)(2,1)S(1)} %shard_map.103), channel_id=1, source_target_pairs={{0,5},{2,7},{4,9},{6,11},{8,13},{10,15},{12,17},{14,19},{16,21},{1... | collective-permute-start | bytes 786440 | tf_op jit(solution)/shard_map/ppermute | solution.py:501
  13.0 2.2 %copy-start = (bf16[4096,512]{1,0:T(8,128)(2,1)S(1)}, bf16[4096,512]{1,0:T(8,128)(2,1)}, u32[]{:S(2)}) copy-start(bf16[4096,512]{1,0:T(8,128)(2,1)} %w_ref.5) | copy-start | bytes 12582916
  15.2 1.2 %copy-start.2 = (bf16[256,2048]{1,0:T(8,128)(2,1)S(1)}, bf16[256,2048]{1,0:T(8,128)(2,1)}, u32[]{:S(2)}) copy-start(bf16[256,2048]{1,0:T(8,128)(2,1)} %own_ref.1) | copy-start | bytes 3145732
  19.1 4.6 %collective-permute-start.6 = (bf16[1024,128]{1,0:T(8,128)(2,1)S(1)}, bf16[1024,128]{1,0:T(8,128)(2,1)S(1)}, u32[]{:S(2)}, u32[]{:S(2)}) collective-permute-start(bf16[1024,128]{1,0:T(8,128)(2,1)S(1)} %collective-permute-done.4.at2_ref), channel_id=1, source_target_pairs={{0,1},{1,0},{2,3},{3,2},{4,5},{5,4},{6,7},{7,6},{8,9},{9,8},{10,11... | collective-permute-start | bytes 786440 | tf_op jit(solution)/shard_map/ppermute | solution.py:504
  19.1 9.1 %collective-permute-start.2 = (bf16[1024,128]{1,0:T(8,128)(2,1)S(1)}, bf16[1024,128]{1,0:T(8,128)(2,1)S(1)}, u32[]{:S(2)}, u32[]{:S(2)}) collective-permute-start(bf16[1024,128]{1,0:T(8,128)(2,1)S(1)} %shard_map.103), channel_id=1, source_target_pairs={{0,2},{2,4},{4,6},{6,8},{8,10},{10,12},{12,14},{14,16},{16,18},{18... | collective-permute-start | bytes 786440 | tf_op jit(solution)/shard_map/ppermute | solution.py:496
  23.7 12.8 %collective-permute-start.7 = (bf16[1024,128]{1,0:T(8,128)(2,1)S(1)}, bf16[1024,128]{1,0:T(8,128)(2,1)S(1)}, u32[]{:S(2)}, u32[]{:S(2)}) collective-permute-start(bf16[1024,128]{1,0:T(8,128)(2,1)S(1)} %collective-permute-done.6.other2_ref), channel_id=1, source_target_pairs={{0,5},{2,7},{4,9},{6,11},{8,13},{10,15},{12,17},{14,19},{16,21},{1... | collective-permute-start | bytes 786440 | tf_op jit(solution)/shard_map/ppermute | solution.py:501
  28.2 5.4 %collective-permute-start.3 = (bf16[512,128]{1,0:T(8,128)(2,1)S(1)}, bf16[512,128]{1,0:T(8,128)(2,1)S(1)}, u32[]{:S(2)}, u32[]{:S(2)}) collective-permute-start(bf16[512,128]{1,0:T(8,128)(2,1)S(1)} %slice.20), channel_id=1, source_target_pairs={{0,1},{1,0},{2,3},{3,2},{4,5},{5,4},{6,7},{7,6},{8,9},{9,8},{10,11... | collective-permute-start | bytes 393224 | tf_op jit(solution)/shard_map/ppermute | solution.py:504
  30.3 6.6 %collective-permute-start.8 = (bf16[1024,128]{1,0:T(8,128)(2,1)S(1)}, bf16[1024,128]{1,0:T(8,128)(2,1)S(1)}, u32[]{:S(2)}, u32[]{:S(2)}) collective-permute-start(bf16[1024,128]{1,0:T(8,128)(2,1)S(1)} %collective-permute-done.6.other2_ref), channel_id=1, source_target_pairs={{0,2},{2,4},{4,6},{6,8},{8,10},{10,12},{12,14},{14,16},{16,18},{18... | collective-permute-start | bytes 786440 | tf_op jit(solution)/shard_map/ppermute | solution.py:496
  36.5 10.7 %copy-start.1 = (bf16[4096,512]{1,0:T(8,128)(2,1)S(1)}, bf16[4096,512]{1,0:T(8,128)(2,1)}, u32[]{:S(2)}) copy-start(bf16[4096,512]{1,0:T(8,128)(2,1)} %w_ref.5) | copy-start | bytes 12582916
  36.5 1.4 %collective-permute-start.9 = (bf16[512,128]{1,0:T(8,128)(2,1)S(1)}, bf16[512,128]{1,0:T(8,128)(2,1)S(1)}, u32[]{:S(2)}, u32[]{:S(2)}) collective-permute-start(bf16[512,128]{1,0:T(8,128)(2,1)S(1)} %slice.16), channel_id=1, source_target_pairs={{0,1},{1,0},{2,3},{3,2},{4,5},{5,4},{6,7},{7,6},{8,9},{9,8},{10,11... | collective-permute-start | bytes 393224 | tf_op jit(solution)/shard_map/ppermute | solution.py:504
  38.0 4.1 %collective-permute-start.10 = (bf16[512,128]{1,0:T(8,128)(2,1)S(1)}, bf16[512,128]{1,0:T(8,128)(2,1)S(1)}, u32[]{:S(2)}, u32[]{:S(2)}) collective-permute-start(bf16[512,128]{1,0:T(8,128)(2,1)S(1)} %slice.17), channel_id=1, source_target_pairs={{0,1},{1,0},{2,3},{3,2},{4,5},{5,4},{6,7},{7,6},{8,9},{9,8},{10,11... | collective-permute-start | bytes 393224 | tf_op jit(solution)/shard_map/ppermute | solution.py:504
  46.8 1.6 %collective-permute-start.11 = (bf16[1024,128]{1,0:T(8,128)(2,1)S(1)}, bf16[1024,128]{1,0:T(8,128)(2,1)S(1)}, u32[]{:S(2)}, u32[]{:S(2)}) collective-permute-start(bf16[1024,128]{1,0:T(8,128)(2,1)S(1)} %get-tuple-element.73), channel_id=1, source_target_pairs={{0,1},{1,0},{2,3},{3,2},{4,5},{5,4},{6,7},{7,6},{8,9},{9,8},{10,11... | collective-permute-start | bytes 786440 | tf_op jit(solution)/shard_map/ppermute | solution.py:504
  48.4 13.7 %collective-permute-start.13 = (bf16[1024,128]{1,0:T(8,128)(2,1)S(1)}, bf16[1024,128]{1,0:T(8,128)(2,1)S(1)}, u32[]{:S(2)}, u32[]{:S(2)}) collective-permute-start(bf16[1024,128]{1,0:T(8,128)(2,1)S(1)} %get-tuple-element.83), channel_id=1, source_target_pairs={{0,5},{2,7},{4,9},{6,11},{8,13},{10,15},{12,17},{14,19},{16,21},{1... | collective-permute-start | bytes 786440 | tf_op jit(solution)/shard_map/ppermute | solution.py:501
  48.5 14.1 %collective-permute-start.12 = (bf16[1024,128]{1,0:T(8,128)(2,1)S(1)}, bf16[1024,128]{1,0:T(8,128)(2,1)S(1)}, u32[]{:S(2)}, u32[]{:S(2)}) collective-permute-start(bf16[1024,128]{1,0:T(8,128)(2,1)S(1)} %get-tuple-element.82), channel_id=1, source_target_pairs={{0,2},{2,4},{4,6},{6,8},{8,10},{10,12},{12,14},{14,16},{16,18},{18... | collective-permute-start | bytes 786440 | tf_op jit(solution)/shard_map/ppermute | solution.py:496
  62.1 1.5 %collective-permute-start.14 = (bf16[1024,128]{1,0:T(8,128)(2,1)S(1)}, bf16[1024,128]{1,0:T(8,128)(2,1)S(1)}, u32[]{:S(2)}, u32[]{:S(2)}) collective-permute-start(bf16[1024,128]{1,0:T(8,128)(2,1)S(1)} %collective-permute-done.13), channel_id=1, source_target_pairs={{0,1},{1,0},{2,3},{3,2},{4,5},{5,4},{6,7},{7,6},{8,9},{9,8},{10,11... | collective-permute-start | bytes 786440 | tf_op jit(solution)/shard_map/ppermute | solution.py:504
  62.1 1.9 %collective-permute-start.15 = (bf16[1024,128]{1,0:T(8,128)(2,1)S(1)}, bf16[1024,128]{1,0:T(8,128)(2,1)S(1)}, u32[]{:S(2)}, u32[]{:S(2)}) collective-permute-start(bf16[1024,128]{1,0:T(8,128)(2,1)S(1)} %get-tuple-element.84), channel_id=1, source_target_pairs={{0,1},{1,0},{2,3},{3,2},{4,5},{5,4},{6,7},{7,6},{8,9},{9,8},{10,11... | collective-permute-start | bytes 786440 | tf_op jit(solution)/shard_map/ppermute | solution.py:504
  64.1 3.5 %collective-permute-start.17 = (bf16[256,2048]{1,0:T(8,128)(2,1)S(1)}, bf16[256,2048]{1,0:T(8,128)(2,1)S(1)}, u32[]{:S(2)}, u32[]{:S(2)}) collective-permute-start(bf16[256,2048]{1,0:T(8,128)(2,1)S(1)} %shard_map.107), channel_id=1, source_target_pairs={{0,1},{1,0},{2,3},{3,2},{4,5},{5,4},{6,7},{7,6},{8,9},{9,8},{10,11... | collective-permute-start | bytes 3145736 | tf_op jit(solution)/shard_map/ppermute | solution.py:504
  64.3 8.3 %collective-permute-start.16 = (bf16[1024,128]{1,0:T(8,128)(2,1)S(1)}, bf16[1024,128]{1,0:T(8,128)(2,1)S(1)}, u32[]{:S(2)}, u32[]{:S(2)}) collective-permute-start(bf16[1024,128]{1,0:T(8,128)(2,1)S(1)} %get-tuple-element.87), channel_id=1, source_target_pairs={{0,2},{2,4},{4,6},{6,8},{8,10},{10,12},{12,14},{14,16},{16,18},{18... | collective-permute-start | bytes 786440 | tf_op jit(solution)/shard_map/ppermute | solution.py:496
  66.2 13.0 %collective-permute-start.18 = (bf16[1024,128]{1,0:T(8,128)(2,1)S(1)}, bf16[1024,128]{1,0:T(8,128)(2,1)S(1)}, u32[]{:S(2)}, u32[]{:S(2)}) collective-permute-start(bf16[1024,128]{1,0:T(8,128)(2,1)S(1)} %get-tuple-element.95), channel_id=1, source_target_pairs={{0,5},{2,7},{4,9},{6,11},{8,13},{10,15},{12,17},{14,19},{16,21},{1... | collective-permute-start | bytes 786440 | tf_op jit(solution)/shard_map/ppermute | solution.py:501
  72.7 6.5 %collective-permute-start.19 = (bf16[512,128]{1,0:T(8,128)(2,1)S(1)}, bf16[512,128]{1,0:T(8,128)(2,1)S(1)}, u32[]{:S(2)}, u32[]{:S(2)}) collective-permute-start(bf16[512,128]{1,0:T(8,128)(2,1)S(1)} %slice.18), channel_id=1, source_target_pairs={{0,1},{1,0},{2,3},{3,2},{4,5},{5,4},{6,7},{7,6},{8,9},{9,8},{10,11... | collective-permute-start | bytes 393224 | tf_op jit(solution)/shard_map/ppermute | solution.py:504
  79.2 1.4 %collective-permute-start.20 = (bf16[512,128]{1,0:T(8,128)(2,1)S(1)}, bf16[512,128]{1,0:T(8,128)(2,1)S(1)}, u32[]{:S(2)}, u32[]{:S(2)}) collective-permute-start(bf16[512,128]{1,0:T(8,128)(2,1)S(1)} %slice.19), channel_id=1, source_target_pairs={{0,1},{1,0},{2,3},{3,2},{4,5},{5,4},{6,7},{7,6},{8,9},{9,8},{10,11... | collective-permute-start | bytes 393224 | tf_op jit(solution)/shard_map/ppermute | solution.py:504

commit v5 on v3

--- a/solution.py
+++ b/solution.py
@@ -402,7 +402,7 @@
         in_specs=[ANY] * n,
         out_specs=VMEM,
         scratch_shapes=[pltpu.SemaphoreType.DMA((n,))],
-        compiler_params=pltpu.CompilerParams(vmem_limit_bytes=BIG),
+        compiler_params=pltpu.CompilerParams(vmem_limit_bytes=48 * 1024 * 1024),
         cost_estimate=pl.CostEstimate(flops=0, bytes_accessed=10**6, transcendentals=0),
     )(*parts)
 
@@ -489,16 +489,17 @@
     core = core.reshape(1)
 
     def step(block, far):
-        ways = [(2 * i, 2 * (i + far)) for i in range(devices - far)]
-        ways += [(2 * (i + far) + 1, 2 * i + 1) for i in range(devices - far)]
+        ways = [(2 * i, 2 * (i + far) if i + far < devices else 2 * i + 1) for i in range(devices)]
+        ways += [(2 * i + 1, 2 * (i - far) + 1 if i >= far else 2 * i) for i in range(devices)]
         return lax.ppermute(block, ("cp", "hd"), ways)
 
     def twin(block):
         return lax.ppermute(block, "hd", [(0, 1), (1, 0)])
 
     own = packed(keys, values)
-    other_keys, other_values, late_grad, own = lax.optimization_barrier((twin(keys), twin(values), out_grad, own))
+    other_keys, other_values, own = lax.optimization_barrier((twin(keys), twin(values), own))
     block = stacked(own, other_keys, other_values)
+    block, late_grad = lax.optimization_barrier((block, out_grad))
     other_grad = twin(late_grad)
     at2 = step(block, 2)
     at1 = step(block, 1)
@@ -510,10 +511,10 @@
         place, doc_lengths.reshape(1, -1), doc_full.reshape(1, -1), queries,
         own, at1, at2, twin(at1[PAIR:]), twin(at2[PAIR:]),
     )
-    at4, top = lax.optimization_barrier((at4, top))
-    at3, twin4 = lax.optimization_barrier((at3, twin(at4[PAIR:])))
+    at4, at3, top = lax.optimization_barrier((at4, at3, top))
+    twin3, twin4 = twin(at3[PAIR:]), twin(at4[PAIR:])
     attn, do_st, qs_st, dos_st, p, stats, dq_far, ahead, across = middle(
-        place, ranges, limit, q_st, win, s, top, at3, at4, twin(at3[PAIR:]), twin4, attn_grad
+        place, ranges, limit, q_st, win, s, top, at3, at4, twin3, twin4, attn_grad
     )
     away = project(1 - core, attn, out_weight)
     across, away = lax.optimization_barrier((twin(across), away))
@@ -529,9 +530,8 @@
     far = step(far_out, 2)
     near = step(near_out, 1)
     layer_out = project(core, attn, out_weight, twin(away))
-    near, layer_out = lax.optimization_barrier((near, layer_out))
-    far, near_twin = lax.optimization_barrier((far, twin(near[PAIR:])))
-    key_grad, value_grad = last_sum(mid, near, far, near_twin, twin(far[PAIR:]))
+    far, near, layer_out = lax.optimization_barrier((far, near, layer_out))
+    key_grad, value_grad = last_sum(mid, near, far, twin(near[PAIR:]), twin(far[PAIR:]))
     return (layer_out, query_grad, key_grad, value_grad)
 
 

time: 87.4 us -> 75.7 us (0.87)
  the two profiles are of different devices: /device:TPU:49 before, /device:TPU:25 now
where the time goes in v5:
time: 75.7 us; the launch traced here: 75.5 us
  starting transfers between devices  33.4 us (44%)
  waiting for transfers between devices  20.9 us (28%)
  Pallas kernels  15.1 us (20%)
  local copies, waits for them, and re-layouts  5.17 us (7%)
  between operations  0.78 us (1%)
    ppermute x8, starting transfers between devices, step(): return lax.ppermute(block, ('cp', 'hd'), ways)  25.4 us
    ppermute x8, waiting for transfers between devices, step(): return lax.ppermute(block, ('cp', 'hd'), ways)  16.6 us
    ppermute x12, starting transfers between devices, twin(): return lax.ppermute(block, 'hd', [(0, 1), (1, 0)])  8 us
    pallas_call x1, Pallas kernels, near_back(): pl.pallas_call(near_back_kernel, out_shape=(bf16(ROWS, GROUPS * DH), bf16...  5.45 us
    unnamed x16, local copies, waits for them, and re-layouts  5.11 us
    ppermute x12, waiting for transfers between devices, twin(): return lax.ppermute(block, 'hd', [(0, 1), (1, 0)])  4.22 us
    pallas_call x2, Pallas kernels, project(): pl.pallas_call(body, out_shape=bf16(rows, cols), in_specs=[SMEM, VMEM, VM...  2.49 us
    pallas_call x1, Pallas kernels, near_scores(): pl.pallas_call(near_scores_kernel, out_shape=(i32(4), i32(8, CHUNK), bf16...  2.45 us
  transfers between devices with their start and end apart: 20, of which 14 were waited for; matrix products, arithmetic and copies ran while one was open for 0% of the time, Pallas kernels for 16%

profile of v5, /device:TPU:25, one launch (start us, length us, event | category | flops | bytes accessed | tf_op | source)
XLA Modules:
  0.0 75.5 jit_solution(6249788678024306900)
XLA Ops:
  0.6 0.8 %collective-permute-start = (bf16[256,128]{1,0:T(8,128)(2,1)}, bf16[256,128]{1,0:T(8,128)(2,1)S(1)}, u32[]{:S(2)}, u32[]{:S(2)}) collective-permute-start(bf16[256,128]{1,0:T(8,128)(2,1)} %refs_0_.1), channel_id=1, source_target_pairs={{0,1},{1,0},{2,3},{3,2},{4,5},{5,4},{6,7},{7,6},{8,9},{9,8},{10,11... | collective-permute-start | bytes 196616 | tf_op jit(solution)/shard_map/ppermute | solution.py:497
  1.4 0.1 collective-permute-start.1
  1.5 0.8 %copy-done.3 = bf16[256,128]{1,0:T(8,128)(2,1)S(1)} copy-done((bf16[256,128]{1,0:T(8,128)(2,1)S(1)}, bf16[256,128]{1,0:T(8,128)(2,1)}, u32[]{:S(2)}) %copy-start.3) | copy-done | bytes 65560
  2.3 0.8 %copy-done.4 = bf16[256,128]{1,0:T(8,128)(2,1)S(1)} copy-done((bf16[256,128]{1,0:T(8,128)(2,1)S(1)}, bf16[256,128]{1,0:T(8,128)(2,1)}, u32[]{:S(2)}) %copy-start.4) | copy-done | bytes 65560
  3.2 0.2 shard_map.102.refs_0_.own_ref
  3.4 0.0 collective-permute-done.1.refs_2_
  3.4 0.5 collective-permute-start.4
  3.9 8.4 %collective-permute-start.3 = (bf16[1024,128]{1,0:T(8,128)(2,1)S(1)}, bf16[1024,128]{1,0:T(8,128)(2,1)S(1)}, u32[]{:S(2)}, u32[]{:S(2)}) collective-permute-start(bf16[1024,128]{1,0:T(8,128)(2,1)S(1)} %shard_map.103), channel_id=1, source_target_pairs={{0,4},{2,6},{4,8},{6,10},{8,12},{10,14},{12,16},{14,18},{16,20},{1... | collective-permute-start | bytes 786440 | tf_op jit(solution)/shard_map/ppermute | solution.py:494
  12.3 0.7 collective-permute-start.2
  13.0 2.2 %copy-done = bf16[4096,512]{1,0:T(8,128)(2,1)S(1)} copy-done((bf16[4096,512]{1,0:T(8,128)(2,1)S(1)}, bf16[4096,512]{1,0:T(8,128)(2,1)}, u32[]{:S(2)}) %copy-start) | copy-done | bytes 4194328
  15.2 1.2 %copy-done.2 = bf16[256,2048]{1,0:T(8,128)(2,1)S(1)} copy-done((bf16[256,2048]{1,0:T(8,128)(2,1)S(1)}, bf16[256,2048]{1,0:T(8,128)(2,1)}, u32[]{:S(2)}) %copy-start.2) | copy-done | bytes 1048600
  16.5 1.3 %shard_map.104.do_ref = bf16[256,512]{1,0:T(8,128)(2,1)S(1)} custom-call(s32[1]{0:T(128)} %bitcast.1.core_ref.half_ref, bf16[256,2048]{1,0:T(8,128)(2,1)S(1)} %copy-done.2, bf16[256,2048]{1,0:T(8,128)(2,1)S(1)} %collective-permute-done.4.other_ref, bf16[4096,512]{1,0:T(8,128)(2,1)S(1)} %copy-done), custom_call_target="tpu_custom_call" | custom-call | flops 1073741824 | bytes 6000000 | tf_op jit(solution)/shard_map/pallas_call | solution.py:453
  17.7 0.7 collective-permute-done.3.at2_ref
  18.4 7.1 %collective-permute-start.7 = (bf16[1024,128]{1,0:T(8,128)(2,1)S(1)}, bf16[1024,128]{1,0:T(8,128)(2,1)S(1)}, u32[]{:S(2)}, u32[]{:S(2)}) collective-permute-start(bf16[1024,128]{1,0:T(8,128)(2,1)S(1)} %collective-permute-done.3.at2_ref), channel_id=1, source_target_pairs={{0,4},{2,6},{4,8},{6,10},{8,12},{10,14},{12,16},{14,18},{16,20},{1... | collective-permute-start | bytes 786440 | tf_op jit(solution)/shard_map/ppermute | solution.py:494
  25.6 0.1 collective-permute-start.5
  25.7 0.6 collective-permute-start.6
  26.3 0.1 pad_add_fusion.place_ref
  26.4 0.7 collective-permute-done.5.twin1_ref
  27.0 0.2 collective-permute-done.6.twin2_ref
  27.3 2.5 %shard_map.105 = (s32[4]{0:T(128)S(1)}, s32[8,256]{1,0:T(8,128)S(1)}, bf16[1024,128]{1,0:T(8,128)(2,1)S(1)}, bf16[2560,128]{1,0:T(8,128)(2,1)S(1)}, f32[1280,1024]{1,0:T(8,128)S(1)}, /*index=5*/f32[8,1024]{1,0:T(8,128)S(1)}) custom-call(s32[2]{0:T(128)S(1)} %pad_add_fusion.place_ref, s32[1,64]{1,0:T(1,128)S(1)} %bitcast.4, s32[1,64]{1,0:T(1,128)S(1)} %bitcast.5, ...), custom_call_target="tpu_custom_call" | custom-call | flops 1000000000 | bytes 6000000 | tf_op jit(solution)/shard_map/pallas_call | solution.py:304
  29.7 0.0 copy-start.1
  29.7 1.8 %collective-permute-done.7.at4_ref = bf16[1024,128]{1,0:T(8,128)(2,1)S(1)} collective-permute-done((bf16[1024,128]{1,0:T(8,128)(2,1)S(1)}, bf16[1024,128]{1,0:T(8,128)(2,1)S(1)}, u32[]{:S(2)}, u32[]{:S(2)}) %collective-permute-start.7) | collective-permute-done | bytes 262176 | tf_op jit(solution)/shard_map/ppermute | solution.py:494
  31.6 2.8 %collective-permute-done.8.at3_ref = bf16[1024,128]{1,0:T(8,128)(2,1)S(1)} collective-permute-done((bf16[1024,128]{1,0:T(8,128)(2,1)S(1)}, bf16[1024,128]{1,0:T(8,128)(2,1)S(1)}, u32[]{:S(2)}, u32[]{:S(2)}) %collective-permute-start.8) | collective-permute-done | bytes 262176 | tf_op jit(solution)/shard_map/ppermute | solution.py:494
  34.4 1.3 %collective-permute-start.10 = (bf16[512,128]{1,0:T(8,128)(2,1)S(1)}, bf16[512,128]{1,0:T(8,128)(2,1)S(1)}, u32[]{:S(2)}, u32[]{:S(2)}) collective-permute-start(bf16[512,128]{1,0:T(8,128)(2,1)S(1)} %slice.21), channel_id=1, source_target_pairs={{0,1},{1,0},{2,3},{3,2},{4,5},{5,4},{6,7},{7,6},{8,9},{9,8},{10,11... | collective-permute-start | bytes 393224 | tf_op jit(solution)/shard_map/ppermute | solution.py:497
  35.7 0.1 collective-permute-start.9
  35.8 0.9 %collective-permute-done.10.twin4_ref = bf16[512,128]{1,0:T(8,128)(2,1)S(1)} collective-permute-done((bf16[512,128]{1,0:T(8,128)(2,1)S(1)}, bf16[512,128]{1,0:T(8,128)(2,1)S(1)}, u32[]{:S(2)}, u32[]{:S(2)}) %collective-permute-start.10) | collective-permute-done | bytes 131104 | tf_op jit(solution)/shard_map/ppermute | solution.py:497
  36.7 0.5 collective-permute-done.9.twin3_ref
  37.2 2.4 %shard_map.106 = (bf16[256,512]{1,0:T(8,128)(2,1)S(1)}, bf16[1024,128]{1,0:T(8,128)(2,1)S(1)}, bf16[1024,128]{1,0:T(8,128)(2,1)S(1)}, bf16[1024,128]{1,0:T(8,128...) custom-call(s32[2]{0:T(128)S(1)} %pad_add_fusion.place_ref, ...), custom_call_target="tpu_custom_call" | custom-call | flops 1000000000 | bytes 6000000 | tf_op jit(solution)/shard_map/pallas_call | solution.py:317
  39.6 0.2 collective-permute-start.11
  39.8 0.7 shard_map.107
  40.6 0.6 collective-permute-done.11.across_ref
  41.2 5.5 %collective-permute-start.12 = (bf16[1024,128]{1,0:T(8,128)(2,1)S(1)}, bf16[1024,128]{1,0:T(8,128)(2,1)S(1)}, u32[]{:S(2)}, u32[]{:S(2)}) collective-permute-start(bf16[1024,128]{1,0:T(8,128)(2,1)S(1)} %get-tuple-element.81), channel_id=1, source_target_pairs={{0,4},{2,6},{4,8},{6,10},{8,12},{10,14},{12,16},{14,18},{16,20},{1... | collective-permute-start | bytes 786440 | tf_op jit(solution)/shard_map/ppermute | solution.py:494
  46.7 5.5 %shard_map.109 = (bf16[256,512]{1,0:T(8,128)(2,1)}, bf16[1024,128]{1,0:T(8,128)(2,1)S(1)}, bf16[1024,128]{1,0:T(8,128)(2,1)S(1)}, bf16[512,128]{1,0:T(8,128)(2,1)S(1)}) custom-call(s32[2]{0:T(128)S(1)} %pad_add_fusion.place_ref, s32[4]{0:T(128)S(1)} %get-tuple-element.57.range_ref, bf16[2560,128]{1,0:T(8,128)(2,1)S(1)} %get-tuple-element.58.near_win.win, ...), custom_call_target="tpu_custom_call" | custom-call | flops 20000000000 | bytes 30000000 | tf_op jit(solution)/shard_map/pallas_call | solution.py:339
  52.1 0.7 collective-permute-done.12.refs_0_
  52.8 3.4 %collective-permute-done.13.refs_1_ = bf16[1024,128]{1,0:T(8,128)(2,1)S(1)} collective-permute-done((bf16[1024,128]{1,0:T(8,128)(2,1)S(1)}, bf16[1024,128]{1,0:T(8,128)(2,1)S(1)}, u32[]{:S(2)}, u32[]{:S(2)}) %collective-permute-start.13) | collective-permute-done | bytes 262176 | tf_op jit(solution)/shard_map/ppermute | solution.py:494
  56.2 0.1 shard_map.110.came_ref
  56.3 0.1 shard_map.111
  56.4 2.1 %collective-permute-start.17 = (bf16[256,2048]{1,0:T(8,128)(2,1)S(1)}, bf16[256,2048]{1,0:T(8,128)(2,1)S(1)}, u32[]{:S(2)}, u32[]{:S(2)}) collective-permute-start(bf16[256,2048]{1,0:T(8,128)(2,1)S(1)} %shard_map.107), channel_id=1, source_target_pairs={{0,1},{1,0},{2,3},{3,2},{4,5},{5,4},{6,7},{7,6},{8,9},{9,8},{10,11... | collective-permute-start | bytes 3145736 | tf_op jit(solution)/shard_map/ppermute | solution.py:497
  58.4 1.9 %collective-permute-start.15 = (bf16[1024,128]{1,0:T(8,128)(2,1)S(1)}, bf16[1024,128]{1,0:T(8,128)(2,1)S(1)}, u32[]{:S(2)}, u32[]{:S(2)}) collective-permute-start(bf16[1024,128]{1,0:T(8,128)(2,1)S(1)} %get-tuple-element.88), channel_id=1, source_target_pairs={{0,4},{2,6},{4,8},{6,10},{8,12},{10,14},{12,16},{14,18},{16,20},{1... | collective-permute-start | bytes 786440 | tf_op jit(solution)/shard_map/ppermute | solution.py:494
  60.3 1.9 %collective-permute-start.16 = (bf16[1024,128]{1,0:T(8,128)(2,1)S(1)}, bf16[1024,128]{1,0:T(8,128)(2,1)S(1)}, u32[]{:S(2)}, u32[]{:S(2)}) collective-permute-start(bf16[1024,128]{1,0:T(8,128)(2,1)S(1)} %get-tuple-element.89), channel_id=1, source_target_pairs={{0,2},{2,4},{4,6},{6,8},{8,10},{10,12},{12,14},{14,16},{16,18},{18... | collective-permute-start | bytes 786440 | tf_op jit(solution)/shard_map/ppermute | solution.py:494
  62.2 1.7 %shard_map.112 = bf16[256,2048]{1,0:T(8,128)(2,1)} custom-call(s32[1]{0:T(128)} %bitcast.1.core_ref.half_ref, bf16[256,512]{1,0:T(8,128)(2,1)S(1)} %get-tuple-element.73.a_ref, bf16[4096,512]{1,0:T(8,128)(2,1)S(1)} %copy-done.1, bf16[256,2048]{1,0:T(8,128)(2,1)S(1)} %collective-permute-done.17.refs_0_), custom_call_target="tpu_custom_call" | custom-call | flops 536870912 | bytes 4000000 | tf_op jit(solution)/shard_map/pallas_call | solution.py:474
  63.9 3.0 %collective-permute-done.15.refs_2_ = bf16[1024,128]{1,0:T(8,128)(2,1)S(1)} collective-permute-done((bf16[1024,128]{1,0:T(8,128)(2,1)S(1)}, bf16[1024,128]{1,0:T(8,128)(2,1)S(1)}, u32[]{:S(2)}, u32[]{:S(2)}) %collective-permute-start.15) | collective-permute-done | bytes 262176 | tf_op jit(solution)/shard_map/ppermute | solution.py:494
  66.9 4.3 %collective-permute-done.16.refs_1_ = bf16[1024,128]{1,0:T(8,128)(2,1)S(1)} collective-permute-done((bf16[1024,128]{1,0:T(8,128)(2,1)S(1)}, bf16[1024,128]{1,0:T(8,128)(2,1)S(1)}, u32[]{:S(2)}, u32[]{:S(2)}) %collective-permute-start.16) | collective-permute-done | bytes 262176 | tf_op jit(solution)/shard_map/ppermute | solution.py:494
  71.2 2.1 %collective-permute-start.18 = (bf16[512,128]{1,0:T(8,128)(2,1)S(1)}, bf16[512,128]{1,0:T(8,128)(2,1)S(1)}, u32[]{:S(2)}, u32[]{:S(2)}) collective-permute-start(bf16[512,128]{1,0:T(8,128)(2,1)S(1)} %slice.22), channel_id=1, source_target_pairs={{0,1},{1,0},{2,3},{3,2},{4,5},{5,4},{6,7},{7,6},{8,9},{9,8},{10,11... | collective-permute-start | bytes 393224 | tf_op jit(solution)/shard_map/ppermute | solution.py:497
  73.3 0.1 collective-permute-start.19
  73.4 0.9 %collective-permute-done.18.refs_3_ = bf16[512,128]{1,0:T(8,128)(2,1)S(1)} collective-permute-done((bf16[512,128]{1,0:T(8,128)(2,1)S(1)}, bf16[512,128]{1,0:T(8,128)(2,1)S(1)}, u32[]{:S(2)}, u32[]{:S(2)}) %collective-permute-start.18) | collective-permute-done | bytes 131104 | tf_op jit(solution)/shard_map/ppermute | solution.py:497
  74.3 0.5 collective-permute-done.19.refs_4_
  74.8 0.7 shard_map.113
  (27 shorter events, 0.2 us)
Async XLA Ops:
  0.6 2.7 %collective-permute-start = (bf16[256,128]{1,0:T(8,128)(2,1)}, bf16[256,128]{1,0:T(8,128)(2,1)S(1)}, u32[]{:S(2)}, u32[]{:S(2)}) collective-permute-start(bf16[256,128]{1,0:T(8,128)(2,1)} %refs_0_.1), channel_id=1, source_target_pairs={{0,1},{1,0},{2,3},{3,2},{4,5},{5,4},{6,7},{7,6},{8,9},{9,8},{10,11... | collective-permute-start | bytes 196616 | tf_op jit(solution)/shard_map/ppermute | solution.py:497
  1.4 2.0 %collective-permute-start.1 = (bf16[256,128]{1,0:T(8,128)(2,1)}, bf16[256,128]{1,0:T(8,128)(2,1)S(1)}, u32[]{:S(2)}, u32[]{:S(2)}) collective-permute-start(bf16[256,128]{1,0:T(8,128)(2,1)} %refs_1_.1), channel_id=1, source_target_pairs={{0,1},{1,0},{2,3},{3,2},{4,5},{5,4},{6,7},{7,6},{8,9},{9,8},{10,11... | collective-permute-start | bytes 196616 | tf_op jit(solution)/shard_map/ppermute | solution.py:497
  1.5 0.8 %copy-start.3 = (bf16[256,128]{1,0:T(8,128)(2,1)S(1)}, bf16[256,128]{1,0:T(8,128)(2,1)}, u32[]{:S(2)}) copy-start(bf16[256,128]{1,0:T(8,128)(2,1)} %refs_0_.1) | copy-start | bytes 196612
  2.3 0.8 %copy-start.4 = (bf16[256,128]{1,0:T(8,128)(2,1)S(1)}, bf16[256,128]{1,0:T(8,128)(2,1)}, u32[]{:S(2)}) copy-start(bf16[256,128]{1,0:T(8,128)(2,1)} %refs_1_.1) | copy-start | bytes 196612
  3.2 24.1 %copy-start.5 = (bf16[256,512]{1,0:T(8,128)(2,1)S(1)}, bf16[256,512]{1,0:T(8,128)(2,1)}, u32[]{:S(2)}) copy-start(bf16[256,512]{1,0:T(8,128)(2,1)} %q_ref.1) | copy-start | bytes 786436
  3.2 24.1 %copy-start.6 = (s32[64]{0:T(128)S(1)}, s32[64]{0:T(128)}, u32[]{:S(2)}) copy-start(s32[64]{0:T(128)} %param.11) | copy-start | bytes 772
  3.2 24.1 %copy-start.7 = (s32[64]{0:T(128)S(1)}, s32[64]{0:T(128)}, u32[]{:S(2)}) copy-start(s32[64]{0:T(128)} %param.12) | copy-start | bytes 772
  3.4 9.6 %collective-permute-start.4 = (bf16[256,2048]{1,0:T(8,128)(2,1)}, bf16[256,2048]{1,0:T(8,128)(2,1)S(1)}, u32[]{:S(2)}, u32[]{:S(2)}) collective-permute-start(bf16[256,2048]{1,0:T(8,128)(2,1)} %own_ref.1), channel_id=1, source_target_pairs={{0,1},{1,0},{2,3},{3,2},{4,5},{5,4},{6,7},{7,6},{8,9},{9,8},{10,11... | collective-permute-start | bytes 3145736 | tf_op jit(solution)/shard_map/ppermute | solution.py:497
  3.9 14.5 %collective-permute-start.3 = (bf16[1024,128]{1,0:T(8,128)(2,1)S(1)}, bf16[1024,128]{1,0:T(8,128)(2,1)S(1)}, u32[]{:S(2)}, u32[]{:S(2)}) collective-permute-start(bf16[1024,128]{1,0:T(8,128)(2,1)S(1)} %shard_map.103), channel_id=1, source_target_pairs={{0,4},{2,6},{4,8},{6,10},{8,12},{10,14},{12,16},{14,18},{16,20},{1... | collective-permute-start | bytes 786440 | tf_op jit(solution)/shard_map/ppermute | solution.py:494
  12.3 13.3 %collective-permute-start.2 = (bf16[1024,128]{1,0:T(8,128)(2,1)S(1)}, bf16[1024,128]{1,0:T(8,128)(2,1)S(1)}, u32[]{:S(2)}, u32[]{:S(2)}) collective-permute-start(bf16[1024,128]{1,0:T(8,128)(2,1)S(1)} %shard_map.103), channel_id=1, source_target_pairs={{0,2},{2,4},{4,6},{6,8},{8,10},{10,12},{12,14},{14,16},{16,18},{18... | collective-permute-start | bytes 786440 | tf_op jit(solution)/shard_map/ppermute | solution.py:494
  13.0 2.2 %copy-start = (bf16[4096,512]{1,0:T(8,128)(2,1)S(1)}, bf16[4096,512]{1,0:T(8,128)(2,1)}, u32[]{:S(2)}) copy-start(bf16[4096,512]{1,0:T(8,128)(2,1)} %w_ref.5) | copy-start | bytes 12582916
  15.2 1.2 %copy-start.2 = (bf16[256,2048]{1,0:T(8,128)(2,1)S(1)}, bf16[256,2048]{1,0:T(8,128)(2,1)}, u32[]{:S(2)}) copy-start(bf16[256,2048]{1,0:T(8,128)(2,1)} %own_ref.1) | copy-start | bytes 3145732
  18.4 13.1 %collective-permute-start.7 = (bf16[1024,128]{1,0:T(8,128)(2,1)S(1)}, bf16[1024,128]{1,0:T(8,128)(2,1)S(1)}, u32[]{:S(2)}, u32[]{:S(2)}) collective-permute-start(bf16[1024,128]{1,0:T(8,128)(2,1)S(1)} %collective-permute-done.3.at2_ref), channel_id=1, source_target_pairs={{0,4},{2,6},{4,8},{6,10},{8,12},{10,14},{12,16},{14,18},{16,20},{1... | collective-permute-start | bytes 786440 | tf_op jit(solution)/shard_map/ppermute | solution.py:494
  25.6 8.8 %collective-permute-start.8 = (bf16[1024,128]{1,0:T(8,128)(2,1)S(1)}, bf16[1024,128]{1,0:T(8,128)(2,1)S(1)}, u32[]{:S(2)}, u32[]{:S(2)}) collective-permute-start(bf16[1024,128]{1,0:T(8,128)(2,1)S(1)} %collective-permute-done.3.at2_ref), channel_id=1, source_target_pairs={{0,2},{2,4},{4,6},{6,8},{8,10},{10,12},{12,14},{14,16},{16,18},{18... | collective-permute-start | bytes 786440 | tf_op jit(solution)/shard_map/ppermute | solution.py:494
  25.6 1.4 %collective-permute-start.5 = (bf16[512,128]{1,0:T(8,128)(2,1)S(1)}, bf16[512,128]{1,0:T(8,128)(2,1)S(1)}, u32[]{:S(2)}, u32[]{:S(2)}) collective-permute-start(bf16[512,128]{1,0:T(8,128)(2,1)S(1)} %slice.24), channel_id=1, source_target_pairs={{0,1},{1,0},{2,3},{3,2},{4,5},{5,4},{6,7},{7,6},{8,9},{9,8},{10,11... | collective-permute-start | bytes 393224 | tf_op jit(solution)/shard_map/ppermute | solution.py:497
  25.7 1.6 %collective-permute-start.6 = (bf16[512,128]{1,0:T(8,128)(2,1)S(1)}, bf16[512,128]{1,0:T(8,128)(2,1)S(1)}, u32[]{:S(2)}, u32[]{:S(2)}) collective-permute-start(bf16[512,128]{1,0:T(8,128)(2,1)S(1)} %slice.19), channel_id=1, source_target_pairs={{0,1},{1,0},{2,3},{3,2},{4,5},{5,4},{6,7},{7,6},{8,9},{9,8},{10,11... | collective-permute-start | bytes 393224 | tf_op jit(solution)/shard_map/ppermute | solution.py:497
  29.7 10.1 %copy-start.1 = (bf16[4096,512]{1,0:T(8,128)(2,1)S(1)}, bf16[4096,512]{1,0:T(8,128)(2,1)}, u32[]{:S(2)}) copy-start(bf16[4096,512]{1,0:T(8,128)(2,1)} %w_ref.5) | copy-start | bytes 12582916
  34.4 2.3 %collective-permute-start.10 = (bf16[512,128]{1,0:T(8,128)(2,1)S(1)}, bf16[512,128]{1,0:T(8,128)(2,1)S(1)}, u32[]{:S(2)}, u32[]{:S(2)}) collective-permute-start(bf16[512,128]{1,0:T(8,128)(2,1)S(1)} %slice.21), channel_id=1, source_target_pairs={{0,1},{1,0},{2,3},{3,2},{4,5},{5,4},{6,7},{7,6},{8,9},{9,8},{10,11... | collective-permute-start | bytes 393224 | tf_op jit(solution)/shard_map/ppermute | solution.py:497
  35.7 1.4 %collective-permute-start.9 = (bf16[512,128]{1,0:T(8,128)(2,1)S(1)}, bf16[512,128]{1,0:T(8,128)(2,1)S(1)}, u32[]{:S(2)}, u32[]{:S(2)}) collective-permute-start(bf16[512,128]{1,0:T(8,128)(2,1)S(1)} %slice.20), channel_id=1, source_target_pairs={{0,1},{1,0},{2,3},{3,2},{4,5},{5,4},{6,7},{7,6},{8,9},{9,8},{10,11... | collective-permute-start | bytes 393224 | tf_op jit(solution)/shard_map/ppermute | solution.py:497
  39.6 1.6 %collective-permute-start.11 = (bf16[1024,128]{1,0:T(8,128)(2,1)S(1)}, bf16[1024,128]{1,0:T(8,128)(2,1)S(1)}, u32[]{:S(2)}, u32[]{:S(2)}) collective-permute-start(bf16[1024,128]{1,0:T(8,128)(2,1)S(1)} %get-tuple-element.72), channel_id=1, source_target_pairs={{0,1},{1,0},{2,3},{3,2},{4,5},{5,4},{6,7},{7,6},{8,9},{9,8},{10,11... | collective-permute-start | bytes 786440 | tf_op jit(solution)/shard_map/ppermute | solution.py:497
  41.2 11.6 %collective-permute-start.12 = (bf16[1024,128]{1,0:T(8,128)(2,1)S(1)}, bf16[1024,128]{1,0:T(8,128)(2,1)S(1)}, u32[]{:S(2)}, u32[]{:S(2)}) collective-permute-start(bf16[1024,128]{1,0:T(8,128)(2,1)S(1)} %get-tuple-element.81), channel_id=1, source_target_pairs={{0,4},{2,6},{4,8},{6,10},{8,12},{10,14},{12,16},{14,18},{16,20},{1... | collective-permute-start | bytes 786440 | tf_op jit(solution)/shard_map/ppermute | solution.py:494
  46.7 9.5 %collective-permute-start.13 = (bf16[1024,128]{1,0:T(8,128)(2,1)S(1)}, bf16[1024,128]{1,0:T(8,128)(2,1)S(1)}, u32[]{:S(2)}, u32[]{:S(2)}) collective-permute-start(bf16[1024,128]{1,0:T(8,128)(2,1)S(1)} %get-tuple-element.82), channel_id=1, source_target_pairs={{0,2},{2,4},{4,6},{6,8},{8,10},{10,12},{12,14},{14,16},{16,18},{18... | collective-permute-start | bytes 786440 | tf_op jit(solution)/shard_map/ppermute | solution.py:494
  52.1 4.1 %collective-permute-start.14 = (bf16[1024,128]{1,0:T(8,128)(2,1)S(1)}, bf16[1024,128]{1,0:T(8,128)(2,1)S(1)}, u32[]{:S(2)}, u32[]{:S(2)}) collective-permute-start(bf16[1024,128]{1,0:T(8,128)(2,1)S(1)} %get-tuple-element.83), channel_id=1, source_target_pairs={{0,1},{1,0},{2,3},{3,2},{4,5},{5,4},{6,7},{7,6},{8,9},{9,8},{10,11... | collective-permute-start | bytes 786440 | tf_op jit(solution)/shard_map/ppermute | solution.py:497
  56.4 5.8 %collective-permute-start.17 = (bf16[256,2048]{1,0:T(8,128)(2,1)S(1)}, bf16[256,2048]{1,0:T(8,128)(2,1)S(1)}, u32[]{:S(2)}, u32[]{:S(2)}) collective-permute-start(bf16[256,2048]{1,0:T(8,128)(2,1)S(1)} %shard_map.107), channel_id=1, source_target_pairs={{0,1},{1,0},{2,3},{3,2},{4,5},{5,4},{6,7},{7,6},{8,9},{9,8},{10,11... | collective-permute-start | bytes 3145736 | tf_op jit(solution)/shard_map/ppermute | solution.py:497
  58.4 8.5 %collective-permute-start.15 = (bf16[1024,128]{1,0:T(8,128)(2,1)S(1)}, bf16[1024,128]{1,0:T(8,128)(2,1)S(1)}, u32[]{:S(2)}, u32[]{:S(2)}) collective-permute-start(bf16[1024,128]{1,0:T(8,128)(2,1)S(1)} %get-tuple-element.88), channel_id=1, source_target_pairs={{0,4},{2,6},{4,8},{6,10},{8,12},{10,14},{12,16},{14,18},{16,20},{1... | collective-permute-start | bytes 786440 | tf_op jit(solution)/shard_map/ppermute | solution.py:494
  60.3 10.9 %collective-permute-start.16 = (bf16[1024,128]{1,0:T(8,128)(2,1)S(1)}, bf16[1024,128]{1,0:T(8,128)(2,1)S(1)}, u32[]{:S(2)}, u32[]{:S(2)}) collective-permute-start(bf16[1024,128]{1,0:T(8,128)(2,1)S(1)} %get-tuple-element.89), channel_id=1, source_target_pairs={{0,2},{2,4},{4,6},{6,8},{8,10},{10,12},{12,14},{14,16},{16,18},{18... | collective-permute-start | bytes 786440 | tf_op jit(solution)/shard_map/ppermute | solution.py:494
  71.2 3.1 %collective-permute-start.18 = (bf16[512,128]{1,0:T(8,128)(2,1)S(1)}, bf16[512,128]{1,0:T(8,128)(2,1)S(1)}, u32[]{:S(2)}, u32[]{:S(2)}) collective-permute-start(bf16[512,128]{1,0:T(8,128)(2,1)S(1)} %slice.22), channel_id=1, source_target_pairs={{0,1},{1,0},{2,3},{3,2},{4,5},{5,4},{6,7},{7,6},{8,9},{9,8},{10,11... | collective-permute-start | bytes 393224 | tf_op jit(solution)/shard_map/ppermute | solution.py:497
  73.3 1.4 %collective-permute-start.19 = (bf16[512,128]{1,0:T(8,128)(2,1)S(1)}, bf16[512,128]{1,0:T(8,128)(2,1)S(1)}, u32[]{:S(2)}, u32[]{:S(2)}) collective-permute-start(bf16[512,128]{1,0:T(8,128)(2,1)S(1)} %slice.23), channel_id=1, source_target_pairs={{0,1},{1,0},{2,3},{3,2},{4,5},{5,4},{6,7},{7,6},{8,9},{9,8},{10,11... | collective-permute-start | bytes 393224 | tf_op jit(solution)/shard_map/ppermute | solution.py:497

commit v6 on v5

--- a/solution.py
+++ b/solution.py
@@ -161,9 +161,18 @@
     out_win[vals_of(at), :] = dot_nn(p_ref[rows_of(at), cols], dos_st[cols, :]).astype(jnp.bfloat16)
 
 
+def scaled_copies(q_st, do_st, inv_row, qs_st, dos_st):
+    for n in range(SUBS * GROUPS):
+        cols = slice(n * SUB, (n + 1) * SUB)
+        inv_col = jnp.broadcast_to(inv_row[:, cols], (DH, SUB)).T
+        dos_st[cols, :] = (do_st[cols, :].astype(jnp.float32) * inv_col).astype(jnp.bfloat16)
+        qs_st[cols, :] = (q_st[cols, :].astype(jnp.float32) * (inv_col * SCALE)).astype(jnp.bfloat16)
+
+
 def near_scores_kernel(
     place_ref, len_ref, full_ref, q_ref, own_ref, at1_ref, at2_ref, twin1_ref, twin2_ref,
-    range_ref, limit_ref, q_st, win, s_ref, top_ref,
+    range_ref, limit_ref, q_st, win, p_ref, acc, top_ref,
+    s_ref,
 ):
     way = 1 - 2 * place_ref[1]
     base = place_ref[0] - SPAN
@@ -190,14 +199,21 @@
 
     none = jnp.full((1, CHUNK), NEG, jnp.float32)
     top = every_near(range_ref, scores, (none,) * (SUBS * CHUNKS))
+    acc[...] = jnp.zeros_like(acc)
+
+    def weigh(subs):
+        return lambda at, total: weigh_block(subs, at, win, s_ref, p_ref, acc, top, total)
+
+    total = every_near(range_ref, weigh, (jnp.zeros((1, CHUNK), jnp.float32),) * (SUBS * CHUNKS))
     for c in range(SUBS * CHUNKS):
         top_ref[0:1, chunk_cols(c)] = top[c]
+        top_ref[1:2, chunk_cols(c)] = total[c]
 
 
 def middle_kernel(
-    place_ref, range_ref, limit_ref, q_st, near_win, near_s, top_ref, at3_ref, at4_ref, twin3_ref, twin4_ref, do_ref,
-    attn_ref, do_st, qs_st, dos_st, near_p, stats_ref, dq_acc, ahead_ref, across_ref,
-    win, out_win, s_scr, p_scr, ds_scr, acc,
+    place_ref, range_ref, limit_ref, q_st, near_acc, top_ref, at3_ref, at4_ref, twin3_ref, twin4_ref, do_ref,
+    attn_ref, do_st, stats_ref, dq_acc, ahead_ref, across_ref,
+    win, out_win, s_scr, p_scr, ds_scr, acc, qs_st, dos_st,
 ):
     core = place_ref[1]
     base = place_ref[0] - SPAN
@@ -207,9 +223,6 @@
 
     for n, ref in enumerate((at4_ref, at3_ref, twin3_ref, twin4_ref)):
         win[pair_of(slot(n)), :] = ref[0:PAIR, :]
-    for sub in range(SUBS):
-        for h in range(GROUPS):
-            do_st[staged(sub, h), :] = do_ref[sub_rows(sub), head_cols(h)]
 
     def scores(subs):
         def body(at, top):
@@ -218,33 +231,35 @@
 
         return body
 
-    top = tuple(top_ref[0:1, chunk_cols(c)] for c in range(SUBS * CHUNKS))
-    top = every_far(range_ref, scores, top)
-    acc[...] = jnp.zeros_like(acc)
+    near_top = tuple(top_ref[0:1, chunk_cols(c)] for c in range(SUBS * CHUNKS))
+    top = every_far(range_ref, scores, near_top)
+    share = [jnp.exp2(near_top[c] - top[c]) for c in range(SUBS * CHUNKS)]
+    for c in range(SUBS * CHUNKS):
+        acc[:, chunk_cols(c)] = near_acc[:, chunk_cols(c)] * share[c]
 
     def weigh(subs):
-        return lambda at, total: weigh_block(subs, at, near_win, near_s, near_p, acc, top, total)
-
-    def weigh_far(subs):
         return lambda at, total: weigh_block(subs, at, win, s_scr, p_scr, acc, top, total)
 
-    total = every_near(range_ref, weigh, (jnp.zeros((1, CHUNK), jnp.float32),) * (SUBS * CHUNKS))
-    total = every_far(range_ref, weigh_far, total)
+    total = tuple(top_ref[1:2, chunk_cols(c)] * share[c] for c in range(SUBS * CHUNKS))
+    total = every_far(range_ref, weigh, total)
     for c in range(SUBS * CHUNKS):
-        stats_ref[0:1, chunk_cols(c)] = 1.0 / total[c]
+        inv = 1.0 / total[c]
+        stats_ref[0:1, chunk_cols(c)] = inv
+        stats_ref[2:3, chunk_cols(c)] = inv * share[c]
     for sub in range(SUBS):
         for h in range(GROUPS):
             cols = staged(sub, h)
-            inv = stats_ref[0:1, cols]
-            attn_t = (acc[:, cols] * inv).astype(jnp.bfloat16).astype(jnp.float32)
+            attn_t = (acc[:, cols] * stats_ref[0:1, cols]).astype(jnp.bfloat16).astype(jnp.float32)
             attn_ref[sub_rows(sub), head_cols(h)] = attn_t.T.astype(jnp.bfloat16)
-            grad = do_st[cols, :].astype(jnp.float32)
-            stats_ref[1:2, cols] = jnp.sum(attn_t * grad.T, axis=0, keepdims=True)
-            inv_col = jnp.broadcast_to(inv, (DH, SUB)).T
-            dos_st[cols, :] = (grad * inv_col).astype(jnp.bfloat16)
-            qs_st[cols, :] = (q_st[cols, :].astype(jnp.float32) * (inv_col * SCALE)).astype(jnp.bfloat16)
+            grad = do_ref[sub_rows(sub), head_cols(h)]
+            do_st[cols, :] = grad
+            stats_ref[1:2, cols] = jnp.sum(attn_t * grad.astype(jnp.float32).T, axis=0, keepdims=True)
     dq_acc[...] = jnp.zeros_like(dq_acc)
     out_win[...] = jnp.zeros_like(out_win)
+
+    @pl.when((range_ref[0] < SIDE) | (range_ref[3] > SIDE + NEAR))
+    def _():
+        scaled_copies(q_st, do_st, stats_ref[0:1, :], qs_st, dos_st)
 
     def back(subs):
         def body(at, carry):
@@ -260,12 +275,13 @@
 
 
 def near_back_kernel(
-    place_ref, range_ref, win, p_ref, do_st, qs_st, dos_st, stats_ref, dq_far,
+    place_ref, range_ref, win, p_ref, q_st, do_st, stats_ref, dq_far,
     dq_ref, ahead_ref, across_ref, mid_ref,
-    out_win, ds_scr, dq_acc,
+    out_win, ds_scr, dq_acc, qs_st, dos_st,
 ):
     way = 1 - 2 * place_ref[1]
-    dq_acc[...] = dq_far[...]
+    dq_acc[...] = jnp.zeros_like(dq_acc)
+    scaled_copies(q_st, do_st, stats_ref[2:3, :], qs_st, dos_st)
     out_win[...] = jnp.zeros_like(out_win)
 
     def back(subs):
@@ -284,7 +300,7 @@
     for sub in range(SUBS):
         for h in range(GROUPS):
             cols = staged(sub, h)
-            dq = dq_acc[:, cols] * (stats_ref[0:1, cols] * SCALE)
+            dq = dq_acc[:, cols] * (stats_ref[2:3, cols] * SCALE) + dq_far[:, cols] * (stats_ref[0:1, cols] * SCALE)
             dq_ref[sub_rows(sub), head_cols(h)] = dq.T.astype(jnp.bfloat16)
 
 
@@ -304,11 +320,13 @@
     return pl.pallas_call(
         near_scores_kernel,
         out_shape=(
-            i32(4), i32(8, CHUNK), bf16(STACK, DH), bf16(NEAR * PAIR, DH), f32(NEAR * ROWS, STACK), f32(8, STACK),
+            i32(4), i32(8, CHUNK), bf16(STACK, DH), bf16(NEAR * PAIR, DH), bf16(NEAR * ROWS, STACK), f32(DH, STACK),
+            f32(8, STACK),
         ),
         in_specs=[SMEM] + [VMEM] * 8,
-        out_specs=(SMEM,) + (VMEM,) * 5,
-        compiler_params=pltpu.CompilerParams(vmem_limit_bytes=16 * 1024 * 1024),
+        out_specs=(SMEM,) + (VMEM,) * 6,
+        scratch_shapes=[pltpu.VMEM((NEAR * ROWS, STACK), jnp.float32)],
+        compiler_params=pltpu.CompilerParams(vmem_limit_bytes=18 * 1024 * 1024),
         cost_estimate=pl.CostEstimate(flops=10**9, bytes_accessed=6 * 10**6, transcendentals=0),
     )(*args)
 
@@ -317,11 +335,11 @@
     return pl.pallas_call(
         middle_kernel,
         out_shape=(
-            bf16(ROWS, GROUPS * DH), bf16(STACK, DH), bf16(STACK, DH), bf16(STACK, DH), bf16(NEAR * ROWS, STACK),
-            f32(8, STACK), f32(DH, STACK), bf16(SIDE * PAIR, DH), bf16(SIDE * PAIR, DH),
+            bf16(ROWS, GROUPS * DH), bf16(STACK, DH), f32(8, STACK), f32(DH, STACK),
+            bf16(SIDE * PAIR, DH), bf16(SIDE * PAIR, DH),
         ),
-        in_specs=[SMEM, SMEM] + [VMEM] * 10,
-        out_specs=(VMEM,) * 9,
+        in_specs=[SMEM, SMEM] + [VMEM] * 9,
+        out_specs=(VMEM,) * 6,
         scratch_shapes=[
             pltpu.VMEM((FAR * PAIR, DH), jnp.bfloat16),
             pltpu.VMEM((FAR * PAIR, DH), jnp.bfloat16),
@@ -329,8 +347,10 @@
             pltpu.VMEM((FAR * ROWS, STACK), jnp.bfloat16),
             pltpu.VMEM((ROWS, STACK), jnp.bfloat16),
             pltpu.VMEM((DH, STACK), jnp.float32),
+            pltpu.VMEM((STACK, DH), jnp.bfloat16),
+            pltpu.VMEM((STACK, DH), jnp.bfloat16),
         ],
-        compiler_params=pltpu.CompilerParams(vmem_limit_bytes=26 * 1024 * 1024),
+        compiler_params=pltpu.CompilerParams(vmem_limit_bytes=20 * 1024 * 1024),
         cost_estimate=pl.CostEstimate(flops=10**9, bytes_accessed=6 * 10**6, transcendentals=10**6),
     )(*args)
 
@@ -339,12 +359,14 @@
     return pl.pallas_call(
         near_back_kernel,
         out_shape=(bf16(ROWS, GROUPS * DH), bf16(REACH * PAIR, DH), bf16(REACH * PAIR, DH), bf16(PAIR, DH)),
-        in_specs=[SMEM, SMEM] + [VMEM] * 7,
+        in_specs=[SMEM, SMEM] + [VMEM] * 6,
         out_specs=(VMEM,) * 4,
         scratch_shapes=[
             pltpu.VMEM((NEAR * PAIR, DH), jnp.bfloat16),
             pltpu.VMEM((ROWS, STACK), jnp.bfloat16),
             pltpu.VMEM((DH, STACK), jnp.float32),
+            pltpu.VMEM((STACK, DH), jnp.bfloat16),
+            pltpu.VMEM((STACK, DH), jnp.bfloat16),
         ],
         compiler_params=pltpu.CompilerParams(vmem_limit_bytes=16 * 1024 * 1024),
         cost_estimate=pl.CostEstimate(flops=2 * 10**10, bytes_accessed=3 * 10**7, transcendentals=0),
@@ -507,14 +529,14 @@
     at2, attn_grad = lax.optimization_barrier((at2, attn_grad))
     at4 = step(at2, 2)
     at3 = step(at2, 1)
-    ranges, limit, q_st, win, s, top = near_scores(
+    ranges, limit, q_st, win, p, near_acc, top = near_scores(
         place, doc_lengths.reshape(1, -1), doc_full.reshape(1, -1), queries,
         own, at1, at2, twin(at1[PAIR:]), twin(at2[PAIR:]),
     )
     at4, at3, top = lax.optimization_barrier((at4, at3, top))
     twin3, twin4 = twin(at3[PAIR:]), twin(at4[PAIR:])
-    attn, do_st, qs_st, dos_st, p, stats, dq_far, ahead, across = middle(
-        place, ranges, limit, q_st, win, s, top, at3, at4, twin3, twin4, attn_grad
+    attn, do_st, stats, dq_far, ahead, across = middle(
+        place, ranges, limit, q_st, near_acc, top, at3, at4, twin3, twin4, attn_grad
     )
     away = project(1 - core, attn, out_weight)
     across, away = lax.optimization_barrier((twin(across), away))
@@ -522,7 +544,7 @@
     out4, out3, stats = lax.optimization_barrier((out4, out3, stats))
     in4 = step(out4, 2)
     in3 = step(out3, 1)
-    query_grad, ahead, across, mid = near_back(place, ranges, win, p, do_st, qs_st, dos_st, stats, dq_far)
+    query_grad, ahead, across, mid = near_back(place, ranges, win, p, q_st, do_st, stats, dq_far)
     came = summed(in4, in3)
     came, across = lax.optimization_barrier((came, twin(across)))
     far_out, near_out = far_and_near(ahead, across, came)

time: 75.7 us -> 75.4 us (level)
  the two profiles are of different devices: /device:TPU:25 before, /device:TPU:9 now
where the time goes in v6:
time: 75.4 us; the launch traced here: 74.5 us
  starting transfers between devices  31.6 us (42%)
  waiting for transfers between devices  20.6 us (27%)
  Pallas kernels  16.3 us (22%)
  local copies, waits for them, and re-layouts  5.16 us (7%)
  between operations  0.78 us (1%)
    ppermute x8, starting transfers between devices, step(): return lax.ppermute(block, ('cp', 'hd'), ways)  23.1 us
    ppermute x8, waiting for transfers between devices, step(): return lax.ppermute(block, ('cp', 'hd'), ways)  16.4 us
    ppermute x12, starting transfers between devices, twin(): return lax.ppermute(block, 'hd', [(0, 1), (1, 0)])  8.45 us
    unnamed x16, local copies, waits for them, and re-layouts  5.11 us
    pallas_call x1, Pallas kernels, near_back(): pl.pallas_call(near_back_kernel, out_shape=(bf16(ROWS, GROUPS * DH), bf16...  4.48 us
    ppermute x12, waiting for transfers between devices, twin(): return lax.ppermute(block, 'hd', [(0, 1), (1, 0)])  4.21 us
    pallas_call x1, Pallas kernels, middle(): pl.pallas_call(middle_kernel, out_shape=(bf16(ROWS, GROUPS * DH), bf16(ST...  3.84 us
    pallas_call x1, Pallas kernels, near_scores(): pl.pallas_call(near_scores_kernel, out_shape=(i32(4), i32(8, CHUNK), bf16...  3.14 us
  transfers between devices with their start and end apart: 20, of which 13 were waited for; matrix products, arithmetic and copies ran while one was open for 0% of the time, Pallas kernels for 16%

profile of v6, /device:TPU:9, one launch (start us, length us, event | category | flops | bytes accessed | tf_op | source)
XLA Modules:
  0.0 74.5 jit_solution(11659844156438345348)
XLA Ops:
  0.6 0.8 %collective-permute-start = (bf16[256,128]{1,0:T(8,128)(2,1)}, bf16[256,128]{1,0:T(8,128)(2,1)S(1)}, u32[]{:S(2)}, u32[]{:S(2)}) collective-permute-start(bf16[256,128]{1,0:T(8,128)(2,1)} %refs_0_.1), channel_id=1, source_target_pairs={{0,1},{1,0},{2,3},{3,2},{4,5},{5,4},{6,7},{7,6},{8,9},{9,8},{10,11... | collective-permute-start | bytes 196616 | tf_op jit(solution)/shard_map/ppermute | solution.py:519
  1.4 0.1 collective-permute-start.1
  1.5 0.8 %copy-done.3 = bf16[256,128]{1,0:T(8,128)(2,1)S(1)} copy-done((bf16[256,128]{1,0:T(8,128)(2,1)S(1)}, bf16[256,128]{1,0:T(8,128)(2,1)}, u32[]{:S(2)}) %copy-start.3) | copy-done | bytes 65560
  2.3 0.8 %copy-done.4 = bf16[256,128]{1,0:T(8,128)(2,1)S(1)} copy-done((bf16[256,128]{1,0:T(8,128)(2,1)S(1)}, bf16[256,128]{1,0:T(8,128)(2,1)}, u32[]{:S(2)}) %copy-start.4) | copy-done | bytes 65560
  3.2 0.2 shard_map.102.refs_0_.own_ref
  3.4 0.0 collective-permute-done.1.refs_2_
  3.4 0.5 collective-permute-start.4
  3.9 8.1 %collective-permute-start.3 = (bf16[1024,128]{1,0:T(8,128)(2,1)S(1)}, bf16[1024,128]{1,0:T(8,128)(2,1)S(1)}, u32[]{:S(2)}, u32[]{:S(2)}) collective-permute-start(bf16[1024,128]{1,0:T(8,128)(2,1)S(1)} %shard_map.103), channel_id=1, source_target_pairs={{0,4},{2,6},{4,8},{6,10},{8,12},{10,14},{12,16},{14,18},{16,20},{1... | collective-permute-start | bytes 786440 | tf_op jit(solution)/shard_map/ppermute | solution.py:516
  12.0 0.7 collective-permute-start.2
  12.7 0.0 collective-permute-done.4.other_ref
  12.8 2.2 %copy-done = bf16[4096,512]{1,0:T(8,128)(2,1)S(1)} copy-done((bf16[4096,512]{1,0:T(8,128)(2,1)S(1)}, bf16[4096,512]{1,0:T(8,128)(2,1)}, u32[]{:S(2)}) %copy-start) | copy-done | bytes 4194328
  14.9 1.2 %copy-done.2 = bf16[256,2048]{1,0:T(8,128)(2,1)S(1)} copy-done((bf16[256,2048]{1,0:T(8,128)(2,1)S(1)}, bf16[256,2048]{1,0:T(8,128)(2,1)}, u32[]{:S(2)}) %copy-start.2) | copy-done | bytes 1048600
  16.2 1.3 %shard_map.104.do_ref = bf16[256,512]{1,0:T(8,128)(2,1)S(1)} custom-call(s32[1]{0:T(128)} %bitcast.1.core_ref.half_ref, bf16[256,2048]{1,0:T(8,128)(2,1)S(1)} %copy-done.2, bf16[256,2048]{1,0:T(8,128)(2,1)S(1)} %collective-permute-done.4.other_ref, bf16[4096,512]{1,0:T(8,128)(2,1)S(1)} %copy-done), custom_call_target="tpu_custom_call" | custom-call | flops 1073741824 | bytes 6000000 | tf_op jit(solution)/shard_map/pallas_call | solution.py:475
  17.4 0.7 collective-permute-done.3.at2_ref
  18.1 7.1 %collective-permute-start.7 = (bf16[1024,128]{1,0:T(8,128)(2,1)S(1)}, bf16[1024,128]{1,0:T(8,128)(2,1)S(1)}, u32[]{:S(2)}, u32[]{:S(2)}) collective-permute-start(bf16[1024,128]{1,0:T(8,128)(2,1)S(1)} %collective-permute-done.3.at2_ref), channel_id=1, source_target_pairs={{0,4},{2,6},{4,8},{6,10},{8,12},{10,14},{12,16},{14,18},{16,20},{1... | collective-permute-start | bytes 786440 | tf_op jit(solution)/shard_map/ppermute | solution.py:516
  25.3 0.1 collective-permute-start.5
  25.4 0.6 collective-permute-start.6
  26.0 0.1 pad_add_fusion.place_ref
  26.1 0.7 collective-permute-done.5.twin1_ref
  26.7 0.2 collective-permute-done.6.twin2_ref
  27.0 3.1 %shard_map.105 = (s32[4]{0:T(128)S(1)}, s32[8,256]{1,0:T(8,128)S(1)}, bf16[1024,128]{1,0:T(8,128)(2,1)S(1)}, bf16[2560,128]{1,0:T(8,128)(2,1)S(1)}, bf16[1280,10...) custom-call(s32[2]{0:T(128)S(1)} %pad_add_fusion.place_ref, s32[1,64]{1,0:T(1,128)S(1)} %bitcast.4, ...), custom_call_target="tpu_custom_call" | custom-call | flops 1000000000 | bytes 6000000 | tf_op jit(solution)/shard_map/pallas_call | solution.py:320
  30.1 1.2 %collective-permute-done.7.at4_ref = bf16[1024,128]{1,0:T(8,128)(2,1)S(1)} collective-permute-done((bf16[1024,128]{1,0:T(8,128)(2,1)S(1)}, bf16[1024,128]{1,0:T(8,128)(2,1)S(1)}, u32[]{:S(2)}, u32[]{:S(2)}) %collective-permute-start.7) | collective-permute-done | bytes 262176 | tf_op jit(solution)/shard_map/ppermute | solution.py:516
  31.3 2.8 %collective-permute-done.8.at3_ref = bf16[1024,128]{1,0:T(8,128)(2,1)S(1)} collective-permute-done((bf16[1024,128]{1,0:T(8,128)(2,1)S(1)}, bf16[1024,128]{1,0:T(8,128)(2,1)S(1)}, u32[]{:S(2)}, u32[]{:S(2)}) %collective-permute-start.8) | collective-permute-done | bytes 262176 | tf_op jit(solution)/shard_map/ppermute | solution.py:516
  34.1 1.3 %collective-permute-start.10 = (bf16[512,128]{1,0:T(8,128)(2,1)S(1)}, bf16[512,128]{1,0:T(8,128)(2,1)S(1)}, u32[]{:S(2)}, u32[]{:S(2)}) collective-permute-start(bf16[512,128]{1,0:T(8,128)(2,1)S(1)} %slice.21), channel_id=1, source_target_pairs={{0,1},{1,0},{2,3},{3,2},{4,5},{5,4},{6,7},{7,6},{8,9},{9,8},{10,11... | collective-permute-start | bytes 393224 | tf_op jit(solution)/shard_map/ppermute | solution.py:519
  35.4 0.1 collective-permute-start.9
  35.5 0.9 %collective-permute-done.10.twin4_ref = bf16[512,128]{1,0:T(8,128)(2,1)S(1)} collective-permute-done((bf16[512,128]{1,0:T(8,128)(2,1)S(1)}, bf16[512,128]{1,0:T(8,128)(2,1)S(1)}, u32[]{:S(2)}, u32[]{:S(2)}) %collective-permute-start.10) | collective-permute-done | bytes 131104 | tf_op jit(solution)/shard_map/ppermute | solution.py:519
  36.4 0.5 collective-permute-done.9.twin3_ref
  36.9 3.8 %shard_map.106 = (bf16[256,512]{1,0:T(8,128)(2,1)S(1)}, bf16[1024,128]{1,0:T(8,128)(2,1)S(1)}, f32[8,1024]{1,0:T(8,128)S(1)}, f32[128,1024]{1,0:T(8,128)S(1)}, b...) custom-call(s32[2]{0:T(128)S(1)} %pad_add_fusion.place_ref, s32[4]{0:T(128)S(1)} %get-tuple-element.55.range_ref, ...), custom_call_target="tpu_custom_call" | custom-call | flops 1000000000 | bytes 6000000 | tf_op jit(solution)/shard_map/pallas_call | solution.py:335
  40.7 0.2 collective-permute-start.11
  41.0 0.7 shard_map.107
  41.7 0.6 collective-permute-done.11.across_ref
  42.4 0.6 collective-permute-start.12
  43.0 4.1 %collective-permute-start.13 = (bf16[1024,128]{1,0:T(8,128)(2,1)S(1)}, bf16[1024,128]{1,0:T(8,128)(2,1)S(1)}, u32[]{:S(2)}, u32[]{:S(2)}) collective-permute-start(bf16[1024,128]{1,0:T(8,128)(2,1)S(1)} %get-tuple-element.78), channel_id=1, source_target_pairs={{0,2},{2,4},{4,6},{6,8},{8,10},{10,12},{12,14},{14,16},{16,18},{18... | collective-permute-start | bytes 786440 | tf_op jit(solution)/shard_map/ppermute | solution.py:516
  47.1 4.5 %shard_map.109 = (bf16[256,512]{1,0:T(8,128)(2,1)}, bf16[1024,128]{1,0:T(8,128)(2,1)S(1)}, bf16[1024,128]{1,0:T(8,128)(2,1)S(1)}, bf16[512,128]{1,0:T(8,128)(2,1)S(1)}) custom-call(s32[2]{0:T(128)S(1)} %pad_add_fusion.place_ref, s32[4]{0:T(128)S(1)} %get-tuple-element.55.range_ref, bf16[2560,128]{1,0:T(8,128)(2,1)S(1)} %get-tuple-element.56.win, ...), custom_call_target="tpu_custom_call" | custom-call | flops 20000000000 | bytes 30000000 | tf_op jit(solution)/shard_map/pallas_call | solution.py:359
  51.6 3.8 %collective-permute-done.13.refs_1_ = bf16[1024,128]{1,0:T(8,128)(2,1)S(1)} collective-permute-done((bf16[1024,128]{1,0:T(8,128)(2,1)S(1)}, bf16[1024,128]{1,0:T(8,128)(2,1)S(1)}, u32[]{:S(2)}, u32[]{:S(2)}) %collective-permute-start.13) | collective-permute-done | bytes 262176 | tf_op jit(solution)/shard_map/ppermute | solution.py:516
  55.4 0.1 shard_map.110.came_ref
  55.5 0.1 shard_map.111
  55.5 2.4 %collective-permute-start.17 = (bf16[256,2048]{1,0:T(8,128)(2,1)S(1)}, bf16[256,2048]{1,0:T(8,128)(2,1)S(1)}, u32[]{:S(2)}, u32[]{:S(2)}) collective-permute-start(bf16[256,2048]{1,0:T(8,128)(2,1)S(1)} %shard_map.107), channel_id=1, source_target_pairs={{0,1},{1,0},{2,3},{3,2},{4,5},{5,4},{6,7},{7,6},{8,9},{9,8},{10,11... | collective-permute-start | bytes 3145736 | tf_op jit(solution)/shard_map/ppermute | solution.py:519
  57.9 1.4 %collective-permute-start.15 = (bf16[1024,128]{1,0:T(8,128)(2,1)S(1)}, bf16[1024,128]{1,0:T(8,128)(2,1)S(1)}, u32[]{:S(2)}, u32[]{:S(2)}) collective-permute-start(bf16[1024,128]{1,0:T(8,128)(2,1)S(1)} %get-tuple-element.84), channel_id=1, source_target_pairs={{0,4},{2,6},{4,8},{6,10},{8,12},{10,14},{12,16},{14,18},{16,20},{1... | collective-permute-start | bytes 786440 | tf_op jit(solution)/shard_map/ppermute | solution.py:516
  59.3 1.0 %collective-permute-start.16 = (bf16[1024,128]{1,0:T(8,128)(2,1)S(1)}, bf16[1024,128]{1,0:T(8,128)(2,1)S(1)}, u32[]{:S(2)}, u32[]{:S(2)}) collective-permute-start(bf16[1024,128]{1,0:T(8,128)(2,1)S(1)} %get-tuple-element.85), channel_id=1, source_target_pairs={{0,2},{2,4},{4,6},{6,8},{8,10},{10,12},{12,14},{14,16},{16,18},{18... | collective-permute-start | bytes 786440 | tf_op jit(solution)/shard_map/ppermute | solution.py:516
  60.3 1.7 %shard_map.112 = bf16[256,2048]{1,0:T(8,128)(2,1)} custom-call(s32[1]{0:T(128)} %bitcast.1.core_ref.half_ref, bf16[256,512]{1,0:T(8,128)(2,1)S(1)} %get-tuple-element.69.a_ref, bf16[4096,512]{1,0:T(8,128)(2,1)S(1)} %copy-done.1, bf16[256,2048]{1,0:T(8,128)(2,1)S(1)} %collective-permute-done.17.refs_0_), custom_call_target="tpu_custom_call" | custom-call | flops 536870912 | bytes 4000000 | tf_op jit(solution)/shard_map/pallas_call | solution.py:496
  62.0 2.1 %collective-permute-done.15.refs_2_ = bf16[1024,128]{1,0:T(8,128)(2,1)S(1)} collective-permute-done((bf16[1024,128]{1,0:T(8,128)(2,1)S(1)}, bf16[1024,128]{1,0:T(8,128)(2,1)S(1)}, u32[]{:S(2)}, u32[]{:S(2)}) %collective-permute-start.15) | collective-permute-done | bytes 262176 | tf_op jit(solution)/shard_map/ppermute | solution.py:516
  64.1 5.9 %collective-permute-done.16.refs_1_ = bf16[1024,128]{1,0:T(8,128)(2,1)S(1)} collective-permute-done((bf16[1024,128]{1,0:T(8,128)(2,1)S(1)}, bf16[1024,128]{1,0:T(8,128)(2,1)S(1)}, u32[]{:S(2)}, u32[]{:S(2)}) %collective-permute-start.16) | collective-permute-done | bytes 262176 | tf_op jit(solution)/shard_map/ppermute | solution.py:516
  70.0 2.3 %collective-permute-start.18 = (bf16[512,128]{1,0:T(8,128)(2,1)S(1)}, bf16[512,128]{1,0:T(8,128)(2,1)S(1)}, u32[]{:S(2)}, u32[]{:S(2)}) collective-permute-start(bf16[512,128]{1,0:T(8,128)(2,1)S(1)} %slice.22), channel_id=1, source_target_pairs={{0,1},{1,0},{2,3},{3,2},{4,5},{5,4},{6,7},{7,6},{8,9},{9,8},{10,11... | collective-permute-start | bytes 393224 | tf_op jit(solution)/shard_map/ppermute | solution.py:519
  72.3 0.1 collective-permute-start.19
  72.4 0.9 %collective-permute-done.18.refs_3_ = bf16[512,128]{1,0:T(8,128)(2,1)S(1)} collective-permute-done((bf16[512,128]{1,0:T(8,128)(2,1)S(1)}, bf16[512,128]{1,0:T(8,128)(2,1)S(1)}, u32[]{:S(2)}, u32[]{:S(2)}) %collective-permute-start.18) | collective-permute-done | bytes 131104 | tf_op jit(solution)/shard_map/ppermute | solution.py:519
  73.3 0.5 collective-permute-done.19.refs_4_
  73.7 0.7 shard_map.113
  (27 shorter events, 0.2 us)
Async XLA Ops:
  0.6 2.7 %collective-permute-start = (bf16[256,128]{1,0:T(8,128)(2,1)}, bf16[256,128]{1,0:T(8,128)(2,1)S(1)}, u32[]{:S(2)}, u32[]{:S(2)}) collective-permute-start(bf16[256,128]{1,0:T(8,128)(2,1)} %refs_0_.1), channel_id=1, source_target_pairs={{0,1},{1,0},{2,3},{3,2},{4,5},{5,4},{6,7},{7,6},{8,9},{9,8},{10,11... | collective-permute-start | bytes 196616 | tf_op jit(solution)/shard_map/ppermute | solution.py:519
  1.4 2.0 %collective-permute-start.1 = (bf16[256,128]{1,0:T(8,128)(2,1)}, bf16[256,128]{1,0:T(8,128)(2,1)S(1)}, u32[]{:S(2)}, u32[]{:S(2)}) collective-permute-start(bf16[256,128]{1,0:T(8,128)(2,1)} %refs_1_.1), channel_id=1, source_target_pairs={{0,1},{1,0},{2,3},{3,2},{4,5},{5,4},{6,7},{7,6},{8,9},{9,8},{10,11... | collective-permute-start | bytes 196616 | tf_op jit(solution)/shard_map/ppermute | solution.py:519
  1.5 0.8 %copy-start.3 = (bf16[256,128]{1,0:T(8,128)(2,1)S(1)}, bf16[256,128]{1,0:T(8,128)(2,1)}, u32[]{:S(2)}) copy-start(bf16[256,128]{1,0:T(8,128)(2,1)} %refs_0_.1) | copy-start | bytes 196612
  2.3 0.8 %copy-start.4 = (bf16[256,128]{1,0:T(8,128)(2,1)S(1)}, bf16[256,128]{1,0:T(8,128)(2,1)}, u32[]{:S(2)}) copy-start(bf16[256,128]{1,0:T(8,128)(2,1)} %refs_1_.1) | copy-start | bytes 196612
  3.2 23.8 %copy-start.5 = (bf16[256,512]{1,0:T(8,128)(2,1)S(1)}, bf16[256,512]{1,0:T(8,128)(2,1)}, u32[]{:S(2)}) copy-start(bf16[256,512]{1,0:T(8,128)(2,1)} %q_ref.1) | copy-start | bytes 786436
  3.2 23.8 %copy-start.6 = (s32[64]{0:T(128)S(1)}, s32[64]{0:T(128)}, u32[]{:S(2)}) copy-start(s32[64]{0:T(128)} %param.11) | copy-start | bytes 772
  3.2 23.8 %copy-start.7 = (s32[64]{0:T(128)S(1)}, s32[64]{0:T(128)}, u32[]{:S(2)}) copy-start(s32[64]{0:T(128)} %param.12) | copy-start | bytes 772
  3.4 9.3 %collective-permute-start.4 = (bf16[256,2048]{1,0:T(8,128)(2,1)}, bf16[256,2048]{1,0:T(8,128)(2,1)S(1)}, u32[]{:S(2)}, u32[]{:S(2)}) collective-permute-start(bf16[256,2048]{1,0:T(8,128)(2,1)} %own_ref.1), channel_id=1, source_target_pairs={{0,1},{1,0},{2,3},{3,2},{4,5},{5,4},{6,7},{7,6},{8,9},{9,8},{10,11... | collective-permute-start | bytes 3145736 | tf_op jit(solution)/shard_map/ppermute | solution.py:519
  3.9 14.2 %collective-permute-start.3 = (bf16[1024,128]{1,0:T(8,128)(2,1)S(1)}, bf16[1024,128]{1,0:T(8,128)(2,1)S(1)}, u32[]{:S(2)}, u32[]{:S(2)}) collective-permute-start(bf16[1024,128]{1,0:T(8,128)(2,1)S(1)} %shard_map.103), channel_id=1, source_target_pairs={{0,4},{2,6},{4,8},{6,10},{8,12},{10,14},{12,16},{14,18},{16,20},{1... | collective-permute-start | bytes 786440 | tf_op jit(solution)/shard_map/ppermute | solution.py:516
  12.0 13.3 %collective-permute-start.2 = (bf16[1024,128]{1,0:T(8,128)(2,1)S(1)}, bf16[1024,128]{1,0:T(8,128)(2,1)S(1)}, u32[]{:S(2)}, u32[]{:S(2)}) collective-permute-start(bf16[1024,128]{1,0:T(8,128)(2,1)S(1)} %shard_map.103), channel_id=1, source_target_pairs={{0,2},{2,4},{4,6},{6,8},{8,10},{10,12},{12,14},{14,16},{16,18},{18... | collective-permute-start | bytes 786440 | tf_op jit(solution)/shard_map/ppermute | solution.py:516
  12.7 2.2 %copy-start = (bf16[4096,512]{1,0:T(8,128)(2,1)S(1)}, bf16[4096,512]{1,0:T(8,128)(2,1)}, u32[]{:S(2)}) copy-start(bf16[4096,512]{1,0:T(8,128)(2,1)} %w_ref.5) | copy-start | bytes 12582916
  14.9 1.2 %copy-start.2 = (bf16[256,2048]{1,0:T(8,128)(2,1)S(1)}, bf16[256,2048]{1,0:T(8,128)(2,1)}, u32[]{:S(2)}) copy-start(bf16[256,2048]{1,0:T(8,128)(2,1)} %own_ref.1) | copy-start | bytes 3145732
  18.1 13.1 %collective-permute-start.7 = (bf16[1024,128]{1,0:T(8,128)(2,1)S(1)}, bf16[1024,128]{1,0:T(8,128)(2,1)S(1)}, u32[]{:S(2)}, u32[]{:S(2)}) collective-permute-start(bf16[1024,128]{1,0:T(8,128)(2,1)S(1)} %collective-permute-done.3.at2_ref), channel_id=1, source_target_pairs={{0,4},{2,6},{4,8},{6,10},{8,12},{10,14},{12,16},{14,18},{16,20},{1... | collective-permute-start | bytes 786440 | tf_op jit(solution)/shard_map/ppermute | solution.py:516
  25.3 8.8 %collective-permute-start.8 = (bf16[1024,128]{1,0:T(8,128)(2,1)S(1)}, bf16[1024,128]{1,0:T(8,128)(2,1)S(1)}, u32[]{:S(2)}, u32[]{:S(2)}) collective-permute-start(bf16[1024,128]{1,0:T(8,128)(2,1)S(1)} %collective-permute-done.3.at2_ref), channel_id=1, source_target_pairs={{0,2},{2,4},{4,6},{6,8},{8,10},{10,12},{12,14},{14,16},{16,18},{18... | collective-permute-start | bytes 786440 | tf_op jit(solution)/shard_map/ppermute | solution.py:516
  25.3 1.4 %collective-permute-start.5 = (bf16[512,128]{1,0:T(8,128)(2,1)S(1)}, bf16[512,128]{1,0:T(8,128)(2,1)S(1)}, u32[]{:S(2)}, u32[]{:S(2)}) collective-permute-start(bf16[512,128]{1,0:T(8,128)(2,1)S(1)} %slice.24), channel_id=1, source_target_pairs={{0,1},{1,0},{2,3},{3,2},{4,5},{5,4},{6,7},{7,6},{8,9},{9,8},{10,11... | collective-permute-start | bytes 393224 | tf_op jit(solution)/shard_map/ppermute | solution.py:519
  25.4 1.6 %collective-permute-start.6 = (bf16[512,128]{1,0:T(8,128)(2,1)S(1)}, bf16[512,128]{1,0:T(8,128)(2,1)S(1)}, u32[]{:S(2)}, u32[]{:S(2)}) collective-permute-start(bf16[512,128]{1,0:T(8,128)(2,1)S(1)} %slice.19), channel_id=1, source_target_pairs={{0,1},{1,0},{2,3},{3,2},{4,5},{5,4},{6,7},{7,6},{8,9},{9,8},{10,11... | collective-permute-start | bytes 393224 | tf_op jit(solution)/shard_map/ppermute | solution.py:519
  26.0 15.0 %copy-start.1 = (bf16[4096,512]{1,0:T(8,128)(2,1)S(1)}, bf16[4096,512]{1,0:T(8,128)(2,1)}, u32[]{:S(2)}) copy-start(bf16[4096,512]{1,0:T(8,128)(2,1)} %w_ref.5) | copy-start | bytes 12582916
  34.1 2.3 %collective-permute-start.10 = (bf16[512,128]{1,0:T(8,128)(2,1)S(1)}, bf16[512,128]{1,0:T(8,128)(2,1)S(1)}, u32[]{:S(2)}, u32[]{:S(2)}) collective-permute-start(bf16[512,128]{1,0:T(8,128)(2,1)S(1)} %slice.21), channel_id=1, source_target_pairs={{0,1},{1,0},{2,3},{3,2},{4,5},{5,4},{6,7},{7,6},{8,9},{9,8},{10,11... | collective-permute-start | bytes 393224 | tf_op jit(solution)/shard_map/ppermute | solution.py:519
  35.4 1.4 %collective-permute-start.9 = (bf16[512,128]{1,0:T(8,128)(2,1)S(1)}, bf16[512,128]{1,0:T(8,128)(2,1)S(1)}, u32[]{:S(2)}, u32[]{:S(2)}) collective-permute-start(bf16[512,128]{1,0:T(8,128)(2,1)S(1)} %slice.20), channel_id=1, source_target_pairs={{0,1},{1,0},{2,3},{3,2},{4,5},{5,4},{6,7},{7,6},{8,9},{9,8},{10,11... | collective-permute-start | bytes 393224 | tf_op jit(solution)/shard_map/ppermute | solution.py:519
  40.7 1.6 %collective-permute-start.11 = (bf16[1024,128]{1,0:T(8,128)(2,1)S(1)}, bf16[1024,128]{1,0:T(8,128)(2,1)S(1)}, u32[]{:S(2)}, u32[]{:S(2)}) collective-permute-start(bf16[1024,128]{1,0:T(8,128)(2,1)S(1)} %get-tuple-element.68), channel_id=1, source_target_pairs={{0,1},{1,0},{2,3},{3,2},{4,5},{5,4},{6,7},{7,6},{8,9},{9,8},{10,11... | collective-permute-start | bytes 786440 | tf_op jit(solution)/shard_map/ppermute | solution.py:519
  42.4 9.2 %collective-permute-start.12 = (bf16[1024,128]{1,0:T(8,128)(2,1)S(1)}, bf16[1024,128]{1,0:T(8,128)(2,1)S(1)}, u32[]{:S(2)}, u32[]{:S(2)}) collective-permute-start(bf16[1024,128]{1,0:T(8,128)(2,1)S(1)} %get-tuple-element.77), channel_id=1, source_target_pairs={{0,4},{2,6},{4,8},{6,10},{8,12},{10,14},{12,16},{14,18},{16,20},{1... | collective-permute-start | bytes 786440 | tf_op jit(solution)/shard_map/ppermute | solution.py:516
  43.0 12.4 %collective-permute-start.13 = (bf16[1024,128]{1,0:T(8,128)(2,1)S(1)}, bf16[1024,128]{1,0:T(8,128)(2,1)S(1)}, u32[]{:S(2)}, u32[]{:S(2)}) collective-permute-start(bf16[1024,128]{1,0:T(8,128)(2,1)S(1)} %get-tuple-element.78), channel_id=1, source_target_pairs={{0,2},{2,4},{4,6},{6,8},{8,10},{10,12},{12,14},{14,16},{16,18},{18... | collective-permute-start | bytes 786440 | tf_op jit(solution)/shard_map/ppermute | solution.py:516
  51.6 3.8 %collective-permute-start.14 = (bf16[1024,128]{1,0:T(8,128)(2,1)S(1)}, bf16[1024,128]{1,0:T(8,128)(2,1)S(1)}, u32[]{:S(2)}, u32[]{:S(2)}) collective-permute-start(bf16[1024,128]{1,0:T(8,128)(2,1)S(1)} %get-tuple-element.79), channel_id=1, source_target_pairs={{0,1},{1,0},{2,3},{3,2},{4,5},{5,4},{6,7},{7,6},{8,9},{9,8},{10,11... | collective-permute-start | bytes 786440 | tf_op jit(solution)/shard_map/ppermute | solution.py:519
  55.5 4.8 %collective-permute-start.17 = (bf16[256,2048]{1,0:T(8,128)(2,1)S(1)}, bf16[256,2048]{1,0:T(8,128)(2,1)S(1)}, u32[]{:S(2)}, u32[]{:S(2)}) collective-permute-start(bf16[256,2048]{1,0:T(8,128)(2,1)S(1)} %shard_map.107), channel_id=1, source_target_pairs={{0,1},{1,0},{2,3},{3,2},{4,5},{5,4},{6,7},{7,6},{8,9},{9,8},{10,11... | collective-permute-start | bytes 3145736 | tf_op jit(solution)/shard_map/ppermute | solution.py:519
  57.9 6.2 %collective-permute-start.15 = (bf16[1024,128]{1,0:T(8,128)(2,1)S(1)}, bf16[1024,128]{1,0:T(8,128)(2,1)S(1)}, u32[]{:S(2)}, u32[]{:S(2)}) collective-permute-start(bf16[1024,128]{1,0:T(8,128)(2,1)S(1)} %get-tuple-element.84), channel_id=1, source_target_pairs={{0,4},{2,6},{4,8},{6,10},{8,12},{10,14},{12,16},{14,18},{16,20},{1... | collective-permute-start | bytes 786440 | tf_op jit(solution)/shard_map/ppermute | solution.py:516
  59.3 10.7 %collective-permute-start.16 = (bf16[1024,128]{1,0:T(8,128)(2,1)S(1)}, bf16[1024,128]{1,0:T(8,128)(2,1)S(1)}, u32[]{:S(2)}, u32[]{:S(2)}) collective-permute-start(bf16[1024,128]{1,0:T(8,128)(2,1)S(1)} %get-tuple-element.85), channel_id=1, source_target_pairs={{0,2},{2,4},{4,6},{6,8},{8,10},{10,12},{12,14},{14,16},{16,18},{18... | collective-permute-start | bytes 786440 | tf_op jit(solution)/shard_map/ppermute | solution.py:516
  70.0 3.3 %collective-permute-start.18 = (bf16[512,128]{1,0:T(8,128)(2,1)S(1)}, bf16[512,128]{1,0:T(8,128)(2,1)S(1)}, u32[]{:S(2)}, u32[]{:S(2)}) collective-permute-start(bf16[512,128]{1,0:T(8,128)(2,1)S(1)} %slice.22), channel_id=1, source_target_pairs={{0,1},{1,0},{2,3},{3,2},{4,5},{5,4},{6,7},{7,6},{8,9},{9,8},{10,11... | collective-permute-start | bytes 393224 | tf_op jit(solution)/shard_map/ppermute | solution.py:519
  72.3 1.4 %collective-permute-start.19 = (bf16[512,128]{1,0:T(8,128)(2,1)S(1)}, bf16[512,128]{1,0:T(8,128)(2,1)S(1)}, u32[]{:S(2)}, u32[]{:S(2)}) collective-permute-start(bf16[512,128]{1,0:T(8,128)(2,1)S(1)} %slice.23), channel_id=1, source_target_pairs={{0,1},{1,0},{2,3},{3,2},{4,5},{5,4},{6,7},{7,6},{8,9},{9,8},{10,11... | collective-permute-start | bytes 393224 | tf_op jit(solution)/shard_map/ppermute | solution.py:519
